TPU v7x, 32 devices: a whole 2x2x4 slice. The times are simulated.
32 devices in a mesh: wide: 4 (over y, x), narrow: 8 (over z, core).
Axes of the slice: x: 2, y: 2, z: 4, core: 2. Of those that a mesh axis runs over, the one named last changes fastest.
Arguments:
- tokens: bfloat16 [32, 1024, 768], P(('wide', 'narrow')), may hold values from -6 to 6
- split_point: int32 [32], P(('wide', 'narrow')), may hold values from 128 to 896
- cotangent: bfloat16 [32, 1024, 768], P(('wide', 'narrow')), may hold values from -6 to 6
- norm_gain: float32 [2, 2, 768], replicated, may hold values from 0.5 to 1.5
- norm_shift: float32 [2, 2, 768], replicated, may hold values from -1.75 to 1.75
- in_weight: bfloat16 [2, 768, 2304], P(None, None, ('wide', 'narrow')), may hold values from -0.21875 to 0.21875
- in_bias: float32 [2, 2304], replicated, may hold values from -3 to 3
- short_taps: float32 [2, 3, 2304], replicated, may hold values from -3.5 to 3.5
- cond_taps: float32 [2, 3, 768], replicated, may hold values from -3.5 to 3.5
- decay_rate: float32 [2, 768], replicated, may hold values from 0.001 to 0.05
- freq_in: float32 [2, 64, 64], replicated, may hold values from -0.75 to 0.75
- freq_bias: float32 [2, 64], replicated, may hold values from -3.140625 to 3.140625
- freq_out: float32 [2, 64, 768], replicated, may hold values from -0.75 to 0.75
- out_weight: bfloat16 [2, 768, 768], P(None, ('wide', 'narrow')), may hold values from -0.4375 to 0.4375
- out_bias: float32 [2, 768], replicated, may hold values from -1.75 to 1.75
- up_weight: bfloat16 [2, 768, 6144], P(None, None, ('wide', 'narrow')), may hold values from -0.21875 to 0.21875
- down_weight: bfloat16 [2, 3072, 768], P(None, ('wide', 'narrow')), may hold values from -0.109375 to 0.109375
- down_bias: float32 [2, 768], replicated, may hold values from -1.75 to 1.75
Outputs:
- layer_outputs: float32 [2, 32, 1024, 768], P(None, ('wide', 'narrow'))
- token_grad: float32 [32, 1024, 768], P(('wide', 'narrow'))
- norm_gain_grad: float32 [2, 2, 768], replicated
- norm_shift_grad: float32 [2, 2, 768], replicated
- in_weight_grad: float32 [2, 768, 2304], P(None, None, ('wide', 'narrow'))
- in_bias_grad: float32 [2, 2304], replicated
- short_taps_grad: float32 [2, 3, 2304], replicated
- cond_taps_grad: float32 [2, 3, 768], replicated
- decay_rate_grad: float32 [2, 768], replicated
- freq_in_grad: float32 [2, 64, 64], replicated
- freq_bias_grad: float32 [2, 64], replicated
- freq_out_grad: float32 [2, 64, 768], replicated
- out_weight_grad: float32 [2, 768, 768], P(None, ('wide', 'narrow'))
- out_bias_grad: float32 [2, 768], replicated
- up_weight_grad: float32 [2, 768, 6144], P(None, None, ('wide', 'narrow'))
- down_weight_grad: float32 [2, 3072, 768], P(None, ('wide', 'narrow'))
- down_bias_grad: float32 [2, 768], replicated
Inputs may be any that keep to these rules, and one draw needn't show every extreme that they name: Each pair has two nonempty segments split at split_point.
All inputs are finite; a program needn't handle non-finite values.
Results may differ from a plain program's by a relative error of at most 0.012.
Values may be sent and summed in bfloat16 or wider, within the bound.
No kernel may reach another device: no remote copies, remote signals or barrier semaphores. Data moves between devices by JAX's collectives and lax.ppermute only.
A program may use at most 576 MiB of HBM per device.

v0:
```python
import math

import jax
import jax.numpy as jnp
from jax import lax
from jax.sharding import PartitionSpec as P

epsilon = 1e-05


def norm_rows(values, gain, shift):
    average = jnp.mean(values, axis=-1, keepdims=True)
    centered = values - average
    variance = jnp.mean(centered * centered, axis=-1, keepdims=True)
    return centered * lax.rsqrt(variance + epsilon) * gain + shift


def gated_unit(values):
    midpoint = values.shape[-1] // 2
    return jax.nn.gelu(values[..., :midpoint], approximate=True) * values[..., midpoint:]


def short_conv(values, tap_weights, segment):
    length = values.shape[-2]
    accumulated = tap_weights[0] * values
    for offset in (1, 2):
        moved = jnp.pad(values, ((0, 0), (offset, 0), (0, 0)))[:, :length, :]
        before = jnp.pad(segment, ((0, 0), (offset, 0)), constant_values=-1)[:, :length]
        same_doc = (before == segment).astype(values.dtype)[..., None]
        accumulated = accumulated + tap_weights[offset] * moved * same_doc
    return accumulated


def filter_kernel(length, decay, freq_in, freq_bias, freq_out):
    feature_half = freq_in.shape[0] // 2
    positions = jnp.arange(length, dtype=jnp.float32)[:, None]
    harmonics = jnp.arange(1, feature_half + 1, dtype=jnp.float32)[None, :]
    angles = positions * harmonics * (2.0 * math.pi / length)
    features = jnp.concatenate([jnp.sin(angles), jnp.cos(angles)], axis=1)
    inner = jnp.sin(jnp.dot(features, freq_in, precision=lax.Precision.HIGHEST) + freq_bias)
    profile = jnp.dot(inner, freq_out, precision=lax.Precision.HIGHEST)
    window = jnp.exp(-positions * decay[None, :]) * jnp.sqrt(2.0 * decay)[None, :]
    return profile * window


def circle_table(period, rows, cols, sign):
    product_index = (
        jnp.arange(rows, dtype=jnp.int32)[:, None]
        * jnp.arange(cols, dtype=jnp.int32)[None, :]
        % period
    )
    angle = product_index.astype(jnp.float32) * (sign * 2.0 * math.pi / period)
    return (jnp.cos(angle), jnp.sin(angle))


def transform(real_part, imag_part, sign, keep_in, keep_out, inner_count, outer_count):
    highest = lax.Precision.HIGHEST
    total = inner_count * outer_count
    batch, _, channels = real_part.shape
    real_part = real_part.reshape(batch, keep_in, inner_count, channels)
    first_cos, first_sin = circle_table(outer_count, outer_count, keep_in, sign)
    section_re = jnp.einsum("kn,snac->skac", first_cos, real_part, precision=highest)
    section_im = jnp.einsum("kn,snac->skac", first_sin, real_part, precision=highest)
    if imag_part is not None:
        imag_part = imag_part.reshape(batch, keep_in, inner_count, channels)
        section_re = section_re - jnp.einsum(
            "kn,snac->skac", first_sin, imag_part, precision=highest
        )
        section_im = section_im + jnp.einsum(
            "kn,snac->skac", first_cos, imag_part, precision=highest
        )
    twist_cos, twist_sin = circle_table(total, outer_count, inner_count, sign)
    twist_cos = twist_cos[:, :, None]
    twist_sin = twist_sin[:, :, None]
    rotated_re = section_re * twist_cos - section_im * twist_sin
    rotated_im = section_re * twist_sin + section_im * twist_cos
    last_cos, last_sin = circle_table(inner_count, keep_out, inner_count, sign)
    final_re = jnp.einsum("jn,sknc->sjkc", last_cos, rotated_re, precision=highest) - jnp.einsum(
        "jn,sknc->sjkc", last_sin, rotated_im, precision=highest
    )
    final_im = jnp.einsum("jn,sknc->sjkc", last_sin, rotated_re, precision=highest) + jnp.einsum(
        "jn,sknc->sjkc", last_cos, rotated_im, precision=highest
    )
    return (
        final_re.reshape(batch, keep_out * outer_count, channels),
        final_im.reshape(batch, keep_out * outer_count, channels),
    )


def spectral_conv(kernel, front_signal, back_signal):
    length = kernel.shape[0]
    total = 2 * length
    inner_count = max(
        (divisor for divisor in range(1, math.isqrt(total) + 1) if total % divisor == 0)
    )
    outer_count = total // inner_count
    kernel_re, kernel_im = transform(
        kernel[None], None, -1.0, outer_count // 2, inner_count, inner_count, outer_count
    )
    signal_re, signal_im = transform(
        front_signal, back_signal, -1.0, outer_count // 2, inner_count, inner_count, outer_count
    )
    spectrum_re = signal_re * kernel_re - signal_im * kernel_im
    spectrum_im = signal_re * kernel_im + signal_im * kernel_re
    result_re, result_im = transform(
        spectrum_re, spectrum_im, 1.0, outer_count, inner_count // 2, inner_count, outer_count
    )
    return (result_re / total, result_im / total)


def mixer(projected, segment, in_bias, short_taps, cond_taps, decay, freq_in, freq_bias, freq_out):
    channels = projected.shape[-1] // 3
    length = projected.shape[-2]
    shortened = short_conv(projected + in_bias, short_taps, segment)
    query = shortened[..., :channels]
    key_part = shortened[..., channels : 2 * channels]
    value_part = shortened[..., 2 * channels :]
    condition = short_conv(value_part, cond_taps, segment)
    channel_scale = jnp.sqrt(jnp.mean(condition * condition, axis=-2, keepdims=True) + epsilon)
    kernel = filter_kernel(length, decay, freq_in, freq_bias, freq_out)
    front_mask = (segment == 0).astype(projected.dtype)[..., None]
    back_mask = 1.0 - front_mask
    product = key_part * value_part
    front_conv, back_conv = spectral_conv(kernel, product * front_mask, product * back_mask)
    return query * channel_scale * (front_conv * front_mask + back_conv * back_mask)


def body(
    tokens,
    split_point,
    cotangent,
    norm_gain,
    norm_shift,
    in_weight,
    in_bias,
    short_taps,
    cond_taps,
    decay_rate,
    freq_in,
    freq_bias,
    freq_out,
    out_weight,
    out_bias,
    up_weight,
    down_weight,
    down_bias,
):
    length = tokens.shape[1]
    layers = in_weight.shape[0]
    segment = (jnp.arange(length, dtype=jnp.int32)[None, :] >= split_point[:, None]).astype(
        jnp.int32
    )
    state = tokens.astype(jnp.float32)
    saved = []
    outputs = []
    for layer_index in range(layers):
        weights = (
            lax.all_gather(in_weight[layer_index], ("wide", "narrow"), axis=1, tiled=True),
            lax.all_gather(out_weight[layer_index], ("wide", "narrow"), axis=0, tiled=True),
            lax.all_gather(up_weight[layer_index], ("wide", "narrow"), axis=1, tiled=True),
            lax.all_gather(down_weight[layer_index], ("wide", "narrow"), axis=0, tiled=True),
        )
        w_in, w_out, w_up, w_down = weights
        normed = norm_rows(state, norm_gain[layer_index, 0], norm_shift[layer_index, 0]).astype(
            jnp.bfloat16
        )
        projected = jnp.einsum("pld,de->ple", normed, w_in, preferred_element_type=jnp.float32)
        mixed = mixer(
            projected,
            segment,
            in_bias[layer_index],
            short_taps[layer_index],
            cond_taps[layer_index],
            decay_rate[layer_index],
            freq_in[layer_index],
            freq_bias[layer_index],
            freq_out[layer_index],
        ).astype(jnp.bfloat16)
        middle = (
            state
            + jnp.einsum("pld,de->ple", mixed, w_out, preferred_element_type=jnp.float32)
            + out_bias[layer_index]
        )
        second = norm_rows(middle, norm_gain[layer_index, 1], norm_shift[layer_index, 1]).astype(
            jnp.bfloat16
        )
        hidden_in = jnp.einsum("pld,df->plf", second, w_up, preferred_element_type=jnp.float32)
        hidden = gated_unit(hidden_in).astype(jnp.bfloat16)
        result = (
            middle
            + jnp.einsum("plf,fd->pld", hidden, w_down, preferred_element_type=jnp.float32)
            + down_bias[layer_index]
        )
        saved.append((state, normed, projected, mixed, middle, second, hidden_in, hidden, weights))
        outputs.append(result)
        state = result
    gradient = cotangent.astype(jnp.float32)
    small_grads = [None] * layers
    big_grads = [None] * layers
    for layer_index in reversed(range(layers)):
        state_in, normed, projected, mixed, middle, second, hidden_in, hidden, weights = saved[
            layer_index
        ]
        w_in, w_out, w_up, w_down = (
            lax.all_gather(in_weight[layer_index], ("wide", "narrow"), axis=1, tiled=True),
            lax.all_gather(out_weight[layer_index], ("wide", "narrow"), axis=0, tiled=True),
            lax.all_gather(up_weight[layer_index], ("wide", "narrow"), axis=1, tiled=True),
            lax.all_gather(down_weight[layer_index], ("wide", "narrow"), axis=0, tiled=True),
        )
        grad_down_bias = jnp.sum(gradient, axis=(0, 1))
        grad_low = gradient.astype(jnp.bfloat16)
        grad_down = jnp.einsum("plf,pld->fd", hidden, grad_low, preferred_element_type=jnp.float32)
        grad_hidden = jnp.einsum(
            "pld,fd->plf", grad_low, w_down, preferred_element_type=jnp.float32
        )
        grad_hidden_in = jax.vjp(gated_unit, hidden_in)[1](grad_hidden)[0].astype(jnp.bfloat16)
        grad_up = jnp.einsum(
            "pld,plf->df", second, grad_hidden_in, preferred_element_type=jnp.float32
        )
        grad_second = jnp.einsum(
            "plf,df->pld", grad_hidden_in, w_up, preferred_element_type=jnp.float32
        )
        pullback = jax.vjp(
            norm_rows, middle, norm_gain[layer_index, 1], norm_shift[layer_index, 1]
        )[1]
        grad_mid_norm, grad_gain_back, grad_shift_back = pullback(grad_second)
        grad_middle = gradient + grad_mid_norm
        grad_out_bias = jnp.sum(grad_middle, axis=(0, 1))
        middle_low = grad_middle.astype(jnp.bfloat16)
        grad_out = jnp.einsum("pld,ple->de", mixed, middle_low, preferred_element_type=jnp.float32)
        grad_mixed = jnp.einsum(
            "ple,de->pld", middle_low, w_out, preferred_element_type=jnp.float32
        )

        def mixer_local(
            values, bias_in, taps_short, taps_cond, decay, weight_first, bias_phase, weight_second
        ):
            return mixer(
                values,
                segment,
                bias_in,
                taps_short,
                taps_cond,
                decay,
                weight_first,
                bias_phase,
                weight_second,
            )

        mixer_pull = jax.vjp(
            mixer_local,
            projected,
            in_bias[layer_index],
            short_taps[layer_index],
            cond_taps[layer_index],
            decay_rate[layer_index],
            freq_in[layer_index],
            freq_bias[layer_index],
            freq_out[layer_index],
        )[1]
        (
            grad_projected,
            grad_in_bias,
            grad_short,
            grad_cond,
            grad_decay,
            grad_freq_in,
            grad_freq_bias,
            grad_freq_out,
        ) = mixer_pull(grad_mixed)
        projected_low = grad_projected.astype(jnp.bfloat16)
        grad_in = jnp.einsum(
            "pld,ple->de", normed, projected_low, preferred_element_type=jnp.float32
        )
        grad_normed = jnp.einsum(
            "ple,de->pld", projected_low, w_in, preferred_element_type=jnp.float32
        )
        front_pull = jax.vjp(
            norm_rows, state_in, norm_gain[layer_index, 0], norm_shift[layer_index, 0]
        )[1]
        grad_state_norm, grad_gain_front, grad_shift_front = front_pull(grad_normed)
        gradient = grad_middle + grad_state_norm
        big_grads[layer_index] = (
            lax.psum_scatter(grad_in, ("wide", "narrow"), scatter_dimension=1, tiled=True),
            lax.psum_scatter(grad_out, ("wide", "narrow"), scatter_dimension=0, tiled=True),
            lax.psum_scatter(grad_up, ("wide", "narrow"), scatter_dimension=1, tiled=True),
            lax.psum_scatter(grad_down, ("wide", "narrow"), scatter_dimension=0, tiled=True),
        )
        small_grads[layer_index] = (
            jnp.stack([grad_gain_front, grad_gain_back]),
            jnp.stack([grad_shift_front, grad_shift_back]),
            grad_in_bias,
            grad_short,
            grad_cond,
            grad_decay,
            grad_freq_in,
            grad_freq_bias,
            grad_freq_out,
            grad_out_bias,
            grad_down_bias,
        )
    stacked_in = jnp.stack([big_grads[index][0] for index in range(layers)])
    stacked_out = jnp.stack([big_grads[index][1] for index in range(layers)])
    stacked_up = jnp.stack([big_grads[index][2] for index in range(layers)])
    stacked_down = jnp.stack([big_grads[index][3] for index in range(layers)])
    gain_stack = jnp.stack([small_grads[index][0] for index in range(layers)])
    shift_stack = jnp.stack([small_grads[index][1] for index in range(layers)])
    in_bias_stack = jnp.stack([small_grads[index][2] for index in range(layers)])
    short_stack = jnp.stack([small_grads[index][3] for index in range(layers)])
    cond_stack = jnp.stack([small_grads[index][4] for index in range(layers)])
    decay_stack = jnp.stack([small_grads[index][5] for index in range(layers)])
    freq_in_stack = jnp.stack([small_grads[index][6] for index in range(layers)])
    freq_bias_stack = jnp.stack([small_grads[index][7] for index in range(layers)])
    freq_out_stack = jnp.stack([small_grads[index][8] for index in range(layers)])
    out_bias_stack = jnp.stack([small_grads[index][9] for index in range(layers)])
    down_bias_stack = jnp.stack([small_grads[index][10] for index in range(layers)])
    summed = lax.psum(
        (
            gain_stack,
            shift_stack,
            in_bias_stack,
            short_stack,
            cond_stack,
            decay_stack,
            freq_in_stack,
            freq_bias_stack,
            freq_out_stack,
            out_bias_stack,
            down_bias_stack,
        ),
        ("wide", "narrow"),
    )
    return (
        jnp.stack(outputs),
        gradient,
        summed[0],
        summed[1],
        stacked_in,
        summed[2],
        summed[3],
        summed[4],
        summed[5],
        summed[6],
        summed[7],
        summed[8],
        stacked_out,
        summed[9],
        stacked_up,
        stacked_down,
        summed[10],
    )


def solution(mesh):
    in_specs = (
        P(("wide", "narrow"), None, None),
        P(("wide", "narrow")),
        P(("wide", "narrow"), None, None),
        P(),
        P(),
        P(None, None, ("wide", "narrow")),
        P(),
        P(),
        P(),
        P(),
        P(),
        P(),
        P(),
        P(None, ("wide", "narrow"), None),
        P(),
        P(None, None, ("wide", "narrow")),
        P(None, ("wide", "narrow"), None),
        P(),
    )
    out_specs = (
        P(None, ("wide", "narrow"), None, None),
        P(("wide", "narrow"), None, None),
        P(),
        P(),
        P(None, None, ("wide", "narrow")),
        P(),
        P(),
        P(),
        P(),
        P(),
        P(),
        P(),
        P(None, ("wide", "narrow"), None),
        P(),
        P(None, None, ("wide", "narrow")),
        P(None, ("wide", "narrow"), None),
        P(),
    )
    return jax.shard_map(body, mesh=mesh, in_specs=in_specs, out_specs=out_specs, check_vma=False)
```

profile of v0, /device:TPU:0, one launch (start us, length us, event | category | flops | bytes accessed | tf_op | source)
XLA Modules:
  0.0 2969.4 jit_solution(1812521682668744100)
XLA Ops:
  109.2 11.1 fusion.340
  137.2 20.7 fusion.119
  157.9 12.7 fusion.224
  200.9 10.7 fusion.348
  222.0 10.9 fusion.357
  232.9 21.7 fusion.109
  271.5 10.6 fusion.208
  285.7 10.8 fusion.210
  296.6 19.0 fusion.105
  363.8 19.7 convolution_bitcast_fusion.1
  383.4 13.3 fusion.26
  436.6 11.1 fusion.328
  464.7 20.7 fusion.101
  485.4 12.5 fusion.192
  528.1 10.9 fusion.360
  549.5 10.6 fusion.369
  560.1 21.8 fusion.91
  602.5 10.7 fusion.176
  623.7 19.2 fusion.87
  692.1 19.7 convolution_bitcast_fusion
  711.9 24.2 bitcast_multiply_fusion.3
  736.0 19.1 fusion.1084
  796.4 16.5 negate_bitcast_fusion.3
  812.9 12.7 fusion.144
  869.5 28.9 fusion.95
  953.9 30.5 %fusion.46 = (f32[32,768,64]{1,0,2:T(8,128)}, f32[32,768,64]{1,0,2:T(8,128)}, f32[32,768,64]{1,0,2:T(8,128)}, f32[32,768,64]{1,0,2:T(8,128)}, f32[1,32,768,64]{2,1,3,0:T(8,128)}) fusion(f32[32,64]{0,1:T(8,128)S(1)} %copy-done.84, f32[32,64]{0,1:T(8,128)S(1)} %copy-done.86, f32[64,768,32]{1,2,0:T(8,128)} %fusion.49, f32[64,768,32]{1,2,0:T(8,128)} %fusion.28, ...), kind=kOutput, calls=%fused_computation.89 | convolution fusion | flops 633878528 | bytes 81805312 | tf_op jit(solution)/shard_map/transpose(jvp(jn,sknc->sjkc))/dot_general | solution.py:81
  1036.6 13.2 multiply_reduce_fusion.2
  1049.9 11.1 fusion.1064
  1078.8 25.3 bitcast_multiply_fusion.1
  1104.1 19.2 fusion.1086
  1165.7 16.4 negate_bitcast_fusion.1
  1182.1 12.7 fusion.136
  1221.7 10.6 add_bitcast_fusion.2
  1238.7 29.0 fusion.113
  1330.6 30.7 %fusion.55 = (f32[32,768,64]{1,0,2:T(8,128)}, f32[32,768,64]{1,0,2:T(8,128)}, f32[32,768,64]{1,0,2:T(8,128)}, f32[32,768,64]{1,0,2:T(8,128)}, f32[1,32,768,64]{2,1,3,0:T(8,128)}) fusion(f32[32,64]{0,1:T(8,128)S(1)} %copy-done.85, f32[32,64]{0,1:T(8,128)S(1)} %copy-done.87, f32[64,768,32]{1,2,0:T(8,128)} %fusion.58, f32[64,768,32]{1,2,0:T(8,128)} %fusion.32, ...), kind=kOutput, calls=%fused_computation.102 | convolution fusion | flops 633878528 | bytes 81805312 | tf_op jit(solution)/shard_map/transpose(jvp(jn,sknc->sjkc))/dot_general | solution.py:81
  1468.9 12.6 multiply_reduce_fusion.5
  1481.7 10.5 fusion.1062
  1571.0 22.3 fusion.408
  1594.0 22.3 fusion.411
  1655.0 101.9 %reduce-scatter.13.cloned.1.call-done = f32[24,768]{1,0:T(8,128)} async-done(((f32[768,768]{1,0:T(8,128)}), f32[24,768]{1,0:T(8,128)}) %reduce-scatter.13.cloned.1.call-update) | async-done | bytes 73744 | tf_op jit(solution)/shard_map/reduce_scatter | solution.py:285
  1756.9 103.3 %reduce-scatter.15.cloned.1.call-done = f32[24,768]{1,0:T(8,128)} async-done(((f32[768,768]{1,0:T(8,128)}), f32[24,768]{1,0:T(8,128)}) %reduce-scatter.15.cloned.1.call-update) | async-done | bytes 73744 | tf_op jit(solution)/shard_map/reduce_scatter | solution.py:285
  1861.8 123.1 %reduce-scatter.11.cloned.1.call-done = f32[768,72]{0,1:T(8,128)} async-done(((f32[768,2304]{0,1:T(8,128)}), f32[768,72]{0,1:T(8,128)}) %reduce-scatter.11.cloned.1.call-update) | async-done | bytes 221200 | tf_op jit(solution)/shard_map/reduce_scatter | solution.py:284
  1984.9 124.1 %reduce-scatter.9.cloned.1.call-done = f32[768,72]{0,1:T(8,128)} async-done(((f32[768,2304]{0,1:T(8,128)}), f32[768,72]{0,1:T(8,128)}) %reduce-scatter.9.cloned.1.call-update) | async-done | bytes 221200 | tf_op jit(solution)/shard_map/reduce_scatter | solution.py:284
  2110.8 139.8 %reduce-scatter.21.cloned.1.call-done = f32[96,768]{1,0:T(8,128)} async-done(((f32[3072,768]{1,0:T(8,128)}), f32[96,768]{1,0:T(8,128)}) %reduce-scatter.21.cloned.1.call-update) | async-done | bytes 294928 | tf_op jit(solution)/shard_map/reduce_scatter | solution.py:287
  2250.7 140.2 %reduce-scatter.23.cloned.1.call-done = f32[96,768]{1,0:T(8,128)} async-done(((f32[3072,768]{1,0:T(8,128)}), f32[96,768]{1,0:T(8,128)}) %reduce-scatter.23.cloned.1.call-update) | async-done | bytes 294928 | tf_op jit(solution)/shard_map/reduce_scatter | solution.py:287
  2392.8 211.4 %reduce-scatter.17.cloned.1.call-done = f32[768,192]{0,1:T(8,128)} async-done(((f32[768,6144]{0,1:T(8,128)}), f32[768,192]{0,1:T(8,128)}) %reduce-scatter.17.cloned.1.call-update) | async-done | bytes 589840 | tf_op jit(solution)/shard_map/reduce_scatter | solution.py:286
  2604.2 213.0 %reduce-scatter.19.cloned.1.call-done = f32[768,192]{0,1:T(8,128)} async-done(((f32[768,6144]{0,1:T(8,128)}), f32[768,192]{0,1:T(8,128)}) %reduce-scatter.19.cloned.1.call-update) | async-done | bytes 589840 | tf_op jit(solution)/shard_map/reduce_scatter | solution.py:286
  2819.5 130.6 %all-reduce.44.cloned.1.call-done = f32[2,64,768]{2,1,0:T(8,128)} async-done(((f32[2,64,768]{2,1,0:T(8,128)}), f32[2,64,768]{2,1,0:T(8,128)}) %all-reduce.44.cloned.1.call-update) | async-done | bytes 393232 | tf_op jit(solution)/shard_map/psum | solution.py:317
  (910 shorter events, 996.9 us)
Async XLA Ops:
  7.2 21.1 copy-start.69
  7.2 72.7 %all-gather.17.cloned.1.call-start = ((), (), s32[]{:S(2)}) async-start(), calls=%async_computation.17 | async-start | bytes 3649536 | tf_op jit(solution)/shard_map/all_gather | solution.py:158
  9.0 349.2 %all-gather.19.cloned.1.call-start = ((), (), s32[]{:S(2)}) async-start(), calls=%async_computation.18 | async-start | bytes 1216512 | tf_op jit(solution)/shard_map/all_gather | solution.py:159
  10.5 353.3 %all-gather.21.cloned.1.call-start = ((), (), s32[]{:S(2)}) async-start(), calls=%async_computation.19 | async-start | bytes 9732096 | tf_op jit(solution)/shard_map/all_gather | solution.py:160
  12.4 384.3 %all-gather.23.cloned.1.call-start = ((), (), s32[]{:S(2)}) async-start(), calls=%async_computation.20 | async-start | bytes 4866048 | tf_op jit(solution)/shard_map/all_gather | solution.py:161
  14.2 393.1 %all-gather.25.cloned.1.call-start = ((), (), s32[]{:S(2)}) async-start(), calls=%async_computation.21 | async-start | bytes 3649536 | tf_op jit(solution)/shard_map/all_gather | solution.py:158
  14.8 671.7 %all-gather.27.cloned.1.call-start = ((), (), s32[]{:S(2)}) async-start(), calls=%async_computation.22 | async-start | bytes 1216512 | tf_op jit(solution)/shard_map/all_gather | solution.py:159
  15.4 676.7 %all-gather.29.cloned.1.call-start = ((), (), s32[]{:S(2)}) async-start(), calls=%async_computation.23 | async-start | bytes 9732096 | tf_op jit(solution)/shard_map/all_gather | solution.py:160
  16.1 695.7 %all-gather.31.cloned.1.call-start = ((), (), s32[]{:S(2)}) async-start(), calls=%async_computation.24 | async-start | bytes 4866048 | tf_op jit(solution)/shard_map/all_gather | solution.py:161
  16.9 1635.2 %all-reduce.46.cloned.1.call-start = ((), (), s32[]{:S(2)}) async-start(), calls=%async_computation.25 | async-start | bytes 452608 | tf_op jit(solution)/shard_map/psum | solution.py:317
  50.8 86.4 %copy-start.104 = (f32[64,32]{0,1:T(8,128)}, f32[64,32]{0,1:T(8,128)S(1)}, u32[]{:S(2)}) copy-start(f32[64,32]{0,1:T(8,128)S(1)} %get-tuple-element.294) | copy-start | bytes 24580
  50.8 86.4 %copy-start.106 = (f32[64,32]{0,1:T(8,128)}, f32[64,32]{0,1:T(8,128)S(1)}, u32[]{:S(2)}) copy-start(f32[64,32]{0,1:T(8,128)S(1)} %get-tuple-element.295) | copy-start | bytes 24580
  50.9 245.6 %copy-start.100 = (f32[64,32]{0,1:T(8,128)}, f32[64,32]{0,1:T(8,128)S(1)}, u32[]{:S(2)}) copy-start(f32[64,32]{0,1:T(8,128)S(1)} %get-tuple-element.296) | copy-start | bytes 24580
  51.0 245.6 %copy-start.102 = (f32[64,32]{0,1:T(8,128)}, f32[64,32]{0,1:T(8,128)S(1)}, u32[]{:S(2)}) copy-start(f32[64,32]{0,1:T(8,128)S(1)} %get-tuple-element.297) | copy-start | bytes 24580
  71.2 287.0 %copy-start.10 = (bf16[1,1024,768]{1,2,0:T(8,128)(2,1)}, bf16[1,1024,768]{1,2,0:T(8,128)(2,1)S(1)}, u32[]{:S(2)}) copy-start(bf16[1,1024,768]{1,2,0:T(8,128)(2,1)S(1)} %copy.297) | copy-start | bytes 4718596
  74.6 604.9 %copy-start.78 = (f32[1,1024]{1,0:T(1,128)}, f32[1,1024]{1,0:T(1,128)S(1)}, u32[]{:S(2)}) copy-start(f32[1,1024]{1,0:T(1,128)S(1)} %get-tuple-element.260) | copy-start | bytes 12292
  74.6 604.9 %copy-start.81 = (f32[1,1024]{1,0:T(1,128)}, f32[1,1024]{1,0:T(1,128)S(1)}, u32[]{:S(2)}) copy-start(f32[1,1024]{1,0:T(1,128)S(1)} %get-tuple-element.261) | copy-start | bytes 12292
  75.4 27.3 copy-start.92
  75.4 27.3 copy-start.96
  76.1 276.1 %copy-start.171 = (f32[768]{0:T(1024)}, f32[768]{0:T(1024)S(1)}, u32[]{:S(2)}) copy-start(f32[768]{0:T(1024)S(1)} %get-tuple-element.103) | copy-start | bytes 9220
  76.1 276.1 %copy-start.195 = (f32[768]{0:T(1024)}, f32[768]{0:T(1024)S(1)}, u32[]{:S(2)}) copy-start(f32[768]{0:T(1024)S(1)} %get-tuple-element.101) | copy-start | bytes 9220
  76.1 276.1 %copy-start.197 = (f32[768]{0:T(1024)}, f32[768]{0:T(1024)S(1)}, u32[]{:S(2)}) copy-start(f32[768]{0:T(1024)S(1)} %get-tuple-element.102) | copy-start | bytes 9220
  76.1 279.0 %copy-start.126 = (f32[1024]{0:T(1024)}, f32[1024]{0:T(1024)S(1)}, u32[]{:S(2)}) copy-start(f32[1024]{0:T(1024)S(1)} %get-tuple-element.292) | copy-start | bytes 12292
  76.1 279.0 %copy-start.129 = (f32[1024]{0:T(1024)}, f32[1024]{0:T(1024)S(1)}, u32[]{:S(2)}) copy-start(f32[1024]{0:T(1024)S(1)} %get-tuple-element.293) | copy-start | bytes 12292
  157.9 22.7 slice-start.20
  200.9 21.1 slice-start.16
  261.1 21.0 slice-start.54
  361.7 21.7 copy-start.123
  405.9 280.6 %copy-start.4 = (f32[1,1024,768]{1,2,0:T(8,128)}, f32[1,1024,768]{1,2,0:T(8,128)S(1)}, u32[]{:S(2)}) copy-start(f32[1,1024,768]{1,2,0:T(8,128)S(1)} %get-tuple-element.275) | copy-start | bytes 9437188
  485.4 22.4 slice-start.18
  528.1 21.4 slice-start.14
  592.1 21.1 copy-start.12
  689.9 72.4 %copy-start.142 = (f32[1024]{0:T(1024)}, f32[1024]{0:T(1024)S(1)}, u32[]{:S(2)}) copy-start(f32[1024]{0:T(1024)S(1)} %broadcast_multiply_fusion.5) | copy-start | bytes 12292
  692.1 70.3 %copy-start.191 = (f32[1024]{0:T(1024)}, f32[1024]{0:T(1024)S(1)}, u32[]{:S(2)}) copy-start(f32[1024]{0:T(1024)S(1)} %fusion.687) | copy-start | bytes 12292
  812.9 29.6 slice-start.52
  1078.8 25.3 copy-start.57
  1182.1 29.4 slice-start.50
  1300.2 22.6 slice-start.28
  1361.4 23.7 slice-start.46
  1518.9 238.0 %reduce-scatter.13.cloned.1.call-start = ((), (), s32[]{:S(2)}) async-start(), calls=%async_computation.11 | async-start | bytes 2433024 | tf_op jit(solution)/shard_map/reduce_scatter | solution.py:285
  1523.3 336.9 %reduce-scatter.15.cloned.1.call-start = ((), (), s32[]{:S(2)}) async-start(), calls=%async_computation.12 | async-start | bytes 2433024 | tf_op jit(solution)/shard_map/reduce_scatter | solution.py:285
  1528.7 456.2 %reduce-scatter.11.cloned.1.call-start = ((), (), s32[]{:S(2)}) async-start(), calls=%async_computation.9 | async-start | bytes 7299072 | tf_op jit(solution)/shard_map/reduce_scatter | solution.py:284
  1539.0 570.0 %reduce-scatter.9.cloned.1.call-start = ((), (), s32[]{:S(2)}) async-start(), calls=%async_computation.8 | async-start | bytes 7299072 | tf_op jit(solution)/shard_map/reduce_scatter | solution.py:284
  1549.6 701.1 %reduce-scatter.21.cloned.1.call-start = ((), (), s32[]{:S(2)}) async-start(), calls=%async_computation.15 | async-start | bytes 9732096 | tf_op jit(solution)/shard_map/reduce_scatter | solution.py:287
  1560.0 830.8 %reduce-scatter.23.cloned.1.call-start = ((), (), s32[]{:S(2)}) async-start(), calls=%async_computation.16 | async-start | bytes 9732096 | tf_op jit(solution)/shard_map/reduce_scatter | solution.py:287
  1570.3 1033.9 %reduce-scatter.17.cloned.1.call-start = ((), (), s32[]{:S(2)}) async-start(), calls=%async_computation.13 | async-start | bytes 19464192 | tf_op jit(solution)/shard_map/reduce_scatter | solution.py:286
  1593.3 1223.9 %reduce-scatter.19.cloned.1.call-start = ((), (), s32[]{:S(2)}) async-start(), calls=%async_computation.14 | async-start | bytes 19464192 | tf_op jit(solution)/shard_map/reduce_scatter | solution.py:286
  1616.2 1333.9 %all-reduce.44.cloned.1.call-start = ((), (), s32[]{:S(2)}) async-start(), calls=%async_computation.10 | async-start | bytes 786432 | tf_op jit(solution)/shard_map/psum | solution.py:317
  (259 other events, 2108.8 us)
Sparse Core Ops, SparseCore 0:
  11.6 62.9 all-gather.16
  78.2 52.9 all-gather.18
  134.8 81.0 all-gather.20
  218.8 62.2 all-gather.22
  283.9 59.0 all-gather.24
  346.5 52.9 all-gather.26
  403.1 81.0 all-gather.28
  487.7 62.2 all-gather.30
  1519.0 132.2 all-reduce.45
  1657.3 99.5 reduce-scatter.12
  1762.2 97.9 reduce-scatter.14
  1866.7 118.1 reduce-scatter.10
  1990.6 118.3 reduce-scatter.8
  2115.8 134.8 reduce-scatter.20
  2256.4 134.4 reduce-scatter.22
  2398.3 205.8 reduce-scatter.16
  2611.6 205.5 reduce-scatter.18
  2823.7 126.3 all-reduce.43
where the time goes:
time: 2980 us; the launch traced here: 2970 us
  waiting for transfers between devices  1290 us (43%)
  matrix products  1250 us (42%)
  other arithmetic  257 us (9%)
  local copies, waits for them, and re-layouts  153 us (5%)
    reduce_scatter x2, waiting for transfers between devices, body(): lax.psum_scatter(grad_up, ('wide', 'narrow'), scatter_dimension=1, tiled=...  424 us
    reduce_scatter x2, waiting for transfers between devices, body(): lax.psum_scatter(grad_down, ('wide', 'narrow'), scatter_dimension=0, tile...  280 us
    reduce_scatter x2, waiting for transfers between devices, body(): lax.psum_scatter(grad_in, ('wide', 'narrow'), scatter_dimension=1, tiled=...  247 us
    reduce_scatter x2, waiting for transfers between devices, body(): lax.psum_scatter(grad_out, ('wide', 'narrow'), scatter_dimension=0, tiled...  205 us
    dot_general x12, matrix products, transform(): jnp.einsum('jn,sknc->sjkc', last_cos, rotated_im, precision=highest)  165 us
    dot_general x12, matrix products, transform(): jnp.einsum('kn,snac->skac', first_cos, real_part, precision=highest)  149 us
    dot_general x12, matrix products, transform(): jnp.einsum('jn,sknc->sjkc', last_cos, rotated_re, precision=highest)  131 us
    psum x2, waiting for transfers between devices, body(): lax.psum((gain_stack, shift_stack, in_bias_stack, short_stack, cond_stack...  131 us
  transfers between devices with their start and end apart: 18, of which 9 were waited for; matrix products, arithmetic and copies ran while one was open for 28% of the time, Pallas kernels for 0%

commit v1 on v0

v1 whole, which is shorter than its diff:
```python
import functools
import math

import jax
import jax.numpy as jnp
import numpy as np
from jax import lax
from jax.experimental import pallas as pl
from jax.experimental.pallas import tpu as pltpu
from jax.sharding import PartitionSpec as P

epsilon = 1e-05
f32 = jnp.float32
bf16 = jnp.bfloat16
AXES = ("wide", "narrow")
BLK = 256
BINS = 2 * BLK
CB = 256
PAD = 8
VMEM = 60 * 2**20
NN = (((1,), (0,)), ((), ()))
NT = (((1,), (1,)), ((), ()))
TN = (((0,), (0,)), ((), ()))
GELU_A = math.sqrt(2.0 / math.pi)
GELU_B = 0.044715


def dot(left, right, dims):
    return lax.dot_general(left, right, dims, preferred_element_type=f32)


def split_low(table):
    high = table.astype(jnp.bfloat16)
    low = (table - high.astype(np.float32)).astype(jnp.bfloat16)
    return np.concatenate([high, high, low], axis=1)


def spectrum_tables():
    t = np.arange(BLK, dtype=np.float64)[None, :]
    k = np.arange(BLK, dtype=np.float64)[:, None]
    angle = 2.0 * np.pi * ((k * t) % BINS) / BINS
    forward = np.concatenate([np.cos(angle), -np.sin(angle)], axis=0)
    forward[BLK] = np.where(np.arange(BLK) % 2 == 0, 1.0, -1.0)
    weight = np.full((BINS, 1), 2.0 / BINS)
    weight[0] = 1.0 / BINS
    weight[BLK] = 1.0 / BINS
    inverse = (forward * weight).T
    return forward.astype(np.float32), inverse.astype(np.float32)


FORWARD, INVERSE = spectrum_tables()


def transform(table, values):
    return dot(table, values.astype(bf16), NN)


def transform_fine(table, values):
    high = values.astype(bf16)
    low = (values - high.astype(f32)).astype(bf16)
    return dot(table, jnp.concatenate([high, low, high], axis=0), NN)


def fold(values):
    rows, cols = values.shape
    return jnp.sum(values.reshape(rows // 8, 8, cols), axis=0)


def loop_rows(total, step, body, init):
    def run(index, carry):
        return body(pl.multiple_of(index * step, step), carry)

    return lax.fori_loop(0, total // step, run, init)


def row_mask(start, rows, cols):
    return start + lax.broadcasted_iota(jnp.int32, (rows, cols), 0)


def earlier(ref, lead, start, rows, cols, split):
    ext = ref[lead + (pl.ds(start, rows + PAD), slice(None))]
    t = row_mask(start, rows, cols)
    one = jnp.where(t != split, pltpu.roll(ext, 1, 0)[PAD:], 0.0)
    two = jnp.where((t != split) & (t != split + 1), pltpu.roll(ext, 2, 0)[PAD:], 0.0)
    return ext[PAD:], one, two


def later(ref, lead, start, rows, cols, split):
    ext = ref[lead + (pl.ds(start, rows + PAD), slice(None))]
    total = rows + PAD
    t = row_mask(start, rows, cols)
    one = jnp.where(t + 1 != split, pltpu.roll(ext, total - 1, 0)[:rows], 0.0)
    two = jnp.where(
        (t + 2 != split) & (t + 1 != split), pltpu.roll(ext, total - 2, 0)[:rows], 0.0
    )
    return ext[:rows], one, two


def norm_parts(values):
    average = jnp.mean(values, axis=-1, keepdims=True)
    centered = values - average
    variance = jnp.mean(centered * centered, axis=-1, keepdims=True)
    rstd = lax.rsqrt(variance + epsilon)
    return centered * rstd, rstd


def part_place(part, boundary):
    block = jnp.where(part <= boundary, part, part - 1)
    return pl.multiple_of(block * BLK, BLK)


def part_keep(part, boundary, split, start):
    t = row_mask(start, BLK, CB)
    front = jnp.where(part <= boundary, 1, 0)
    return jnp.where(t < split, 1, 0) == front


def load_part(ref, part, parts, boundary, split):
    start = part_place(part, boundary)
    return jnp.where(part_keep(part, boundary, split, start), ref[pl.ds(start, BLK), :], 0.0)


def store_part(ref, part, boundary, split, values):
    start = part_place(part, boundary)
    keep = part_keep(part, boundary, split, start)
    ref[pl.ds(start, BLK), :] = jnp.where(keep, values, ref[pl.ds(start, BLK), :])


def first_row(shape):
    return lax.broadcasted_iota(jnp.int32, shape, 0) == 0


def sum_terms(terms):
    total = terms[0]
    for term in terms[1:]:
        total = total + term
    return total


def mixer_forward_kernel(
    split_ref,
    state_ref,
    norm_ref,
    chan_ref,
    win_ref,
    khat_ref,
    fwd_ref,
    inv_ref,
    wout_ref,
    middle_ref,
    second_ref,
    normed_ref,
    biased_ref,
    conv_ref,
    scale_ref,
    val_ref,
    query_ref,
    prod_ref,
    spec_ref,
    res_ref,
):
    step = pl.program_id(0)
    length, width = state_ref.shape
    split = split_ref[0]
    boundary = split // BLK
    parts = length // BLK + 1

    @pl.when(step == 0)
    def _():
        def norm(row, carry):
            hat, _ = norm_parts(state_ref[pl.ds(row, 64), :])
            normed_ref[pl.ds(row, 64), :] = (hat * norm_ref[0:1, :] + norm_ref[1:2, :]).astype(bf16)
            return carry

        loop_rows(length, 64, norm, 0)
        val_ref[0:PAD, :] = jnp.zeros((PAD, CB), f32)

    biased_ref[:, 0:PAD, :] = jnp.zeros((3, PAD, CB), f32)
    for stream in range(3):
        biased = dot(normed_ref[...], win_ref[stream], NT) + chan_ref[stream : stream + 1, :]
        biased_ref[stream, PAD:, :] = biased

    rows = 32

    def shorten(row, carry):
        out = []
        for stream in range(3):
            now, one, two = earlier(biased_ref, (stream,), row, rows, CB, split)
            out.append(
                chan_ref[3 + stream : 4 + stream, :] * now
                + chan_ref[6 + stream : 7 + stream, :] * one
                + chan_ref[9 + stream : 10 + stream, :] * two
            )
        query_ref[pl.ds(row, rows), :] = out[0]
        val_ref[pl.ds(row + PAD, rows), :] = out[2]
        prod_ref[pl.ds(row, rows), :] = out[1] * out[2]
        return carry

    loop_rows(length, rows, shorten, 0)

    def condition(row, total):
        now, one, two = earlier(val_ref, (), row, rows, CB, split)
        cond = chan_ref[12:13, :] * now + chan_ref[13:14, :] * one + chan_ref[14:15, :] * two
        return total + fold(cond * cond)

    squares = loop_rows(length, rows, condition, jnp.zeros((8, CB), f32))
    scale = jnp.sqrt(jnp.sum(squares, axis=0, keepdims=True) * (1.0 / length) + epsilon)
    scale_ref[...] = jnp.broadcast_to(scale, (8, CB))

    for part in range(parts):
        spec_ref[part] = transform_fine(
            fwd_ref[...], load_part(prod_ref, part, parts, boundary, split)
        )

    def pairs_into(part, bound):
        low = 0 if part <= bound else bound + 1
        return [(part - source, source) for source in range(low, part + 1)]

    for bound in range(parts - 1):

        @pl.when(boundary == bound)
        def _():
            def multiply(row, carry):
                k_re = [khat_ref[m, pl.ds(row, 8), :] for m in range(parts - 1)]
                k_im = [khat_ref[m, pl.ds(row + BLK, 8), :] for m in range(parts - 1)]
                s_re = [spec_ref[v, pl.ds(row, 8), :] for v in range(parts)]
                s_im = [spec_ref[v, pl.ds(row + BLK, 8), :] for v in range(parts)]
                for part in range(parts):
                    pairs = pairs_into(part, bound)
                    res_ref[part, pl.ds(row, 8), :] = sum_terms(
                        [k_re[m] * s_re[v] - k_im[m] * s_im[v] for m, v in pairs]
                    )
                    res_ref[part, pl.ds(row + BLK, 8), :] = sum_terms(
                        [k_re[m] * s_im[v] + k_im[m] * s_re[v] for m, v in pairs]
                    )
                return carry

            loop_rows(BLK, 8, multiply, 0)
            top = first_row((8, CB))
            for part in range(parts):
                pairs = pairs_into(part, bound)
                for base in (0, BLK):
                    real = sum_terms(
                        [khat_ref[m, base : base + 8, :] * spec_ref[v, base : base + 8, :] for m, v in pairs]
                    )
                    res_ref[part, base : base + 8, :] = jnp.where(
                        top, real, res_ref[part, base : base + 8, :]
                    )

    for part in range(parts):
        store_part(conv_ref, part, boundary, split, transform_fine(inv_ref[...], res_ref[part]))

    mixed = (query_ref[...] * scale * conv_ref[...]).astype(bf16)
    update = dot(mixed, wout_ref[...], NN)

    @pl.when(step == 0)
    def _():
        middle_ref[...] = update

    @pl.when(step > 0)
    def _():
        middle_ref[...] += update

    @pl.when(step == pl.num_programs(0) - 1)
    def _():
        def finish(row, carry):
            here = pl.ds(row, 64)
            middle = state_ref[here, :] + middle_ref[here, :] + norm_ref[4:5, :]
            middle_ref[here, :] = middle
            hat, _ = norm_parts(middle)
            second_ref[here, :] = (hat * norm_ref[2:3, :] + norm_ref[3:4, :]).astype(bf16)
            return carry

        loop_rows(length, 64, finish, 0)


def whole_block(shape):
    return pl.BlockSpec(shape, lambda *index: (0,) * len(shape))


def fixed_block(shape):
    return pl.BlockSpec(shape, lambda *index: (0,) * len(shape), pipeline_mode=pl.Buffered(1))


def mixer_forward(split, state, norm_pack, chan_pack, w_in, khat, w_out):
    length, width = state.shape
    steps = width // CB
    parts = length // BLK + 1
    forward = jnp.asarray(split_low(FORWARD))
    inverse = jnp.asarray(split_low(INVERSE))
    return pl.pallas_call(
        mixer_forward_kernel,
        grid=(steps,),
        in_specs=[
            pl.BlockSpec(memory_space=pltpu.SMEM),
            fixed_block((length, width)),
            fixed_block(norm_pack.shape),
            pl.BlockSpec((16, CB), lambda i: (0, i)),
            pl.BlockSpec((3, CB, width), lambda i: (0, i, 0)),
            pl.BlockSpec((parts - 1, BINS, CB), lambda i: (0, 0, i)),
            fixed_block(forward.shape),
            fixed_block(inverse.shape),
            pl.BlockSpec((CB, width), lambda i: (i, 0)),
        ],
        out_specs=[
            whole_block((length, width)),
            whole_block((length, width)),
            whole_block((length, width)),
            pl.BlockSpec((3, length + PAD, CB), lambda i: (0, 0, i)),
            pl.BlockSpec((length, CB), lambda i: (0, i)),
            pl.BlockSpec((8, CB), lambda i: (0, i)),
        ],
        out_shape=[
            jax.ShapeDtypeStruct((length, width), f32),
            jax.ShapeDtypeStruct((length, width), bf16),
            jax.ShapeDtypeStruct((length, width), bf16),
            jax.ShapeDtypeStruct((3, length + PAD, width), f32),
            jax.ShapeDtypeStruct((length, width), f32),
            jax.ShapeDtypeStruct((8, width), f32),
        ],
        scratch_shapes=[
            pltpu.VMEM((length + PAD, CB), f32),
            pltpu.VMEM((length, CB), f32),
            pltpu.VMEM((length, CB), f32),
            pltpu.VMEM((parts, BINS, CB), f32),
            pltpu.VMEM((parts, BINS, CB), f32),
        ],
        compiler_params=pltpu.CompilerParams(vmem_limit_bytes=VMEM),
        cost_estimate=cost(20e9, 40 * 2**20),
        name="mixer_forward",
    )(split, state, norm_pack, chan_pack, w_in.reshape(3, width, width), khat, forward, inverse, w_out)


PARTS = 2


def cost(flops, moved):
    return pl.CostEstimate(flops=int(flops), bytes_accessed=int(moved), transcendentals=0)


def flat(block):
    return block.reshape(-1, block.shape[-1])


def gated_forward_kernel(
    first, second_ref, gate_w_ref, value_w_ref, down_ref, middle_ref, norm_ref, gate_ref, value_ref, out_ref
):
    step = pl.program_id(0)
    length = second_ref.shape[0]
    rows = 256
    gate_w = flat(gate_w_ref[...])
    value_w = flat(value_w_ref[...])
    down_w = flat(down_ref[...])

    @pl.when(step == 0)
    def _():
        if first:
            out_ref[...] = middle_ref[...] + norm_ref[5:6, :]
        else:
            out_ref[...] = middle_ref[...]

    for row in range(0, length, rows):
        here = slice(row, row + rows)
        gate = dot(second_ref[here, :], gate_w, NT)
        value = dot(second_ref[here, :], value_w, NT)
        gate_ref[here, :] = gate.astype(bf16)
        value_ref[here, :] = value.astype(bf16)
        bent = jnp.tanh(GELU_A * gate * (1.0 + GELU_B * gate * gate))
        hidden = (0.5 * gate * (1.0 + bent) * value).astype(bf16)
        out_ref[here, :] += dot(hidden, down_w, NN)


def pieces_of(weight, group):
    grouped = weight.reshape(-1, PARTS, group // PARTS, weight.shape[-1])
    return [grouped[:, part] for part in range(PARTS)]


def gated_forward(second, up, down, before, norm_pack, first, block=768):
    length, width = second.shape
    piece = down.shape[1]
    hidden = down.shape[0] * piece
    steps = hidden // block
    tile = (block // piece, piece, width)
    return pl.pallas_call(
        functools.partial(gated_forward_kernel, first),
        grid=(steps,),
        in_specs=[
            fixed_block((length, width)),
            pl.BlockSpec(tile, lambda i: (i, 0, 0)),
            pl.BlockSpec(tile, lambda i: (i + steps, 0, 0)),
            pl.BlockSpec(tile, lambda i: (i, 0, 0)),
            fixed_block((length, width)),
            fixed_block(norm_pack.shape),
        ],
        out_specs=[
            pl.BlockSpec((length, block), lambda i: (0, i)),
            pl.BlockSpec((length, block), lambda i: (0, i)),
            whole_block((length, width)),
        ],
        out_shape=[
            jax.ShapeDtypeStruct((length, hidden), bf16),
            jax.ShapeDtypeStruct((length, hidden), bf16),
            jax.ShapeDtypeStruct((length, width), f32),
        ],
        compiler_params=pltpu.CompilerParams(vmem_limit_bytes=VMEM),
        cost_estimate=cost(6 * length * width * hidden, 20 * 2**20),
        name="gated_forward",
    )(second, up, up, down, before, norm_pack)


def norm_backward(values, grad_out, gain):
    hat, rstd = norm_parts(values)
    grad_hat = grad_out * gain
    mean_one = jnp.mean(grad_hat, axis=-1, keepdims=True)
    mean_two = jnp.mean(grad_hat * hat, axis=-1, keepdims=True)
    return rstd * (grad_hat - mean_one - hat * mean_two), grad_out * hat


def gated_backward_kernel(
    first,
    last,
    slots,
    me_ref,
    grad_ref,
    before_ref,
    second_ref,
    middle_ref,
    norm_ref,
    gate_ref,
    value_ref,
    gate_w_ref,
    value_w_ref,
    down_ref,
    one_ref,
    two_ref,
    out_ref,
    small_ref,
    glow_ref,
    hidden_ref,
    dgate_ref,
    dvalue_ref,
    stage_ref,
    sems,
):
    step = pl.program_id(0)
    steps = pl.num_programs(0)
    length, width = grad_ref.shape
    rows = 256
    count, piece, _ = gate_w_ref.shape
    side = step % 2
    gate_w = flat(gate_w_ref[...])
    value_w = flat(value_w_ref[...])
    down_w = flat(down_ref[...])

    @pl.when(step == 0)
    def _():
        glow_ref[...] = grad_ref[...].astype(bf16)
        if first:
            out_ref[...] = jnp.zeros_like(out_ref)
        else:
            out_ref[...] = before_ref[...]

    def copies(at_step, kind, item):
        source = stage_ref.at[at_step % 2, kind, pl.ds(item * piece, piece), :]
        half = at_step * count + item
        if not slots:
            if kind == 2:
                return source, [(None, two_ref.at[half])]
            return source, [(None, one_ref.at[half + kind * steps * count])]
        if kind == 2:
            mask = half ^ me_ref[0]
            rows_at = pl.ds(2 * piece, piece)
        else:
            mask = ((half >> 1) + kind * (steps * count >> 1)) ^ me_ref[0]
            rows_at = pl.ds((half & 1) * piece, piece)
        place = mask >> 1
        core = mask & 1
        return source, [
            (core == 0, one_ref.at[place, rows_at, :]),
            (core == 1, two_ref.at[place, rows_at, :]),
        ]

    def send(kind):
        def go(item, carry):
            source, targets = copies(step, kind, item)
            for condition, target in targets:
                move = pltpu.make_async_copy(source, target, sems.at[side, kind, item])
                if condition is None:
                    move.start()
                else:
                    pl.when(condition)(move.start)
            return carry

        lax.fori_loop(0, count, go, 0)

    def drain(at_step):
        def go(item, carry):
            for kind in range(3):
                source, targets = copies(at_step, kind, item)
                pltpu.make_async_copy(
                    source, targets[0][1], sems.at[at_step % 2, kind, item]
                ).wait()
            return carry

        lax.fori_loop(0, count, go, 0)

    for row in range(0, length, rows):
        here = slice(row, row + rows)
        grad_hidden = dot(glow_ref[here, :], down_w, NT)
        gate = gate_ref[here, :].astype(f32)
        value = value_ref[here, :].astype(f32)
        square = gate * gate
        bent = jnp.tanh(GELU_A * gate * (1.0 + GELU_B * square))
        half = 0.5 * (1.0 + bent)
        unit = half * gate
        slope = half + 0.5 * gate * (1.0 - bent * bent) * (GELU_A * (1.0 + 3.0 * GELU_B * square))
        hidden_ref[here, :] = (unit * value).astype(bf16)
        dgate = (grad_hidden * value * slope).astype(bf16)
        dvalue = (grad_hidden * unit).astype(bf16)
        dgate_ref[here, :] = dgate
        dvalue_ref[here, :] = dvalue
        out_ref[here, :] += dot(dgate, gate_w, NN) + dot(dvalue, value_w, NN)

    @pl.when(step > 1)
    def _():
        drain(step - 2)

    stage_ref[side, 0] = dot(dgate_ref[...], second_ref[...], TN).astype(bf16)
    send(0)
    stage_ref[side, 1] = dot(dvalue_ref[...], second_ref[...], TN).astype(bf16)
    send(1)
    stage_ref[side, 2] = dot(hidden_ref[...], glow_ref[...], TN).astype(bf16)
    send(2)

    @pl.when(step == steps - 1)
    def _():
        if not last:
            small_ref[...] = jnp.zeros_like(small_ref)
        else:

            def finish(row, carry):
                here = pl.ds(row, 32)
                grad_out = out_ref[here, :]
                grad = grad_ref[here, :]
                change, gain_rows = norm_backward(middle_ref[here, :], grad_out, norm_ref[2:3, :])
                total = grad + change
                out_ref[here, :] = total
                return (
                    carry[0] + fold(gain_rows),
                    carry[1] + fold(grad_out),
                    carry[2] + fold(total),
                    carry[3] + fold(grad),
                )

            zero = jnp.zeros((8, width), f32)
            sums = loop_rows(length, 32, finish, (zero, zero, zero, zero))
            small_ref[...] = jnp.concatenate(
                [jnp.sum(part, axis=0, keepdims=True) for part in sums]
                + [jnp.zeros((4, width), f32)],
                axis=0,
            )

        @pl.when(steps > 1)
        def _():
            drain(step - 1)

        drain(step)


def gated_backward(
    part, me, grad, before, second, middle, norm_pack, gate, value, up, down, size, block=768
):
    length, width = second.shape
    piece = down.shape[1]
    hidden = down.shape[0] * piece
    inner = hidden // block
    count = block // piece
    tile = (count, piece, width)
    slots = size == 32
    column = pl.BlockSpec((length, block), lambda i: (0, i))
    anywhere = pl.BlockSpec(memory_space=pl.ANY)
    if slots:
        places = [jax.ShapeDtypeStruct((size // 2, 3 * piece, width), bf16)] * 2
    else:
        places = [
            jax.ShapeDtypeStruct((up.shape[0], piece, width), bf16),
            jax.ShapeDtypeStruct((down.shape[0], piece, width), bf16),
        ]
    last = part == PARTS - 1
    return pl.pallas_call(
        functools.partial(gated_backward_kernel, part == 0, last, slots),
        grid=(inner,),
        in_specs=[
            pl.BlockSpec(memory_space=pltpu.SMEM),
            fixed_block((length, width)),
            fixed_block(before.shape),
            fixed_block((length, width)),
            fixed_block((length, width)),
            fixed_block(norm_pack.shape),
            column,
            column,
            pl.BlockSpec(tile, lambda i: (i, 0, 0)),
            pl.BlockSpec(tile, lambda i: (i + inner, 0, 0)),
            pl.BlockSpec(tile, lambda i: (i, 0, 0)),
        ],
        out_specs=[anywhere, anywhere, whole_block((length, width)), whole_block((8, width))],
        out_shape=places
        + [
            jax.ShapeDtypeStruct((length, width), f32),
            jax.ShapeDtypeStruct((8, width), f32),
        ],
        scratch_shapes=[
            pltpu.VMEM((length, width), bf16),
            pltpu.VMEM((length, block), bf16),
            pltpu.VMEM((length, block), bf16),
            pltpu.VMEM((length, block), bf16),
            pltpu.VMEM((2, 3, block, width), bf16),
            pltpu.SemaphoreType.DMA((2, 3, count)),
        ],
        compiler_params=pltpu.CompilerParams(vmem_limit_bytes=VMEM),
        cost_estimate=cost(12 * length * width * hidden, 20 * 2**20),
        name="gated_backward",
    )(me, grad, before, second, middle, norm_pack, gate, value, up, up, down)


def mixer_backward_kernel(
    first,
    last,
    split_ref,
    grad_ref,
    before_ref,
    state_ref,
    normed_ref,
    norm_ref,
    chan_ref,
    biased_ref,
    conv_ref,
    scale_ref,
    khat_ref,
    fwd_ref,
    inv_ref,
    wout_ref,
    win_ref,
    win_g_ref,
    wout_g_ref,
    kern_g_ref,
    chan_g_ref,
    out_ref,
    small_ref,
    mlow_ref,
    key_ref,
    val_ref,
    prod_ref,
    dconv_ref,
    mixed_ref,
    cond_ref,
    dpad_ref,
    low_ref,
    spec_ref,
    dspec_ref,
    res_ref,
    gram_ref,
):
    step = pl.program_id(0)
    length, width = state_ref.shape
    split = split_ref[0]
    boundary = split // BLK
    parts = length // BLK + 1
    rows = 32

    @pl.when(step == 0)
    def _():
        mlow_ref[...] = grad_ref[...].astype(bf16)
        val_ref[0:PAD, :] = jnp.zeros((PAD, CB), f32)
        cond_ref[length:, :] = jnp.zeros((PAD, CB), f32)
        dpad_ref[:, length:, :] = jnp.zeros((3, PAD, CB), f32)

    dconv_ref[...] = dot(mlow_ref[...], wout_ref[...], NT)
    scale = scale_ref[0:1, :]

    def gate(row, total):
        here = pl.ds(row, rows)
        out = []
        for stream in range(3):
            now, one, two = earlier(biased_ref, (stream,), row, rows, CB, split)
            out.append(
                chan_ref[3 + stream : 4 + stream, :] * now
                + chan_ref[6 + stream : 7 + stream, :] * one
                + chan_ref[9 + stream : 10 + stream, :] * two
            )
        query, key, value = out
        key_ref[here, :] = key
        val_ref[pl.ds(row + PAD, rows), :] = value
        prod_ref[here, :] = key * value
        grad = dconv_ref[here, :]
        conv = conv_ref[here, :]
        mixed_ref[here, :] = (query * scale * conv).astype(bf16)
        dpad_ref[0, here, :] = grad * scale * conv
        through = grad * query
        dconv_ref[here, :] = through * scale
        return total + fold(through * conv)

    scale_sum = loop_rows(length, rows, gate, jnp.zeros((8, CB), f32))
    grad_scale = jnp.sum(scale_sum, axis=0, keepdims=True)
    factor = grad_scale / (scale * float(length))

    def condition(row, carry):
        now, one, two = earlier(val_ref, (), row, rows, CB, split)
        cond_ref[pl.ds(row, rows), :] = (
            chan_ref[12:13, :] * now + chan_ref[13:14, :] * one + chan_ref[14:15, :] * two
        )
        return carry

    loop_rows(length, rows, condition, 0)

    for part in range(parts):
        spec_ref[part] = transform(fwd_ref[...], load_part(prod_ref, part, parts, boundary, split))
        dspec_ref[part] = transform(fwd_ref[...], load_part(dconv_ref, part, parts, boundary, split))

    def pairs_from(source, bound):
        high = bound if source <= bound else parts - 1
        return [(part - source, part) for part in range(source, high + 1)]

    def pairs_apart(lag, bound):
        found = []
        for source in range(parts - lag):
            if (source <= bound) == (source + lag <= bound):
                found.append((source, source + lag))
        return found

    odd_sign = jnp.where(lax.broadcasted_iota(jnp.int32, (8, CB), 0) % 2 == 0, 1.0, -1.0)

    def chain(grams):
        return [
            grams[lag] + odd_sign * grams[lag + 1] if lag + 1 < parts - 1 else grams[lag]
            for lag in range(parts - 1)
        ]

    def or_zero(terms):
        return sum_terms(terms) if terms else jnp.zeros((8, CB), f32)

    for bound in range(parts - 1):

        @pl.when(boundary == bound)
        def _():
            def multiply(row, carry):
                k_re = [khat_ref[m, pl.ds(row, 8), :] for m in range(parts - 1)]
                k_im = [khat_ref[m, pl.ds(row + BLK, 8), :] for m in range(parts - 1)]
                e_re = [dspec_ref[v, pl.ds(row, 8), :] for v in range(parts)]
                e_im = [dspec_ref[v, pl.ds(row + BLK, 8), :] for v in range(parts)]
                for source in range(parts):
                    pairs = pairs_from(source, bound)
                    res_ref[source, pl.ds(row, 8), :] = sum_terms(
                        [k_re[m] * e_re[v] + k_im[m] * e_im[v] for m, v in pairs]
                    )
                    res_ref[source, pl.ds(row + BLK, 8), :] = sum_terms(
                        [k_re[m] * e_im[v] - k_im[m] * e_re[v] for m, v in pairs]
                    )
                s_re = [spec_ref[v, pl.ds(row, 8), :] for v in range(parts)]
                s_im = [spec_ref[v, pl.ds(row + BLK, 8), :] for v in range(parts)]
                real, imag = [], []
                for lag in range(parts - 1):
                    pairs = pairs_apart(lag, bound)
                    real.append(
                        or_zero([s_re[j] * e_re[i] + s_im[j] * e_im[i] for j, i in pairs])
                    )
                    imag.append(
                        or_zero([s_re[j] * e_im[i] - s_im[j] * e_re[i] for j, i in pairs])
                    )
                for lag, (one, two) in enumerate(zip(chain(real), chain(imag))):
                    gram_ref[lag, pl.ds(row, 8), :] = one
                    gram_ref[lag, pl.ds(row + BLK, 8), :] = two
                return carry

            loop_rows(BLK, 8, multiply, 0)
            top = first_row((8, CB))
            for base in (0, BLK):
                tile = slice(base, base + 8)
                for source in range(parts):
                    real = sum_terms(
                        [khat_ref[m, tile, :] * dspec_ref[v, tile, :] for m, v in pairs_from(source, bound)]
                    )
                    res_ref[source, tile, :] = jnp.where(top, real, res_ref[source, tile, :])
                grams = [
                    or_zero([spec_ref[j, tile, :] * dspec_ref[i, tile, :] for j, i in pairs_apart(lag, bound)])
                    for lag in range(parts - 1)
                ]
                for lag, real in enumerate(chain(grams)):
                    gram_ref[lag, tile, :] = jnp.where(top, real, gram_ref[lag, tile, :])

    for part in range(parts):
        store_part(prod_ref, part, boundary, split, transform(inv_ref[...], res_ref[part]))
    for lag in range(parts - 1):
        kern_g_ref[lag * BLK : (lag + 1) * BLK, :] = transform(inv_ref[...], gram_ref[lag])

    def spread(row, carry):
        here = pl.ds(row, rows)
        change = prod_ref[here, :]
        value = val_ref[pl.ds(row + PAD, rows), :]
        dpad_ref[1, here, :] = change * value
        now, one, two = later(cond_ref, (), row, rows, CB, split)
        from_cond = chan_ref[12:13, :] * now + chan_ref[13:14, :] * one + chan_ref[14:15, :] * two
        dpad_ref[2, here, :] = change * key_ref[here, :] + factor * from_cond
        return (
            carry[0] + fold(value * now),
            carry[1] + fold(value * one),
            carry[2] + fold(value * two),
        )

    zero = jnp.zeros((8, CB), f32)
    cond_sums = loop_rows(length, rows, spread, (zero, zero, zero))
    sums = [None] * 12
    for stream in range(3):

        def back(row, carry, stream=stream):
            now, one, two = later(dpad_ref, (stream,), row, rows, CB, split)
            biased = biased_ref[stream, pl.ds(row + PAD, rows), :]
            change = (
                chan_ref[3 + stream : 4 + stream, :] * now
                + chan_ref[6 + stream : 7 + stream, :] * one
                + chan_ref[9 + stream : 10 + stream, :] * two
            )
            low_ref[stream, pl.ds(row, rows), :] = change.astype(bf16)
            return (
                carry[0] + fold(change),
                carry[1] + fold(biased * now),
                carry[2] + fold(biased * one),
                carry[3] + fold(biased * two),
            )

        got = loop_rows(length, rows, back, (zero, zero, zero, zero))
        for index in range(4):
            sums[3 * index + stream] = got[index]
    chan_g_ref[...] = jnp.concatenate(
        [jnp.sum(part, axis=0, keepdims=True) for part in sums]
        + [factor * jnp.sum(part, axis=0, keepdims=True) for part in cond_sums]
        + [jnp.zeros((1, CB), f32)],
        axis=0,
    )
    wout_g_ref[...] = dot(mixed_ref[...], mlow_ref[...], TN).astype(bf16)
    for stream in range(3):
        win_g_ref[stream] = dot(low_ref[stream], normed_ref[...], TN).astype(bf16)
    update = sum_terms([dot(low_ref[stream], win_ref[stream], NN) for stream in range(3)])

    @pl.when(step == 0)
    def _():
        if first:
            out_ref[...] = update
        else:
            out_ref[...] = before_ref[...] + update

    @pl.when(step > 0)
    def _():
        out_ref[...] += update

    if not last:
        small_ref[...] = jnp.zeros_like(small_ref)
        return

    @pl.when(step == pl.num_programs(0) - 1)
    def _():
        def finish(row, carry):
            here = pl.ds(row, 32)
            grad_out = out_ref[here, :]
            change, gain_rows = norm_backward(state_ref[here, :], grad_out, norm_ref[0:1, :])
            out_ref[here, :] = grad_ref[here, :] + change
            return carry[0] + fold(gain_rows), carry[1] + fold(grad_out)

        wide_zero = jnp.zeros((8, width), f32)
        got = loop_rows(length, 32, finish, (wide_zero, wide_zero))
        small_ref[...] = jnp.concatenate(
            [jnp.sum(part, axis=0, keepdims=True) for part in got] + [jnp.zeros((6, width), f32)],
            axis=0,
        )


def mixer_backward(start, steps, split, grad, before, state, normed, norm_pack, chan_pack, biased, conv, scale, khat, w_out, w_in):
    length, width = state.shape
    last = (start + steps) * CB == width
    parts = length // BLK + 1
    forward = jnp.asarray(FORWARD, bf16)
    inverse = jnp.asarray(INVERSE, bf16)
    full = fixed_block((length, width))
    tall = pltpu.VMEM((length, CB), f32)
    tall_pad = pltpu.VMEM((length + PAD, CB), f32)
    spectrum = pltpu.VMEM((parts, BINS, CB), f32)
    return pl.pallas_call(
        functools.partial(mixer_backward_kernel, start == 0, last),
        grid=(steps,),
        in_specs=[
            pl.BlockSpec(memory_space=pltpu.SMEM),
            full,
            fixed_block(before.shape),
            full,
            full,
            fixed_block(norm_pack.shape),
            pl.BlockSpec((16, CB), lambda i: (0, i + start)),
            pl.BlockSpec((3, length + PAD, CB), lambda i: (0, 0, i + start)),
            pl.BlockSpec((length, CB), lambda i: (0, i + start)),
            pl.BlockSpec((8, CB), lambda i: (0, i + start)),
            pl.BlockSpec((parts - 1, BINS, CB), lambda i: (0, 0, i + start)),
            fixed_block(forward.shape),
            fixed_block(inverse.shape),
            pl.BlockSpec((CB, width), lambda i: (i + start, 0)),
            pl.BlockSpec((3, CB, width), lambda i: (0, i + start, 0)),
        ],
        out_specs=[
            pl.BlockSpec((3, CB, width), lambda i: (0, i, 0)),
            pl.BlockSpec((CB, width), lambda i: (i, 0)),
            pl.BlockSpec((length, CB), lambda i: (0, i)),
            pl.BlockSpec((16, CB), lambda i: (0, i)),
            whole_block((length, width)),
            whole_block((8, width)),
        ],
        out_shape=[
            jax.ShapeDtypeStruct((3, steps * CB, width), bf16),
            jax.ShapeDtypeStruct((steps * CB, width), bf16),
            jax.ShapeDtypeStruct((length, steps * CB), f32),
            jax.ShapeDtypeStruct((16, steps * CB), f32),
            jax.ShapeDtypeStruct((length, width), f32),
            jax.ShapeDtypeStruct((8, width), f32),
        ],
        scratch_shapes=[
            pltpu.VMEM((length, width), bf16),
            tall,
            tall_pad,
            tall,
            tall,
            pltpu.VMEM((length, CB), bf16),
            tall_pad,
            pltpu.VMEM((3, length + PAD, CB), f32),
            pltpu.VMEM((3, length, CB), bf16),
            spectrum,
            spectrum,
            spectrum,
            pltpu.VMEM((parts - 1, BINS, CB), f32),
        ],
        compiler_params=pltpu.CompilerParams(vmem_limit_bytes=VMEM),
        cost_estimate=cost(12e9 * steps, 14 * 2**20 * steps),
        name="mixer_backward",
    )(
        split,
        grad,
        before,
        state,
        normed,
        norm_pack,
        chan_pack,
        biased,
        conv,
        scale,
        khat,
        forward,
        inverse,
        w_out,
        w_in.reshape(3, width, width),
    )


def filter_features(length, count):
    half = count // 2
    positions = np.arange(length, dtype=np.float64)[:, None]
    harmonics = np.arange(1, half + 1, dtype=np.float64)[None, :]
    angles = 2.0 * np.pi * ((positions * harmonics) % length) / length
    return np.concatenate([np.sin(angles), np.cos(angles)], axis=1).astype(np.float32)


def highest(left, right, dims):
    return lax.dot_general(left, right, dims, precision=lax.Precision.HIGHEST)


def filter_kernel_body(inner_ref, out_ref, decay_ref, fwd_ref, kernel_ref, khat_ref):
    length = inner_ref.shape[0]
    decay = decay_ref[0:1, :]
    level = jnp.sqrt(2.0 * decay)
    sign = jnp.where(lax.broadcasted_iota(jnp.int32, (BINS, CB), 0) % 2 == 0, 1.0, -1.0)
    before = None
    for block in range(length // BLK):
        here = slice(block * BLK, (block + 1) * BLK)
        profile = lax.dot_general(
            inner_ref[here, :],
            out_ref[...],
            NN,
            precision=lax.Precision.HIGHEST,
            preferred_element_type=f32,
        )
        position = row_mask(block * BLK, BLK, CB).astype(f32)
        kernel = profile * (jnp.exp(-position * decay) * level)
        kernel_ref[here, :] = kernel
        spectrum = transform_fine(fwd_ref[...], kernel)
        khat_ref[block] = spectrum if before is None else spectrum + sign * before
        before = spectrum


def filter_forward(length, decay, freq_in, freq_bias, freq_out):
    features = jnp.asarray(filter_features(length, freq_in.shape[0]))
    phase = highest(features, freq_in, NN) + freq_bias
    inner = jnp.sin(phase)
    width = decay.shape[0]
    hidden = inner.shape[1]
    table = jnp.asarray(split_low(FORWARD))
    blocks = length // BLK
    kernel, khat = pl.pallas_call(
        filter_kernel_body,
        grid=(width // CB,),
        in_specs=[
            fixed_block((length, hidden)),
            pl.BlockSpec((hidden, CB), lambda i: (0, i)),
            pl.BlockSpec((8, CB), lambda i: (0, i)),
            fixed_block(table.shape),
        ],
        out_specs=[
            pl.BlockSpec((length, CB), lambda i: (0, i)),
            pl.BlockSpec((blocks, BINS, CB), lambda i: (0, 0, i)),
        ],
        out_shape=[
            jax.ShapeDtypeStruct((length, width), f32),
            jax.ShapeDtypeStruct((blocks, BINS, width), f32),
        ],
        compiler_params=pltpu.CompilerParams(vmem_limit_bytes=VMEM),
        cost_estimate=cost(6e9, 10 * 2**20),
        name="filter_forward",
    )(inner, freq_out, jnp.broadcast_to(decay[None], (8, width)), table)
    positions = jnp.arange(length, dtype=f32)[:, None]
    window = jnp.exp(-positions * decay[None, :]) * jnp.sqrt(2.0 * decay)[None, :]
    return khat, (features, phase, inner, window, kernel, positions)


def filter_backward(grad_kernel, kept, decay, freq_out):
    features, phase, inner, window, kernel, positions = kept
    grad_profile = grad_kernel * window
    grad_freq_out = highest(inner, grad_profile, TN)
    grad_phase = highest(grad_profile, freq_out, NT) * jnp.cos(phase)
    grad_freq_in = highest(features, grad_phase, TN)
    grad_freq_bias = jnp.sum(grad_phase, axis=0)
    grad_decay = jnp.sum(grad_kernel * kernel * (0.5 / decay[None, :] - positions), axis=0)
    return grad_decay, grad_freq_in, grad_freq_bias, grad_freq_out


def cube_orders(size):
    bits = [1 << place for place in range(1, size.bit_length() - 1)]
    if len(bits) < 2:
        return [bits + [1], bits + [1]]
    return [bits + [1], bits[:-2] + [bits[-1], bits[-2]] + [1]]


def slot_table(order, size):
    table = np.zeros(size, np.int32)
    for slot in range(size):
        mask = sum(bit for place, bit in enumerate(order) if slot >> place & 1)
        table[mask] = slot
    return table


def swap(values, bit, size):
    return lax.ppermute(values, AXES, [(index, index ^ bit) for index in range(size)])


def cube_gather(block, order, size, me):
    held = block[None]
    for bit in order:
        held = jnp.concatenate([held, swap(held, bit, size)], axis=0)
    places = jnp.asarray(slot_table(order, size))[jnp.arange(size, dtype=jnp.int32) ^ me]
    return jnp.take(held, places, axis=0)


def cube_scatter(blocks, order, size, me):
    masks = np.zeros(size, np.int32)
    masks[slot_table(order, size)] = np.arange(size)
    held = jnp.take(blocks, jnp.asarray(masks) ^ me, axis=0)
    for place in reversed(range(len(order))):
        half = 1 << place
        got = swap(held[half:], order[place], size)
        held = held[:half].astype(f32) + got.astype(f32)
        if place:
            held = held.astype(bf16)
    return held[0]


def cube_sum(values, size):
    for place in range(size.bit_length() - 1):
        values = values + swap(values, 1 << place, size)
    return values


def halves(rows):
    if rows < 32:
        return rows // 2
    return (rows // 2 + 15) // 16 * 16


def gather_rows(block, size, me):
    cut = halves(block.shape[0])
    orders = cube_orders(size)
    one = cube_gather(block[:cut], orders[0], size, me)
    two = cube_gather(block[cut:], orders[1], size, me)
    return jnp.concatenate([one, two], axis=1)


def scatter_rows(blocks, size, me):
    cut = halves(blocks.shape[1])
    orders = cube_orders(size)
    one = cube_scatter(blocks[:, :cut], orders[0], size, me)
    two = cube_scatter(blocks[:, cut:], orders[1], size, me)
    return jnp.concatenate([one, two], axis=0)


def tie(value, *others):
    return lax.optimization_barrier((value,) + others)[0]


def gather_pieces(block, start_after=(), spread_after=()):
    size = 32
    if start_after:
        block = tie(block, *start_after)
    line = jnp.stack([block] + [swap(block, bit, size) for bit in (2, 4, 6)])
    if spread_after:
        line = tie(line, *spread_after)
    along_x = swap(line, 8, size)
    along_y = swap(line, 16, size)
    corner_one = swap(along_x[:2], 16, size)
    corner_two = swap(along_y[2:], 8, size)
    places = (0, 2, 4, 6)
    held = [
        (line, places),
        (along_x, tuple(8 + place for place in places)),
        (along_y, tuple(16 + place for place in places)),
        (corner_one, (24, 26)),
        (corner_two, (28, 30)),
    ]
    pieces = []
    for piece, masks in held:
        pieces.append((piece, masks))
        pieces.append((swap(piece, 1, size), tuple(mask + 1 for mask in masks)))
    return pieces, (line,), (along_x, along_y)


def place_kernel(masks, cuts, me_ref, *refs):
    pieces = refs[: len(masks)]
    targets = refs[len(masks) : len(masks) + len(cuts)]
    held, in_sems, out_sems = refs[-3:]
    loads = []
    slot = 0
    for index, (piece, own) in enumerate(zip(pieces, masks)):
        load = pltpu.make_async_copy(piece, held.at[slot : slot + len(own)], in_sems.at[index])
        load.start()
        loads.append((load, slot, own))
        slot += len(own)
    moves = []
    for load, slot, own in loads:
        load.wait()
        for place, mask in enumerate(own):
            device = me_ref[0] ^ mask
            start = 0
            for target, rows in zip(targets, cuts):
                move = pltpu.make_async_copy(
                    held.at[slot + place, start : start + rows, :],
                    target.at[device],
                    out_sems.at[len(moves)],
                )
                move.start()
                moves.append(move)
                start += rows
    for move in moves:
        move.wait()


def place_pieces(pieces, cuts, me):
    arrays = [piece for piece, _ in pieces]
    masks = [own for _, own in pieces]
    size = sum(len(own) for own in masks)
    width = arrays[0].shape[-1]
    anywhere = pl.BlockSpec(memory_space=pl.ANY)
    return pl.pallas_call(
        functools.partial(place_kernel, masks, cuts),
        in_specs=[pl.BlockSpec(memory_space=pltpu.SMEM)] + [anywhere] * len(arrays),
        out_specs=[anywhere] * len(cuts),
        out_shape=[jax.ShapeDtypeStruct((size, rows, width), bf16) for rows in cuts],
        scratch_shapes=[
            pltpu.VMEM((size, sum(cuts), width), bf16),
            pltpu.SemaphoreType.DMA((len(masks),)),
            pltpu.SemaphoreType.DMA((size * len(cuts),)),
        ],
        compiler_params=pltpu.CompilerParams(vmem_limit_bytes=VMEM),
        cost_estimate=cost(0, 2 * sum(cuts) * size * width * 2),
        name="place_pieces",
    )(me, *arrays)


def scatter_steps(keep, send, done):
    size = 32
    shape = (4, 4) + keep.shape[1:]
    keep = keep.reshape(shape)
    got = swap(send, 1, size).reshape(shape)
    yield [send]

    def both(group):
        return keep[group].astype(f32) + got[group].astype(f32)

    corner = both(3).astype(bf16)
    from_y = swap(corner[:2], 16, size)
    from_x = swap(corner[2:], 8, size)
    yield [corner]
    to_x = both(1)
    to_x = jnp.concatenate([to_x[:2] + from_y.astype(f32), to_x[2:]], axis=0).astype(bf16)
    to_y = both(2)
    to_y = jnp.concatenate([to_y[:2], to_y[2:] + from_x.astype(f32)], axis=0).astype(bf16)
    got_x, got_y = swap(to_x, 8, size), swap(to_y, 16, size)
    yield [to_x, to_y]
    line = both(0) + got_x.astype(f32) + got_y.astype(f32)
    low = [line[place].astype(bf16) for place in (1, 2, 3)]
    came = [swap(piece, 2 * place + 2, size) for place, piece in enumerate(low)]
    yield low
    done(sum_terms([line[0]] + [piece.astype(f32) for piece in came]))


def sum_steps(values, size, done):
    for place in range(size.bit_length() - 1):
        came = swap(values, 1 << place, size)
        yield [values]
        values = values + came
    done(values)


class Flight:
    def __init__(self):
        self.running = []

    def add(self, steps):
        self.running.append(steps)

    def advance(self):
        sent = []
        still = []
        for steps in self.running:
            try:
                sent.extend(next(steps))
                still.append(steps)
            except StopIteration:
                pass
        self.running = still
        return sent

    def finish(self):
        while self.running:
            self.advance()


def body(
    size,
    tokens,
    split_point,
    cotangent,
    norm_gain,
    norm_shift,
    in_weight,
    in_bias,
    short_taps,
    cond_taps,
    decay_rate,
    freq_in,
    freq_bias,
    freq_out,
    out_weight,
    out_bias,
    up_weight,
    down_weight,
    down_bias,
):
    layers = in_weight.shape[0]
    length, width = tokens.shape[1:]
    me = lax.axis_index(AXES)
    split = split_point.astype(jnp.int32)
    state = tokens[0].astype(f32)
    in_rows = in_weight.shape[2]
    out_rows = out_weight.shape[1]

    packs = []
    for layer in range(layers):
        norm_pack = jnp.concatenate(
            [
                jnp.stack([norm_gain[layer, 0], norm_shift[layer, 0]]),
                jnp.stack([norm_gain[layer, 1], norm_shift[layer, 1]]),
                out_bias[layer][None],
                down_bias[layer][None],
                jnp.zeros((2, width), f32),
            ]
        )
        chan_pack = jnp.concatenate(
            [
                in_bias[layer].reshape(3, width),
                short_taps[layer].reshape(9, width),
                cond_taps[layer],
                jnp.zeros((1, width), f32),
            ]
        )
        packs.append((norm_pack, chan_pack))

    mine = me.astype(jnp.int32)[None]
    up_rows = up_weight.shape[2]
    down_rows = down_weight.shape[1]
    special = size == 32
    mixer_w = [None] * layers
    gated_w = [None] * layers
    lines = {}
    after_start, after_spread = (), ()
    for layer in range(layers):
        mixer_block = jnp.concatenate([in_weight[layer].T, out_weight[layer]], axis=0)
        up_own, down_own = up_weight[layer].T, down_weight[layer]
        if special:
            pieces, after_start, after_spread = gather_pieces(mixer_block, after_start, after_spread)
            lines[layer, "mixer"] = after_start + after_spread
            (mixer_rows,) = place_pieces(pieces, (in_rows + out_rows,), mine)
            gated_w[layer] = []
            halved = up_own.reshape(2, PARTS, -1, width)
            for part in range(PARTS):
                block = jnp.concatenate(
                    [halved[0, part], halved[1, part], down_own.reshape(PARTS, -1, width)[part]], axis=0
                )
                pieces, after_start, after_spread = gather_pieces(block, after_start, after_spread)
                lines[layer, part] = after_start + after_spread
                up, down = place_pieces(pieces, (up_rows // PARTS, down_rows // PARTS), mine)
                gated_w[layer].append((up.reshape(-1, down_rows // PARTS, width), down))
        else:
            mixer_rows = gather_rows(mixer_block, size, me)
            gated_rows = gather_rows(jnp.concatenate([up_own, down_own], axis=0), size, me)
            ups = pieces_of(gated_rows[:, :up_rows].reshape(-1, width), 96)
            downs = pieces_of(gated_rows[:, up_rows:].reshape(-1, width), 96)
            gated_w[layer] = list(zip(ups, downs))
        mixer_w[layer] = (
            mixer_rows[:, :in_rows].reshape(3 * width, width),
            mixer_rows[:, in_rows:].reshape(width, width),
        )

    filters = [
        filter_forward(length, decay_rate[layer], freq_in[layer], freq_bias[layer], freq_out[layer])
        for layer in range(layers)
    ]

    saved = []
    outputs = []
    for layer in range(layers):
        w_in, w_out = mixer_w[layer]
        norm_pack, chan_pack = packs[layer]
        if special:
            state = tie(state, *lines[layer, 0][:1])
        middle, second, normed, biased, conv, scale = mixer_forward(
            split, state, norm_pack, chan_pack, w_in, filters[layer][0], w_out
        )
        total = middle
        kept = []
        for part in range(PARTS):
            up, down = gated_w[layer][part]
            if special and part + 1 < PARTS:
                second = tie(second, *lines[layer, part + 1])
            elif special and layer + 1 < layers:
                second = tie(second, *lines[layer + 1, "mixer"][:1])
            gate, value, total = gated_forward(second, up, down, total, norm_pack, part == 0)
            kept.append((gate, value))
        saved.append((state, normed, biased, conv, scale, middle, second, kept))
        outputs.append(total)
        state = total

    gradient = cotangent[0].astype(f32)
    big = [[None] * 4 for _ in range(layers)]
    small = [None] * layers
    flight = Flight()
    nothing = jnp.zeros((8, width), f32)
    for layer in reversed(range(layers)):
        w_in, w_out = mixer_w[layer]
        norm_pack, chan_pack = packs[layer]
        state_in, normed, biased, conv, scale, middle, second, kept = saved[layer]
        passed = nothing
        gated_g = []
        owned = [None] * PARTS
        for part in range(PARTS):
            gate, value = kept[part]
            up, down = gated_w[layer][part]
            one, two, passed, sums_two = gated_backward(
                part,
                mine,
                tie(gradient, *flight.advance()),
                passed,
                second,
                middle,
                norm_pack,
                gate,
                value,
                up,
                down,
                size,
            )
            gated_g.append((one, two))
            if special:
                flight.add(scatter_steps(one, two, functools.partial(owned.__setitem__, part)))
        grad_middle = passed
        passed = nothing
        found = []
        splits = [3] if layer else [1, 1, 1]
        start = 0
        for steps in splits:
            *got, passed, sums_one = mixer_backward(
                start,
                steps,
                split,
                tie(grad_middle, *flight.advance()),
                passed,
                state_in,
                normed,
                norm_pack,
                chan_pack,
                biased,
                conv,
                scale,
                filters[layer][0],
                w_out,
                w_in,
            )
            found.append(got)
            start += steps
        gradient = passed
        in_g = jnp.concatenate([got[0] for got in found], axis=1)
        out_g = jnp.concatenate([got[1] for got in found], axis=0)
        kernel_g = jnp.concatenate([got[2] for got in found], axis=1)
        chan_g = jnp.concatenate([got[3] for got in found], axis=1)
        mixer_g = jnp.concatenate(
            [in_g.reshape(size, in_rows, width), out_g.reshape(size, out_rows, width)], axis=1
        )

        mixer_own = [None]
        if special:
            order = jnp.arange(size // 2, dtype=jnp.int32) * 2 ^ me
            keep, send = [
                mixer_g.at[places].get(mode="promise_in_bounds") for places in (order, order ^ 1)
            ]
            flight.add(scatter_steps(keep, send, functools.partial(mixer_own.__setitem__, 0)))
        else:
            up_g = jnp.stack([one for one, _ in gated_g], axis=1).reshape(size, -1, width)
            down_g = jnp.stack([two for _, two in gated_g], axis=1).reshape(size, -1, width)
            owned = (scatter_rows(up_g, size, me), scatter_rows(down_g, size, me))
            mixer_own[0] = scatter_rows(mixer_g, size, me)
        grad_decay, grad_freq_in, grad_freq_bias, grad_freq_out = filter_backward(
            kernel_g, filters[layer][1], decay_rate[layer], freq_out[layer]
        )
        pieces = [
            jnp.stack([sums_one[0], sums_two[0]]),
            jnp.stack([sums_one[1], sums_two[1]]),
            chan_g[0:3].reshape(3 * width),
            chan_g[3:12].reshape(3, 3 * width),
            chan_g[12:15],
            grad_decay,
            grad_freq_in,
            grad_freq_bias,
            grad_freq_out,
            sums_two[2],
            sums_two[3],
        ]
        vector = jnp.concatenate([piece.reshape(-1) for piece in pieces])
        vector = jnp.pad(vector, (0, -vector.size % 1024)).reshape(-1, 128)
        summed = [None]
        flight.add(sum_steps(vector, size, functools.partial(summed.__setitem__, 0)))
        small[layer] = (pieces, summed)
        big[layer] = (owned, mixer_own)
    flight.finish()

    for layer in range(layers):
        owned, mixer_own = big[layer]
        if special:
            piece = down_rows // PARTS
            up_own = jnp.concatenate(
                [part[at * piece : (at + 1) * piece] for at in range(2) for part in owned], axis=0
            )
            down_own = jnp.concatenate([part[2 * piece :] for part in owned], axis=0)
        else:
            up_own, down_own = owned
        big[layer] = (mixer_own[0][:in_rows].T, mixer_own[0][in_rows:], up_own.T, down_own)
        pieces, summed = small[layer]
        vector = summed[0].reshape(-1)
        taken = []
        start = 0
        for piece in pieces:
            taken.append(vector[start : start + piece.size].reshape(piece.shape))
            start += piece.size
        small[layer] = taken

    small = [jnp.stack([small[layer][index] for layer in range(layers)]) for index in range(11)]
    big = [jnp.stack([big[layer][index] for layer in range(layers)]) for index in range(4)]
    return (
        jnp.stack(outputs)[:, None],
        gradient[None],
        small[0],
        small[1],
        big[0],
        small[2],
        small[3],
        small[4],
        small[5],
        small[6],
        small[7],
        small[8],
        big[1],
        small[9],
        big[2],
        big[3],
        small[10],
    )


def solution(mesh):
    pairs = P(AXES, None, None)
    columns = P(None, None, AXES)
    rows = P(None, AXES, None)
    in_specs = (
        (pairs, P(AXES), pairs, P(), P(), columns)
        + (P(),) * 7
        + (rows, P(), columns, rows, P())
    )
    out_specs = (
        (P(None, AXES, None, None), pairs, P(), P(), columns)
        + (P(),) * 7
        + (rows, P(), columns, rows, P())
    )
    size = math.prod(mesh.shape.values())
    return jax.shard_map(
        functools.partial(body, size),
        mesh=mesh,
        in_specs=in_specs,
        out_specs=out_specs,
        check_vma=False,
    )
```

time: 2980 us -> 1040 us (0.35)
  matrix products: 1250 us -> 28.5 us
  waiting for transfers between devices: 1290 us -> 192 us
  Pallas kernels: 0 us -> 483 us
  other arithmetic: 257 us -> 98.2 us
  starting transfers between devices: 1.52 us -> 122 us
  local copies, waits for them, and re-layouts: 153 us -> 100 us
    dot_general x122 -> x8, matrix products: 1250 us -> 28.5 us  [highest(): return lax.dot_general(left, right, dims, precision=lax.Precision.HIGHEST)]
    reduce_scatter x8 -> x0, waiting for transfers between devices: 1160 us -> none  [the longest x2 424 us: body(): lax.psum_scatter(grad_up, ('wide', 'narrow'), scatter_dimension=1, tiled=...]
    pallas_call x0 -> x22, Pallas kernels: none -> 483 us  [the longest x4 148 us: gated_backward(): pl.pallas_call(functools.partial(gated_backward_kernel, part == 0, last,...]
    ppermute x0 -> x130, waiting for transfers between devices: none -> 192 us  [swap(): lax.ppermute(values, AXES, [(index, index ^ bit) for index in range(size)])]
    psum x2 -> x0, waiting for transfers between devices: 131 us -> none  [body(): lax.psum((gain_stack, shift_stack, in_bias_stack, short_stack, cond_stack...]
    ppermute x0 -> x130, starting transfers between devices: none -> 122 us  [swap(): lax.ppermute(values, AXES, [(index, index ^ bit) for index in range(size)])]
    reduce_sum x23 -> x2, other arithmetic: 90.9 us -> 4.24 us  [filter_backward(): jnp.sum(grad_kernel * kernel * (0.5 / decay[None, :] - positions), axis=0)]
    add_any x5 -> x0, other arithmetic: 73.5 us -> none  [the longest x2 57.9 us: spectral_conv(): spectrum_re = signal_re * kernel_re - signal_im * kernel_im]
  transfers between devices with their start and end apart: 18 -> 130, of which waited for: 9 -> 43; matrix products, arithmetic and copies ran while one was open for 28% -> 21% of each run, Pallas kernels for 0% -> 47%
where the time goes in v1:
time: 1040 us; the launch traced here: 1030 us
  Pallas kernels  483 us (46%)
  waiting for transfers between devices  192 us (18%)
  starting transfers between devices  122 us (12%)
  local copies, waits for them, and re-layouts  100 us (10%)
  other arithmetic  98.2 us (9%)
  matrix products  28.5 us (3%)
    ppermute x130, waiting for transfers between devices, swap(): lax.ppermute(values, AXES, [(index, index ^ bit) for index in range(size)])  192 us
    pallas_call x4, Pallas kernels, gated_backward(): pl.pallas_call(functools.partial(gated_backward_kernel, part == 0, last,...  148 us
    pallas_call x4, Pallas kernels, mixer_backward(): pl.pallas_call(functools.partial(mixer_backward_kernel, start == 0, last)...  141 us
    ppermute x130, starting transfers between devices, swap(): lax.ppermute(values, AXES, [(index, index ^ bit) for index in range(size)])  122 us
    pallas_call x2, Pallas kernels, mixer_forward(): pl.pallas_call(mixer_forward_kernel, grid=(steps,), in_specs=[pl.BlockSpe...  81.4 us
    pallas_call x4, Pallas kernels, gated_forward(): pl.pallas_call(functools.partial(gated_forward_kernel, first), grid=(step...  58.6 us
    pallas_call x6, Pallas kernels, place_pieces(): pl.pallas_call(functools.partial(place_kernel, masks, cuts), in_specs=[pl...  34 us
    dot_general x8, matrix products, highest(): return lax.dot_general(left, right, dims, precision=lax.Precision.HIGHEST)  28.5 us
  transfers between devices with their start and end apart: 130, of which 43 were waited for; matrix products, arithmetic and copies ran while one was open for 21% of the time, Pallas kernels for 47%

profile of v1, /device:TPU:0, one launch (start us, length us, event | category | flops | bytes accessed | tf_op | source)
XLA Modules:
  0.0 1027.8 jit_solution(1924021275621267139)
XLA Ops:
  11.5 4.9 collective-permute-done.1
  30.6 13.5 %collective-permute-done.4 = bf16[144,768]{1,0:T(8,128)(2,1)S(1)} collective-permute-done((bf16[144,768]{1,0:T(8,128)(2,1)S(1)}, bf16[144,768]{1,0:T(8,128)(2,1)S(1)}, u32[]{:S(2)}, u32[]{:S(2)}) %collective-permute-start.4) | collective-permute-done | bytes 221216 | tf_op jit(solution)/shard_map/ppermute | solution.py:1056
  51.8 4.6 collective-permute-done.17
  56.3 7.2 collective-permute-start.15
  76.5 10.1 filter_forward.2
  95.0 5.8 collective-permute-done.24
  116.1 4.6 collective-permute-done.37.refs_8_
  123.5 9.0 collective-permute-done.40
  133.7 10.3 filter_forward.3
  168.7 8.4 collective-permute-done.53
  177.1 5.6 collective-permute-start.51
  197.6 40.5 %mixer_forward.2 = (f32[1024,768]{1,0:T(8,128)}, bf16[1024,768]{1,0:T(8,128)(2,1)}, bf16[1024,768]{1,0:T(8,128)(2,1)}, f32[3,1032,768]{2,1,0:T(8,128)}, f32[1024,768]{1,0:T(8,128)}, /*index=5*/f32[8,768]{1,0:T(8,128)}) custom-call(s32[1]{0:T(128)S(6)} %copy.91.split_ref, f32[1024,768]{1,0:T(8,128)} %bitcast_convert_fusion.state_ref, ...), custom_call_target="tpu_custom_call" | custom-call | flops 20000000000 | bytes 41943040 | tf_op jit(solution)/shard_map/mixer_forward/pallas_call | solution.py:291
  238.1 6.4 place_pieces.8
  248.6 14.8 %gated_forward.4 = (bf16[1024,1536]{1,0:T(8,128)(2,1)}, bf16[1024,1536]{1,0:T(8,128)(2,1)}, f32[1024,768]{1,0:T(8,128)}) custom-call(bf16[1024,768]{1,0:T(8,128)(2,1)} %get-tuple-element.121.second_ref, bf16[64,48,768]{2,1,0:T(8,128)(2,1)} %bitcast.360, bf16[64,48,768]{2,1,0:T(8,128)(2,1)} %bitcast.361, bf16[32,48,768]{2,1,0:T(8,128)(2,1)} %get-tuple-element.125.down_ref, ...), custom_call_target="tpu_custom_call" | custom-call | flops 7247757312 | bytes 20971520 | tf_op jit(solution)/shard_map/gated_forward/pallas_call | solution.py:384
  263.4 6.4 place_pieces.7
  273.8 14.6 %gated_forward.5 = (bf16[1024,1536]{1,0:T(8,128)(2,1)}, bf16[1024,1536]{1,0:T(8,128)(2,1)}, f32[1024,768]{1,0:T(8,128)}) custom-call(bf16[1024,768]{1,0:T(8,128)(2,1)} %get-tuple-element.121.second_ref, bf16[64,48,768]{2,1,0:T(8,128)(2,1)} %bitcast.356, bf16[64,48,768]{2,1,0:T(8,128)(2,1)} %bitcast.357, bf16[32,48,768]{2,1,0:T(8,128)(2,1)} %get-tuple-element.123.down_ref, ...), custom_call_target="tpu_custom_call" | custom-call | flops 7247757312 | bytes 20971520 | tf_op jit(solution)/shard_map/gated_forward/pallas_call | solution.py:384
  300.2 40.8 %mixer_forward.3 = (f32[1024,768]{1,0:T(8,128)}, bf16[1024,768]{1,0:T(8,128)(2,1)}, bf16[1024,768]{1,0:T(8,128)(2,1)}, f32[3,1032,768]{2,1,0:T(8,128)}, f32[1024,768]{1,0:T(8,128)}, /*index=5*/f32[8,768]{1,0:T(8,128)}) custom-call(s32[1]{0:T(128)S(6)} %copy.91.split_ref, f32[1024,768]{1,0:T(8,128)} %get-tuple-element.131.state_ref, ...), custom_call_target="tpu_custom_call" | custom-call | flops 20000000000 | bytes 41943040 | tf_op jit(solution)/shard_map/mixer_forward/pallas_call | solution.py:291
  341.6 6.4 place_pieces.11
  348.0 14.7 %gated_forward.6 = (bf16[1024,1536]{1,0:T(8,128)(2,1)}, bf16[1024,1536]{1,0:T(8,128)(2,1)}, f32[1024,768]{1,0:T(8,128)}) custom-call(bf16[1024,768]{1,0:T(8,128)(2,1)} %get-tuple-element.136.second_ref, bf16[64,48,768]{2,1,0:T(8,128)(2,1)} %bitcast.368, bf16[64,48,768]{2,1,0:T(8,128)(2,1)} %bitcast.369, bf16[32,48,768]{2,1,0:T(8,128)(2,1)} %get-tuple-element.140.down_ref, ...), custom_call_target="tpu_custom_call" | custom-call | flops 7247757312 | bytes 20971520 | tf_op jit(solution)/shard_map/gated_forward/pallas_call | solution.py:384
  363.3 32.1 %gated_backward.4 = (bf16[16,144,768]{2,1,0:T(8,128)(2,1)}, bf16[16,144,768]{2,1,0:T(8,128)(2,1)}, f32[1024,768]{1,0:T(8,128)}, f32[8,768]{1,0:T(8,128)}) custom-call(s32[1]{0:T(128)} %bitcast.25.me_ref, f32[1024,768]{1,0:T(8,128)} %bitcast_convert_fusion.1.grad_ref, f32[8,768]{1,0:T(8,128)} %broadcast_in_dim.40.before_ref, ...), custom_call_target="tpu_custom_call" | custom-call | flops 14495514624 | bytes 20971520 | tf_op jit(solution)/shard_map/gated_backward/pallas_call | solution.py:590
  400.3 8.8 collective-permute-done.63.refs_8_
  413.8 6.4 place_pieces.10
  420.2 14.5 %gated_forward.7 = (bf16[1024,1536]{1,0:T(8,128)(2,1)}, bf16[1024,1536]{1,0:T(8,128)(2,1)}, f32[1024,768]{1,0:T(8,128)}) custom-call(bf16[1024,768]{1,0:T(8,128)(2,1)} %get-tuple-element.136.second_ref, bf16[64,48,768]{2,1,0:T(8,128)(2,1)} %bitcast.364, bf16[64,48,768]{2,1,0:T(8,128)(2,1)} %bitcast.365, bf16[32,48,768]{2,1,0:T(8,128)(2,1)} %get-tuple-element.138.down_ref, ...), custom_call_target="tpu_custom_call" | custom-call | flops 7247757312 | bytes 20971520 | tf_op jit(solution)/shard_map/gated_forward/pallas_call | solution.py:384
  434.7 42.0 %gated_backward.5 = (bf16[16,144,768]{2,1,0:T(8,128)(2,1)}, bf16[16,144,768]{2,1,0:T(8,128)(2,1)}, f32[1024,768]{1,0:T(8,128)}, f32[8,768]{1,0:T(8,128)}) custom-call(s32[1]{0:T(128)} %bitcast.25.me_ref, f32[1024,768]{1,0:T(8,128)} %bitcast_convert_fusion.1.grad_ref, f32[1024,768]{1,0:T(8,128)} %get-tuple-element.148.before_ref, ...), custom_call_target="tpu_custom_call" | custom-call | flops 14495514624 | bytes 20971520 | tf_op jit(solution)/shard_map/gated_backward/pallas_call | solution.py:590
  477.8 5.2 maximum_bitcast_fusion
  486.8 62.7 %mixer_backward.4 = (bf16[3,768,768]{2,1,0:T(8,128)(2,1)}, bf16[768,768]{1,0:T(8,128)(2,1)}, f32[1024,768]{1,0:T(8,128)}, f32[16,768]{1,0:T(8,128)}, f32[1024,768]{1,0:T(8,128)}, /*index=5*/f32[8,768]{1,0:T(8,128)}) custom-call(s32[1]{0:T(128)S(6)} %copy.91.split_ref, f32[1024,768]{1,0:T(8,128)} %get-tuple-element.154.grad_ref, ...), custom_call_target="tpu_custom_call" | custom-call | flops 35999997952 | bytes 44040192 | tf_op jit(solution)/shard_map/mixer_backward/pallas_call | solution.py:887
  554.9 6.4 fusion.89
  580.3 4.4 gather_fusion.1
  591.1 6.0 collective-permute-done.82
  601.1 11.5 %collective-permute-done.83 = f32[552,128]{1,0:T(8,128)S(1)} collective-permute-done((f32[552,128]{1,0:T(8,128)S(1)}, f32[552,128]{1,0:T(8,128)S(1)}, u32[]{:S(2)}, u32[]{:S(2)}) %collective-permute-start.83) | collective-permute-done | bytes 282656 | tf_op jit(solution)/shard_map/ppermute | solution.py:1056
  619.9 32.0 %gated_backward.6 = (bf16[16,144,768]{2,1,0:T(8,128)(2,1)}, bf16[16,144,768]{2,1,0:T(8,128)(2,1)}, f32[1024,768]{1,0:T(8,128)}, f32[8,768]{1,0:T(8,128)}) custom-call(s32[1]{0:T(128)} %bitcast.25.me_ref, f32[1024,768]{1,0:T(8,128)} %get-tuple-element.172.grad_ref, f32[8,768]{1,0:T(8,128)} %broadcast_in_dim.40.before_ref, ...), custom_call_target="tpu_custom_call" | custom-call | flops 14495514624 | bytes 20971520 | tf_op jit(solution)/shard_map/gated_backward/pallas_call | solution.py:590
  661.6 4.9 collective-permute-done.78
  686.5 5.0 collective-permute-done.98
  704.8 41.5 %gated_backward.7 = (bf16[16,144,768]{2,1,0:T(8,128)(2,1)}, bf16[16,144,768]{2,1,0:T(8,128)(2,1)}, f32[1024,768]{1,0:T(8,128)}, f32[8,768]{1,0:T(8,128)}) custom-call(s32[1]{0:T(128)} %bitcast.25.me_ref, f32[1024,768]{1,0:T(8,128)} %get-tuple-element.172.grad_ref, f32[1024,768]{1,0:T(8,128)} %get-tuple-element.173.before_ref, ...), custom_call_target="tpu_custom_call" | custom-call | flops 14495514624 | bytes 20971520 | tf_op jit(solution)/shard_map/gated_backward/pallas_call | solution.py:590
  750.4 7.1 collective-permute-done.93
  761.8 6.2 collective-permute-done.96
  786.6 5.3 collective-permute-done.88
  799.0 22.3 %mixer_backward.5 = (bf16[3,256,768]{2,1,0:T(8,128)(2,1)}, bf16[256,768]{1,0:T(8,128)(2,1)}, f32[1024,256]{1,0:T(8,128)}, f32[16,256]{1,0:T(8,128)}, f32[1024,768]{1,0:T(8,128)}, /*index=5*/f32[8,768]{1,0:T(8,128)}) custom-call(s32[1]{0:T(128)S(6)} %copy.91.split_ref, f32[1024,768]{1,0:T(8,128)} %get-tuple-element.182.grad_ref, ...), custom_call_target="tpu_custom_call" | custom-call | flops 12000000000 | bytes 14680064 | tf_op jit(solution)/shard_map/mixer_backward/pallas_call | solution.py:887
  840.4 23.3 %mixer_backward.6 = (bf16[3,256,768]{2,1,0:T(8,128)(2,1)}, bf16[256,768]{1,0:T(8,128)(2,1)}, f32[1024,256]{1,0:T(8,128)}, f32[16,256]{1,0:T(8,128)}, f32[1024,768]{1,0:T(8,128)}, /*index=5*/f32[8,768]{1,0:T(8,128)}) custom-call(s32[1]{0:T(128)S(6)} %copy.91.split_ref, f32[1024,768]{1,0:T(8,128)} %get-tuple-element.182.grad_ref, ...), custom_call_target="tpu_custom_call" | custom-call | flops 12000000000 | bytes 14680064 | tf_op jit(solution)/shard_map/mixer_backward/pallas_call | solution.py:887
  871.3 32.5 %mixer_backward.7 = (bf16[3,256,768]{2,1,0:T(8,128)(2,1)}, bf16[256,768]{1,0:T(8,128)(2,1)}, f32[1024,256]{1,0:T(8,128)}, f32[16,256]{1,0:T(8,128)}, f32[1024,768]{1,0:T(8,128)}, /*index=5*/f32[8,768]{1,0:T(8,128)}) custom-call(s32[1]{0:T(128)S(6)} %copy.91.split_ref, f32[1024,768]{1,0:T(8,128)} %get-tuple-element.182.grad_ref, ...), custom_call_target="tpu_custom_call" | custom-call | flops 12000000000 | bytes 14680064 | tf_op jit(solution)/shard_map/mixer_backward/pallas_call | solution.py:887
  925.4 6.9 collective-permute-done.100
  932.6 11.5 %collective-permute-done.119 = bf16[4,144,768]{2,1,0:T(8,128)(2,1)S(1)} collective-permute-done((bf16[4,144,768]{2,1,0:T(8,128)(2,1)}, bf16[4,144,768]{2,1,0:T(8,128)(2,1)S(1)}, u32[]{:S(2)}, u32[]{:S(2)}) %collective-permute-start.119) | collective-permute-done | bytes 884768 | tf_op jit(solution)/shard_map/ppermute | solution.py:1056
  957.5 4.5 gather_fusion.3
  964.9 6.1 collective-permute-done.122
  975.1 5.6 collective-permute-done.103
  989.4 4.9 collective-permute-done.108
  999.9 9.4 collective-permute-done.109
  1021.0 5.0 collective-permute-done.111
  (736 shorter events, 361.5 us)
Async XLA Ops:
  44.3 29.4 %collective-permute-start.19 = (bf16[4,144,768]{2,1,0:T(8,128)(2,1)S(1)}, bf16[4,144,768]{2,1,0:T(8,128)(2,1)S(1)}, u32[]{:S(2)}, u32[]{:S(2)}) collective-permute-start(bf16[4,144,768]{2,1,0:T(8,128)(2,1)S(1)} %pad_maximum_fusion.5.refs_0_), channel_id=1, source_target_pairs={{0,16},{1,17},{2,18},{3,19},{4,20},{5,21},{6,22},{7,23},{8,24},{9,... | collective-permute-start | bytes 2654216 | tf_op jit(solution)/shard_map/ppermute | solution.py:1056
  44.9 28.9 %collective-permute-start.18 = (bf16[4,144,768]{2,1,0:T(8,128)(2,1)S(1)}, bf16[4,144,768]{2,1,0:T(8,128)(2,1)}, u32[]{:S(2)}, u32[]{:S(2)}) collective-permute-start(bf16[4,144,768]{2,1,0:T(8,128)(2,1)S(1)} %pad_maximum_fusion.5.refs_0_), channel_id=1, source_target_pairs={{0,8},{1,9},{2,10},{3,11},{4,12},{5,13},{6,14},{7,15},{8,0},{9,1},... | collective-permute-start | bytes 2654216 | tf_op jit(solution)/shard_map/ppermute | solution.py:1056
  46.1 28.3 %collective-permute-start.8 = (bf16[4,96,768]{2,1,0:T(8,128)(2,1)S(1)}, bf16[4,96,768]{2,1,0:T(8,128)(2,1)S(1)}, u32[]{:S(2)}, u32[]{:S(2)}) collective-permute-start(bf16[4,96,768]{2,1,0:T(8,128)(2,1)S(1)} %pad_maximum_fusion.17.refs_0_), channel_id=1, source_target_pairs={{0,1},{1,0},{2,3},{3,2},{4,5},{5,4},{6,7},{7,6},{8,9},{9,8},{10,11... | collective-permute-start | bytes 1769480 | tf_op jit(solution)/shard_map/ppermute | solution.py:1056
  73.8 34.3 %collective-permute-start.21 = (bf16[4,144,768]{2,1,0:T(8,128)(2,1)S(1)}, bf16[4,144,768]{2,1,0:T(8,128)(2,1)}, u32[]{:S(2)}, u32[]{:S(2)}) collective-permute-start(bf16[4,144,768]{2,1,0:T(8,128)(2,1)S(1)} %pad_maximum_fusion.6.refs_0_), channel_id=1, source_target_pairs={{0,16},{1,17},{2,18},{3,19},{4,20},{5,21},{6,22},{7,23},{8,24},{9,... | collective-permute-start | bytes 2654216 | tf_op jit(solution)/shard_map/ppermute | solution.py:1056
  74.3 34.2 %collective-permute-start.20 = (bf16[4,144,768]{2,1,0:T(8,128)(2,1)S(1)}, bf16[4,144,768]{2,1,0:T(8,128)(2,1)}, u32[]{:S(2)}, u32[]{:S(2)}) collective-permute-start(bf16[4,144,768]{2,1,0:T(8,128)(2,1)S(1)} %pad_maximum_fusion.6.refs_0_), channel_id=1, source_target_pairs={{0,8},{1,9},{2,10},{3,11},{4,12},{5,13},{6,14},{7,15},{8,0},{9,1},... | collective-permute-start | bytes 2654216 | tf_op jit(solution)/shard_map/ppermute | solution.py:1056
  123.4 30.7 %collective-permute-start.25 = (bf16[4,144,768]{2,1,0:T(8,128)(2,1)S(1)}, bf16[4,144,768]{2,1,0:T(8,128)(2,1)}, u32[]{:S(2)}, u32[]{:S(2)}) collective-permute-start(bf16[4,144,768]{2,1,0:T(8,128)(2,1)S(1)} %pad_maximum_fusion.6.refs_0_), channel_id=1, source_target_pairs={{0,1},{1,0},{2,3},{3,2},{4,5},{5,4},{6,7},{7,6},{8,9},{9,8},{10,11... | collective-permute-start | bytes 2654216 | tf_op jit(solution)/shard_map/ppermute | solution.py:1056
  154.1 41.5 %collective-permute-start.55 = (bf16[4,144,768]{2,1,0:T(8,128)(2,1)S(1)}, bf16[4,144,768]{2,1,0:T(8,128)(2,1)S(1)}, u32[]{:S(2)}, u32[]{:S(2)}) collective-permute-start(bf16[4,144,768]{2,1,0:T(8,128)(2,1)S(1)} %pad_maximum_fusion.7.refs_0_), channel_id=1, source_target_pairs={{0,16},{1,17},{2,18},{3,19},{4,20},{5,21},{6,22},{7,23},{8,24},{9,... | collective-permute-start | bytes 2654216 | tf_op jit(solution)/shard_map/ppermute | solution.py:1056
  155.6 41.5 %collective-permute-start.54 = (bf16[4,144,768]{2,1,0:T(8,128)(2,1)S(1)}, bf16[4,144,768]{2,1,0:T(8,128)(2,1)}, u32[]{:S(2)}, u32[]{:S(2)}) collective-permute-start(bf16[4,144,768]{2,1,0:T(8,128)(2,1)S(1)} %pad_maximum_fusion.7.refs_0_), channel_id=1, source_target_pairs={{0,8},{1,9},{2,10},{3,11},{4,12},{5,13},{6,14},{7,15},{8,0},{9,1},... | collective-permute-start | bytes 2654216 | tf_op jit(solution)/shard_map/ppermute | solution.py:1056
  165.3 30.2 %collective-permute-start.31 = (bf16[2,144,768]{2,1,0:T(8,128)(2,1)}, bf16[2,144,768]{2,1,0:T(8,128)(2,1)}, u32[]{:S(2)}, u32[]{:S(2)}) collective-permute-start(bf16[2,144,768]{2,1,0:T(8,128)(2,1)} %collective-permute-done.30.refs_8_), channel_id=1, source_target_pairs={{0,1},{1,0},{2,3},{3,2},{4,5},{5,4},{6,7},{7,6},{8,9},{9,8},{10,11... | collective-permute-start | bytes 1327112 | tf_op jit(solution)/shard_map/ppermute | solution.py:1056
  168.6 26.3 %collective-permute-start.52 = (bf16[144,768]{1,0:T(8,128)(2,1)S(1)}, bf16[144,768]{1,0:T(8,128)(2,1)S(1)}, u32[]{:S(2)}, u32[]{:S(2)}) collective-permute-start(bf16[144,768]{1,0:T(8,128)(2,1)S(1)} %copy-done.44), channel_id=1, source_target_pairs={{0,4},{1,5},{2,6},{3,7},{4,0},{5,1},{6,2},{7,3},{8,12},{9,13},{10,... | collective-permute-start | bytes 663560 | tf_op jit(solution)/shard_map/ppermute | solution.py:1056
  194.9 50.9 %collective-permute-start.27 = (bf16[4,144,768]{2,1,0:T(8,128)(2,1)}, bf16[4,144,768]{2,1,0:T(8,128)(2,1)}, u32[]{:S(2)}, u32[]{:S(2)}) collective-permute-start(bf16[4,144,768]{2,1,0:T(8,128)(2,1)} %collective-permute-done.21.refs_4_), channel_id=1, source_target_pairs={{0,1},{1,0},{2,3},{3,2},{4,5},{5,4},{6,7},{7,6},{8,9},{9,8},{10,11... | collective-permute-start | bytes 2654216 | tf_op jit(solution)/shard_map/ppermute | solution.py:1056
  195.0 53.1 %collective-permute-start.26 = (bf16[4,144,768]{2,1,0:T(8,128)(2,1)}, bf16[4,144,768]{2,1,0:T(8,128)(2,1)}, u32[]{:S(2)}, u32[]{:S(2)}) collective-permute-start(bf16[4,144,768]{2,1,0:T(8,128)(2,1)} %collective-permute-done.20.refs_2_), channel_id=1, source_target_pairs={{0,1},{1,0},{2,3},{3,2},{4,5},{5,4},{6,7},{7,6},{8,9},{9,8},{10,11... | collective-permute-start | bytes 2654216 | tf_op jit(solution)/shard_map/ppermute | solution.py:1056
  195.5 51.0 %collective-permute-start.29 = (bf16[2,144,768]{2,1,0:T(8,128)(2,1)}, bf16[2,144,768]{2,1,0:T(8,128)(2,1)}, u32[]{:S(2)}, u32[]{:S(2)}) collective-permute-start(bf16[2,144,768]{2,1,0:T(8,128)(2,1)} %collective-permute-done.28.refs_6_), channel_id=1, source_target_pairs={{0,1},{1,0},{2,3},{3,2},{4,5},{5,4},{6,7},{7,6},{8,9},{9,8},{10,11... | collective-permute-start | bytes 1327112 | tf_op jit(solution)/shard_map/ppermute | solution.py:1056
  195.6 50.3 %collective-permute-start.49 = (bf16[2,96,768]{2,1,0:T(8,128)(2,1)}, bf16[2,96,768]{2,1,0:T(8,128)(2,1)S(1)}, u32[]{:S(2)}, u32[]{:S(2)}) collective-permute-start(bf16[2,96,768]{2,1,0:T(8,128)(2,1)} %slice.1025), channel_id=1, source_target_pairs={{0,8},{1,9},{2,10},{3,11},{4,12},{5,13},{6,14},{7,15},{8,0},{9,1},... | collective-permute-start | bytes 884744 | tf_op jit(solution)/shard_map/ppermute | solution.py:1056
  197.1 49.3 %collective-permute-start.47 = (bf16[2,96,768]{2,1,0:T(8,128)(2,1)S(1)}, bf16[2,96,768]{2,1,0:T(8,128)(2,1)}, u32[]{:S(2)}, u32[]{:S(2)}) collective-permute-start(bf16[2,96,768]{2,1,0:T(8,128)(2,1)S(1)} %slice.1024), channel_id=1, source_target_pairs={{0,16},{1,17},{2,18},{3,19},{4,20},{5,21},{6,22},{7,23},{8,24},{9,... | collective-permute-start | bytes 884744 | tf_op jit(solution)/shard_map/ppermute | solution.py:1056
  245.8 26.0 %collective-permute-start.46 = (bf16[4,96,768]{2,1,0:T(8,128)(2,1)S(1)}, bf16[4,96,768]{2,1,0:T(8,128)(2,1)}, u32[]{:S(2)}, u32[]{:S(2)}) collective-permute-start(bf16[4,96,768]{2,1,0:T(8,128)(2,1)S(1)} %copy-done.30), channel_id=1, source_target_pairs={{0,1},{1,0},{2,3},{3,2},{4,5},{5,4},{6,7},{7,6},{8,9},{9,8},{10,11... | collective-permute-start | bytes 1769480 | tf_op jit(solution)/shard_map/ppermute | solution.py:1056
  245.9 25.8 %collective-permute-start.50 = (bf16[2,96,768]{2,1,0:T(8,128)(2,1)S(1)}, bf16[2,96,768]{2,1,0:T(8,128)(2,1)}, u32[]{:S(2)}, u32[]{:S(2)}) collective-permute-start(bf16[2,96,768]{2,1,0:T(8,128)(2,1)S(1)} %collective-permute-done.49.refs_8_), channel_id=1, source_target_pairs={{0,1},{1,0},{2,3},{3,2},{4,5},{5,4},{6,7},{7,6},{8,9},{9,8},{10,11... | collective-permute-start | bytes 884744 | tf_op jit(solution)/shard_map/ppermute | solution.py:1056
  246.4 27.0 %collective-permute-start.48 = (bf16[2,96,768]{2,1,0:T(8,128)(2,1)}, bf16[2,96,768]{2,1,0:T(8,128)(2,1)}, u32[]{:S(2)}, u32[]{:S(2)}) collective-permute-start(bf16[2,96,768]{2,1,0:T(8,128)(2,1)} %collective-permute-done.47.refs_6_), channel_id=1, source_target_pairs={{0,1},{1,0},{2,3},{3,2},{4,5},{5,4},{6,7},{7,6},{8,9},{9,8},{10,11... | collective-permute-start | bytes 884744 | tf_op jit(solution)/shard_map/ppermute | solution.py:1056
  246.5 53.2 %collective-permute-start.57 = (bf16[4,144,768]{2,1,0:T(8,128)(2,1)S(1)}, bf16[4,144,768]{2,1,0:T(8,128)(2,1)}, u32[]{:S(2)}, u32[]{:S(2)}) collective-permute-start(bf16[4,144,768]{2,1,0:T(8,128)(2,1)S(1)} %pad_maximum_fusion.8.refs_0_), channel_id=1, source_target_pairs={{0,16},{1,17},{2,18},{3,19},{4,20},{5,21},{6,22},{7,23},{8,24},{9,... | collective-permute-start | bytes 2654216 | tf_op jit(solution)/shard_map/ppermute | solution.py:1056
  248.1 52.0 %collective-permute-start.56 = (bf16[4,144,768]{2,1,0:T(8,128)(2,1)S(1)}, bf16[4,144,768]{2,1,0:T(8,128)(2,1)}, u32[]{:S(2)}, u32[]{:S(2)}) collective-permute-start(bf16[4,144,768]{2,1,0:T(8,128)(2,1)S(1)} %pad_maximum_fusion.8.refs_0_), channel_id=1, source_target_pairs={{0,8},{1,9},{2,10},{3,11},{4,12},{5,13},{6,14},{7,15},{8,0},{9,1},... | collective-permute-start | bytes 2654216 | tf_op jit(solution)/shard_map/ppermute | solution.py:1056
  271.8 27.3 %collective-permute-start.70 = (bf16[2,144,768]{2,1,0:T(8,128)(2,1)}, bf16[2,144,768]{2,1,0:T(8,128)(2,1)S(1)}, u32[]{:S(2)}, u32[]{:S(2)}) collective-permute-start(bf16[2,144,768]{2,1,0:T(8,128)(2,1)} %slice.1033), channel_id=1, source_target_pairs={{0,8},{1,9},{2,10},{3,11},{4,12},{5,13},{6,14},{7,15},{8,0},{9,1},... | collective-permute-start | bytes 1327112 | tf_op jit(solution)/shard_map/ppermute | solution.py:1056
  273.4 26.2 %collective-permute-start.68 = (bf16[2,144,768]{2,1,0:T(8,128)(2,1)S(1)}, bf16[2,144,768]{2,1,0:T(8,128)(2,1)}, u32[]{:S(2)}, u32[]{:S(2)}) collective-permute-start(bf16[2,144,768]{2,1,0:T(8,128)(2,1)S(1)} %slice.1032), channel_id=1, source_target_pairs={{0,16},{1,17},{2,18},{3,19},{4,20},{5,21},{6,22},{7,23},{8,24},{9,... | collective-permute-start | bytes 1327112 | tf_op jit(solution)/shard_map/ppermute | solution.py:1056
  288.4 52.7 %collective-permute-start.65 = (bf16[4,144,768]{2,1,0:T(8,128)(2,1)S(1)}, bf16[4,144,768]{2,1,0:T(8,128)(2,1)}, u32[]{:S(2)}, u32[]{:S(2)}) collective-permute-start(bf16[4,144,768]{2,1,0:T(8,128)(2,1)S(1)} %pad_maximum_fusion.7.refs_0_), channel_id=1, source_target_pairs={{0,1},{1,0},{2,3},{3,2},{4,5},{5,4},{6,7},{7,6},{8,9},{9,8},{10,11... | collective-permute-start | bytes 2654216 | tf_op jit(solution)/shard_map/ppermute | solution.py:1056
  299.1 42.5 %collective-permute-start.67 = (bf16[4,144,768]{2,1,0:T(8,128)(2,1)S(1)}, bf16[4,144,768]{2,1,0:T(8,128)(2,1)}, u32[]{:S(2)}, u32[]{:S(2)}) collective-permute-start(bf16[4,144,768]{2,1,0:T(8,128)(2,1)S(1)} %collective-permute-done.55.refs_4_), channel_id=1, source_target_pairs={{0,1},{1,0},{2,3},{3,2},{4,5},{5,4},{6,7},{7,6},{8,9},{9,8},{10,11... | collective-permute-start | bytes 2654216 | tf_op jit(solution)/shard_map/ppermute | solution.py:1056
  299.6 41.9 %collective-permute-start.66 = (bf16[4,144,768]{2,1,0:T(8,128)(2,1)}, bf16[4,144,768]{2,1,0:T(8,128)(2,1)}, u32[]{:S(2)}, u32[]{:S(2)}) collective-permute-start(bf16[4,144,768]{2,1,0:T(8,128)(2,1)} %collective-permute-done.54.refs_2_), channel_id=1, source_target_pairs={{0,1},{1,0},{2,3},{3,2},{4,5},{5,4},{6,7},{7,6},{8,9},{9,8},{10,11... | collective-permute-start | bytes 2654216 | tf_op jit(solution)/shard_map/ppermute | solution.py:1056
  299.7 41.8 %collective-permute-start.71 = (bf16[2,144,768]{2,1,0:T(8,128)(2,1)S(1)}, bf16[2,144,768]{2,1,0:T(8,128)(2,1)}, u32[]{:S(2)}, u32[]{:S(2)}) collective-permute-start(bf16[2,144,768]{2,1,0:T(8,128)(2,1)S(1)} %collective-permute-done.70.refs_8_), channel_id=1, source_target_pairs={{0,1},{1,0},{2,3},{3,2},{4,5},{5,4},{6,7},{7,6},{8,9},{9,8},{10,11... | collective-permute-start | bytes 1327112 | tf_op jit(solution)/shard_map/ppermute | solution.py:1056
  300.1 41.4 %collective-permute-start.69 = (bf16[2,144,768]{2,1,0:T(8,128)(2,1)}, bf16[2,144,768]{2,1,0:T(8,128)(2,1)}, u32[]{:S(2)}, u32[]{:S(2)}) collective-permute-start(bf16[2,144,768]{2,1,0:T(8,128)(2,1)} %collective-permute-done.68.refs_6_), channel_id=1, source_target_pairs={{0,1},{1,0},{2,3},{3,2},{4,5},{5,4},{6,7},{7,6},{8,9},{9,8},{10,11... | collective-permute-start | bytes 1327112 | tf_op jit(solution)/shard_map/ppermute | solution.py:1056
  341.1 58.8 %collective-permute-start.58 = (bf16[4,144,768]{2,1,0:T(8,128)(2,1)S(1)}, bf16[4,144,768]{2,1,0:T(8,128)(2,1)S(1)}, u32[]{:S(2)}, u32[]{:S(2)}) collective-permute-start(bf16[4,144,768]{2,1,0:T(8,128)(2,1)S(1)} %pad_maximum_fusion.8.refs_0_), channel_id=1, source_target_pairs={{0,1},{1,0},{2,3},{3,2},{4,5},{5,4},{6,7},{7,6},{8,9},{9,8},{10,11... | collective-permute-start | bytes 2654216 | tf_op jit(solution)/shard_map/ppermute | solution.py:1056
  395.3 87.7 %collective-permute-start.72 = (bf16[16,144,768]{2,1,0:T(8,128)(2,1)}, bf16[16,144,768]{2,1,0:T(8,128)(2,1)}, u32[]{:S(2)}, u32[]{:S(2)}) collective-permute-start(bf16[16,144,768]{2,1,0:T(8,128)(2,1)} %get-tuple-element.146), channel_id=1, source_target_pairs={{0,1},{1,0},{2,3},{3,2},{4,5},{5,4},{6,7},{7,6},{8,9},{9,8},{10,11... | collective-permute-start | bytes 10616840 | tf_op jit(solution)/shard_map/ppermute | solution.py:1056
  476.7 136.4 %collective-permute-start.77 = (bf16[16,144,768]{2,1,0:T(8,128)(2,1)}, bf16[16,144,768]{2,1,0:T(8,128)(2,1)}, u32[]{:S(2)}, u32[]{:S(2)}) collective-permute-start(bf16[16,144,768]{2,1,0:T(8,128)(2,1)} %get-tuple-element.153), channel_id=1, source_target_pairs={{0,1},{1,0},{2,3},{3,2},{4,5},{5,4},{6,7},{7,6},{8,9},{9,8},{10,11... | collective-permute-start | bytes 10616840 | tf_op jit(solution)/shard_map/ppermute | solution.py:1056
  587.7 112.6 %collective-permute-start.80 = (bf16[16,96,768]{2,1,0:T(8,128)(2,1)}, bf16[16,96,768]{2,1,0:T(8,128)(2,1)}, u32[]{:S(2)}, u32[]{:S(2)}) collective-permute-start(bf16[16,96,768]{2,1,0:T(8,128)(2,1)} %gather_fusion.1), channel_id=1, source_target_pairs={{0,1},{1,0},{2,3},{3,2},{4,5},{5,4},{6,7},{7,6},{8,9},{9,8},{10,11... | collective-permute-start | bytes 7077896 | tf_op jit(solution)/shard_map/ppermute | solution.py:1056
  590.5 62.9 %collective-permute-start.76 = (bf16[4,144,768]{2,1,0:T(8,128)(2,1)}, bf16[4,144,768]{2,1,0:T(8,128)(2,1)}, u32[]{:S(2)}, u32[]{:S(2)}) collective-permute-start(bf16[4,144,768]{2,1,0:T(8,128)(2,1)} %pad_maximum_fusion.10), channel_id=1, source_target_pairs={{0,16},{1,17},{2,18},{3,19},{4,20},{5,21},{6,22},{7,23},{8,24},{9,... | collective-permute-start | bytes 2654216 | tf_op jit(solution)/shard_map/ppermute | solution.py:1056
  600.3 55.1 %collective-permute-start.74 = (bf16[4,144,768]{2,1,0:T(8,128)(2,1)}, bf16[4,144,768]{2,1,0:T(8,128)(2,1)}, u32[]{:S(2)}, u32[]{:S(2)}) collective-permute-start(bf16[4,144,768]{2,1,0:T(8,128)(2,1)} %pad_maximum_fusion.9), channel_id=1, source_target_pairs={{0,8},{1,9},{2,10},{3,11},{4,12},{5,13},{6,14},{7,15},{8,0},{9,1},... | collective-permute-start | bytes 2654216 | tf_op jit(solution)/shard_map/ppermute | solution.py:1056
  612.6 40.6 %collective-permute-start.84 = (f32[552,128]{1,0:T(8,128)S(1)}, f32[552,128]{1,0:T(8,128)S(1)}, u32[]{:S(2)}, u32[]{:S(2)}) collective-permute-start(f32[552,128]{1,0:T(8,128)S(1)} %add.302), channel_id=1, source_target_pairs={{0,8},{1,9},{2,10},{3,11},{4,12},{5,13},{6,14},{7,15},{8,0},{9,1},... | collective-permute-start | bytes 847880 | tf_op jit(solution)/shard_map/ppermute | solution.py:1056
  618.3 49.4 %collective-permute-start.79 = (bf16[2,144,768]{2,1,0:T(8,128)(2,1)}, bf16[2,144,768]{2,1,0:T(8,128)(2,1)}, u32[]{:S(2)}, u32[]{:S(2)}) collective-permute-start(bf16[2,144,768]{2,1,0:T(8,128)(2,1)} %get-tuple-element.296), channel_id=1, source_target_pairs={{0,8},{1,9},{2,10},{3,11},{4,12},{5,13},{6,14},{7,15},{8,0},{9,1},... | collective-permute-start | bytes 1327112 | tf_op jit(solution)/shard_map/ppermute | solution.py:1056
  679.7 100.0 %collective-permute-start.85 = (bf16[16,144,768]{2,1,0:T(8,128)(2,1)}, bf16[16,144,768]{2,1,0:T(8,128)(2,1)}, u32[]{:S(2)}, u32[]{:S(2)}) collective-permute-start(bf16[16,144,768]{2,1,0:T(8,128)(2,1)} %get-tuple-element.171), channel_id=1, source_target_pairs={{0,1},{1,0},{2,3},{3,2},{4,5},{5,4},{6,7},{7,6},{8,9},{9,8},{10,11... | collective-permute-start | bytes 10616840 | tf_op jit(solution)/shard_map/ppermute | solution.py:1056
  696.0 61.9 %collective-permute-start.129 = (bf16[144,768]{1,0:T(8,128)(2,1)}, bf16[144,768]{1,0:T(8,128)(2,1)S(1)}, u32[]{:S(2)}, u32[]{:S(2)}) collective-permute-start(bf16[144,768]{1,0:T(8,128)(2,1)} %get-tuple-element.286), channel_id=1, source_target_pairs={{0,6},{1,7},{2,4},{3,5},{4,2},{5,3},{6,0},{7,1},{8,14},{9,15},{10,... | collective-permute-start | bytes 663560 | tf_op jit(solution)/shard_map/ppermute | solution.py:1056
  697.5 63.1 %collective-permute-start.128 = (bf16[144,768]{1,0:T(8,128)(2,1)}, bf16[144,768]{1,0:T(8,128)(2,1)S(1)}, u32[]{:S(2)}, u32[]{:S(2)}) collective-permute-start(bf16[144,768]{1,0:T(8,128)(2,1)} %get-tuple-element.287), channel_id=1, source_target_pairs={{0,4},{1,5},{2,6},{3,7},{4,0},{5,1},{6,2},{7,3},{8,12},{9,13},{10,... | collective-permute-start | bytes 663560 | tf_op jit(solution)/shard_map/ppermute | solution.py:1056
  697.5 63.1 %collective-permute-start.127 = (bf16[144,768]{1,0:T(8,128)(2,1)}, bf16[144,768]{1,0:T(8,128)(2,1)}, u32[]{:S(2)}, u32[]{:S(2)}) collective-permute-start(bf16[144,768]{1,0:T(8,128)(2,1)} %get-tuple-element.288), channel_id=1, source_target_pairs={{0,2},{1,3},{2,0},{3,1},{4,6},{5,7},{6,4},{7,5},{8,10},{9,11},{10,... | collective-permute-start | bytes 663560 | tf_op jit(solution)/shard_map/ppermute | solution.py:1056
  704.3 44.3 %collective-permute-start.95 = (bf16[2,96,768]{2,1,0:T(8,128)(2,1)}, bf16[2,96,768]{2,1,0:T(8,128)(2,1)}, u32[]{:S(2)}, u32[]{:S(2)}) collective-permute-start(bf16[2,96,768]{2,1,0:T(8,128)(2,1)} %get-tuple-element.312), channel_id=1, source_target_pairs={{0,8},{1,9},{2,10},{3,11},{4,12},{5,13},{6,14},{7,15},{8,0},{9,1},... | collective-permute-start | bytes 884744 | tf_op jit(solution)/shard_map/ppermute | solution.py:1056
  760.6 72.3 %collective-permute-start.90 = (bf16[16,144,768]{2,1,0:T(8,128)(2,1)}, bf16[16,144,768]{2,1,0:T(8,128)(2,1)}, u32[]{:S(2)}, u32[]{:S(2)}) collective-permute-start(bf16[16,144,768]{2,1,0:T(8,128)(2,1)} %get-tuple-element.179), channel_id=1, source_target_pairs={{0,1},{1,0},{2,3},{3,2},{4,5},{5,4},{6,7},{7,6},{8,9},{9,8},{10,11... | collective-permute-start | bytes 10616840 | tf_op jit(solution)/shard_map/ppermute | solution.py:1056
  792.1 32.3 %collective-permute-start.89 = (bf16[4,144,768]{2,1,0:T(8,128)(2,1)S(1)}, bf16[4,144,768]{2,1,0:T(8,128)(2,1)S(1)}, u32[]{:S(2)}, u32[]{:S(2)}) collective-permute-start(bf16[4,144,768]{2,1,0:T(8,128)(2,1)S(1)} %pad_maximum_fusion.14), channel_id=1, source_target_pairs={{0,16},{1,17},{2,18},{3,19},{4,20},{5,21},{6,22},{7,23},{8,24},{9,... | collective-permute-start | bytes 2654216 | tf_op jit(solution)/shard_map/ppermute | solution.py:1056
  828.5 91.9 %collective-permute-start.118 = (bf16[144,768]{1,0:T(8,128)(2,1)}, bf16[144,768]{1,0:T(8,128)(2,1)}, u32[]{:S(2)}, u32[]{:S(2)}) collective-permute-start(bf16[144,768]{1,0:T(8,128)(2,1)} %get-tuple-element.291), channel_id=1, source_target_pairs={{0,6},{1,7},{2,4},{3,5},{4,2},{5,3},{6,0},{7,1},{8,14},{9,15},{10,... | collective-permute-start | bytes 663560 | tf_op jit(solution)/shard_map/ppermute | solution.py:1056
  829.8 90.6 %collective-permute-start.117 = (bf16[144,768]{1,0:T(8,128)(2,1)}, bf16[144,768]{1,0:T(8,128)(2,1)}, u32[]{:S(2)}, u32[]{:S(2)}) collective-permute-start(bf16[144,768]{1,0:T(8,128)(2,1)} %get-tuple-element.292), channel_id=1, source_target_pairs={{0,4},{1,5},{2,6},{3,7},{4,0},{5,1},{6,2},{7,3},{8,12},{9,13},{10,... | collective-permute-start | bytes 663560 | tf_op jit(solution)/shard_map/ppermute | solution.py:1056
  829.9 90.5 %collective-permute-start.116 = (bf16[144,768]{1,0:T(8,128)(2,1)}, bf16[144,768]{1,0:T(8,128)(2,1)}, u32[]{:S(2)}, u32[]{:S(2)}) collective-permute-start(bf16[144,768]{1,0:T(8,128)(2,1)} %get-tuple-element.293), channel_id=1, source_target_pairs={{0,2},{1,3},{2,0},{3,1},{4,6},{5,7},{6,4},{7,5},{8,10},{9,11},{10,... | collective-permute-start | bytes 663560 | tf_op jit(solution)/shard_map/ppermute | solution.py:1056
  837.4 29.7 %collective-permute-start.92 = (bf16[2,144,768]{2,1,0:T(8,128)(2,1)}, bf16[2,144,768]{2,1,0:T(8,128)(2,1)}, u32[]{:S(2)}, u32[]{:S(2)}) collective-permute-start(bf16[2,144,768]{2,1,0:T(8,128)(2,1)} %get-tuple-element.289), channel_id=1, source_target_pairs={{0,8},{1,9},{2,10},{3,11},{4,12},{5,13},{6,14},{7,15},{8,0},{9,1},... | collective-permute-start | bytes 1327112 | tf_op jit(solution)/shard_map/ppermute | solution.py:1056
  838.7 30.5 %collective-permute-start.91 = (bf16[2,144,768]{2,1,0:T(8,128)(2,1)}, bf16[2,144,768]{2,1,0:T(8,128)(2,1)}, u32[]{:S(2)}, u32[]{:S(2)}) collective-permute-start(bf16[2,144,768]{2,1,0:T(8,128)(2,1)} %get-tuple-element.290), channel_id=1, source_target_pairs={{0,16},{1,17},{2,18},{3,19},{4,20},{5,21},{6,22},{7,23},{8,24},{9,... | collective-permute-start | bytes 1327112 | tf_op jit(solution)/shard_map/ppermute | solution.py:1056
  932.4 29.7 %collective-permute-start.101 = (f32[552,128]{1,0:T(8,128)S(1)}, f32[552,128]{1,0:T(8,128)}, u32[]{:S(2)}, u32[]{:S(2)}) collective-permute-start(f32[552,128]{1,0:T(8,128)S(1)} %fusion.101), channel_id=1, source_target_pairs={{0,4},{1,5},{2,6},{3,7},{4,0},{5,1},{6,2},{7,3},{8,12},{9,13},{10,... | collective-permute-start | bytes 847880 | tf_op jit(solution)/shard_map/ppermute | solution.py:1056
  (205 other events, 3879.2 us)

commit v2 on v1

--- a/solution.py
+++ b/solution.py
@@ -27,6 +27,12 @@
 
 def dot(left, right, dims):
     return lax.dot_general(left, right, dims, preferred_element_type=f32)
+
+
+def dot_fine(left, right, dims):
+    return lax.dot_general(
+        left, right, dims, precision=lax.Precision.HIGHEST, preferred_element_type=f32
+    )
 
 
 def split_low(table):
@@ -282,13 +288,14 @@
     return pl.BlockSpec(shape, lambda *index: (0,) * len(shape), pipeline_mode=pl.Buffered(1))
 
 
-def mixer_forward(split, state, norm_pack, chan_pack, w_in, khat, w_out):
+def mixer_forward(after, split, state, norm_pack, chan_pack, w_in, khat, w_out):
     length, width = state.shape
     steps = width // CB
     parts = length // BLK + 1
     forward = jnp.asarray(split_low(FORWARD))
     inverse = jnp.asarray(split_low(INVERSE))
-    return pl.pallas_call(
+    return call_after(
+        after,
         mixer_forward_kernel,
         grid=(steps,),
         in_specs=[
@@ -334,6 +341,18 @@
 PARTS = 2
 
 
+def call_after(after, kernel, in_specs, **options):
+    count = len(after)
+
+    def run(*refs):
+        kernel(*refs[count:])
+
+    call = pl.pallas_call(
+        run, in_specs=[pl.BlockSpec(memory_space=pl.ANY)] * count + in_specs, **options
+    )
+    return functools.partial(call, *after)
+
+
 def cost(flops, moved):
     return pl.CostEstimate(flops=int(flops), bytes_accessed=int(moved), transcendentals=0)
 
@@ -342,15 +361,60 @@
     return block.reshape(-1, block.shape[-1])
 
 
-def gated_forward_kernel(
-    first, second_ref, gate_w_ref, value_w_ref, down_ref, middle_ref, norm_ref, gate_ref, value_ref, out_ref
-):
+def load_weights(masks, taken, me_ref, refs, up_ref, down_ref, sems):
+    moves = []
+    size, piece = down_ref.shape[0] // len(taken), down_ref.shape[1]
+    for array, own in zip(refs, masks):
+        for slot, mask in enumerate(own):
+            device = slot if mask is None else me_ref[0] ^ mask
+            for part, source in enumerate(taken):
+                start = 3 * piece * source
+                targets = [
+                    up_ref.at[2 * (size * part + device)],
+                    up_ref.at[2 * (size * part + device) + 1],
+                    down_ref.at[size * part + device],
+                ]
+                for place, target in enumerate(targets):
+                    rows = slice(start + place * piece, start + (place + 1) * piece)
+                    moves.append(
+                        pltpu.make_async_copy(array.at[slot, rows, :], target, sems.at[len(moves)])
+                    )
+    for move in moves:
+        move.start()
+    return moves
+
+
+def weight_blocks(up_ref, down_ref, parts, inner, count, step):
+    size = down_ref.shape[0] // parts
+    part, block = step // inner, step % inner
+    base = block * count
+    return (
+        flat(up_ref[pl.ds(2 * size * part + base, count)]),
+        flat(up_ref[pl.ds(2 * size * part + size + base, count)]),
+        flat(down_ref[pl.ds(size * part + base, count)]),
+    )
+
+
+def gated_forward_kernel(first, masks, taken, block, me_ref, second_ref, middle_ref, norm_ref, *refs):
     step = pl.program_id(0)
     length = second_ref.shape[0]
     rows = 256
-    gate_w = flat(gate_w_ref[...])
-    value_w = flat(value_w_ref[...])
-    down_w = flat(down_ref[...])
+    if masks:
+        gate_ref, value_ref, out_ref, up_ref, down_ref, sems = refs[len(masks) :]
+
+        @pl.when(step == 0)
+        def _():
+            moves = load_weights(masks, taken, me_ref, refs[: len(masks)], up_ref, down_ref, sems)
+            for move in moves:
+                move.wait()
+
+    else:
+        up_ref, down_ref, gate_ref, value_ref, out_ref = refs
+    count = block // down_ref.shape[1]
+    parts = len(taken)
+    gate_w, value_w, down_w = weight_blocks(
+        up_ref, down_ref, parts, pl.num_programs(0) // parts, count, step
+    )
 
     @pl.when(step == 0)
     def _():
@@ -375,23 +439,38 @@
     return [grouped[:, part] for part in range(PARTS)]
 
 
-def gated_forward(second, up, down, before, norm_pack, first, block=768):
+def weight_operands(weights, parts):
+    anywhere = pl.BlockSpec(memory_space=pl.ANY)
+    if isinstance(weights, dict):
+        arrays = [piece for piece, _ in weights["pieces"]]
+        masks = [own for _, own in weights["pieces"]]
+        size = sum(len(own) for own in masks)
+        width = arrays[0].shape[2]
+        piece = weights["rows"]
+        scratch = [
+            pltpu.VMEM((2 * size * parts, piece, width), bf16),
+            pltpu.VMEM((size * parts, piece, width), bf16),
+            pltpu.SemaphoreType.DMA((3 * size * parts,)),
+        ]
+        return arrays, [anywhere] * len(arrays), masks, scratch, piece
+    return list(weights), [fixed_block(part.shape) for part in weights], None, [], weights[1].shape[1]
+
+
+def gated_forward(after, me, second, weights, before, norm_pack, hidden, first, taken=(0,), block=768):
     length, width = second.shape
-    piece = down.shape[1]
-    hidden = down.shape[0] * piece
     steps = hidden // block
-    tile = (block // piece, piece, width)
-    return pl.pallas_call(
-        functools.partial(gated_forward_kernel, first),
+    arrays, specs, masks, scratch, _ = weight_operands(weights, len(taken))
+    return call_after(
+        after,
+        functools.partial(gated_forward_kernel, first, masks, taken, block),
         grid=(steps,),
         in_specs=[
+            pl.BlockSpec(memory_space=pltpu.SMEM),
             fixed_block((length, width)),
-            pl.BlockSpec(tile, lambda i: (i, 0, 0)),
-            pl.BlockSpec(tile, lambda i: (i + steps, 0, 0)),
-            pl.BlockSpec(tile, lambda i: (i, 0, 0)),
             fixed_block((length, width)),
             fixed_block(norm_pack.shape),
-        ],
+        ]
+        + specs,
         out_specs=[
             pl.BlockSpec((length, block), lambda i: (0, i)),
             pl.BlockSpec((length, block), lambda i: (0, i)),
@@ -402,10 +481,11 @@
             jax.ShapeDtypeStruct((length, hidden), bf16),
             jax.ShapeDtypeStruct((length, width), f32),
         ],
+        scratch_shapes=scratch,
         compiler_params=pltpu.CompilerParams(vmem_limit_bytes=VMEM),
         cost_estimate=cost(6 * length * width * hidden, 20 * 2**20),
         name="gated_forward",
-    )(second, up, up, down, before, norm_pack)
+    )(me, second, before, norm_pack, *arrays)
 
 
 def norm_backward(values, grad_out, gain):
@@ -419,7 +499,10 @@
 def gated_backward_kernel(
     first,
     last,
-    slots,
+    masks,
+    own_order,
+    taken,
+    block,
     me_ref,
     grad_ref,
     before_ref,
@@ -428,51 +511,59 @@
     norm_ref,
     gate_ref,
     value_ref,
-    gate_w_ref,
-    value_w_ref,
-    down_ref,
-    one_ref,
-    two_ref,
-    out_ref,
-    small_ref,
-    glow_ref,
-    hidden_ref,
-    dgate_ref,
-    dvalue_ref,
-    stage_ref,
-    sems,
+    *refs,
 ):
     step = pl.program_id(0)
     steps = pl.num_programs(0)
     length, width = grad_ref.shape
     rows = 256
-    count, piece, _ = gate_w_ref.shape
+    slots = bool(masks)
+    if slots:
+        pieces, refs = refs[: len(masks)], refs[len(masks) :]
+    else:
+        up_ref, down_ref = refs[:2]
+        refs = refs[2:]
+    one_ref, two_ref, out_ref, small_ref, glow_ref, hidden_ref, dgate_ref, dvalue_ref, stage_ref, sems = refs[:10]
+    if slots:
+        up_ref, down_ref, load_sems = refs[10:]
+    piece = down_ref.shape[1]
+    count = block // piece
     side = step % 2
-    gate_w = flat(gate_w_ref[...])
-    value_w = flat(value_w_ref[...])
-    down_w = flat(down_ref[...])
 
     @pl.when(step == 0)
     def _():
+        moves = []
+        if slots:
+            moves = load_weights(masks, taken, me_ref, pieces, up_ref, down_ref, load_sems)
         glow_ref[...] = grad_ref[...].astype(bf16)
         if first:
             out_ref[...] = jnp.zeros_like(out_ref)
         else:
             out_ref[...] = before_ref[...]
+        for move in moves:
+            move.wait()
+
+    parts = len(taken)
+    inner = steps // parts
+    gate_w, value_w, down_w = weight_blocks(up_ref, down_ref, parts, inner, count, step)
 
     def copies(at_step, kind, item):
         source = stage_ref.at[at_step % 2, kind, pl.ds(item * piece, piece), :]
-        half = at_step * count + item
+        half = at_step % inner * count + item
+        start = at_step // inner * 3 * piece
         if not slots:
             if kind == 2:
                 return source, [(None, two_ref.at[half])]
-            return source, [(None, one_ref.at[half + kind * steps * count])]
+            return source, [(None, one_ref.at[half + kind * inner * count])]
         if kind == 2:
-            mask = half ^ me_ref[0]
-            rows_at = pl.ds(2 * piece, piece)
+            device = half
+            rows_at = pl.ds(start + 2 * piece, piece)
         else:
-            mask = ((half >> 1) + kind * (steps * count >> 1)) ^ me_ref[0]
-            rows_at = pl.ds((half & 1) * piece, piece)
+            device = (half >> 1) + kind * (inner * count >> 1)
+            rows_at = pl.ds(start + (half & 1) * piece, piece)
+        if not own_order:
+            return source, [(None, one_ref.at[device, rows_at, :])]
+        mask = device ^ me_ref[0]
         place = mask >> 1
         core = mask & 1
         return source, [
@@ -567,28 +658,36 @@
         drain(step)
 
 
-def gated_backward(
-    part, me, grad, before, second, middle, norm_pack, gate, value, up, down, size, block=768
+def gated_backward(after,
+    me, grad, before, second, middle, norm_pack, gate, value, weights, first, last, own_order, taken=(0,), block=768
 ):
     length, width = second.shape
-    piece = down.shape[1]
-    hidden = down.shape[0] * piece
-    inner = hidden // block
+    parts = len(taken)
+    inner = gate.shape[1] // block
+    start = 0
+    if isinstance(weights, dict):
+        start = taken[0] * inner // PARTS
+        inner = parts * inner // PARTS
+    hidden = inner * block
+    arrays, specs, masks, scratch, piece = weight_operands(weights, parts)
     count = block // piece
-    tile = (count, piece, width)
-    slots = size == 32
-    column = pl.BlockSpec((length, block), lambda i: (0, i))
+    column = pl.BlockSpec((length, block), lambda i: (0, i + start))
     anywhere = pl.BlockSpec(memory_space=pl.ANY)
-    if slots:
-        places = [jax.ShapeDtypeStruct((size // 2, 3 * piece, width), bf16)] * 2
+    if masks:
+        size = sum(len(own) for own in masks)
+        places = [jax.ShapeDtypeStruct((size // 2, 3 * piece * parts, width), bf16)] * 2
+        if not own_order:
+            places = [
+                jax.ShapeDtypeStruct((size, 3 * piece * parts, width), bf16),
+                jax.ShapeDtypeStruct((16, width), bf16),
+            ]
     else:
-        places = [
-            jax.ShapeDtypeStruct((up.shape[0], piece, width), bf16),
-            jax.ShapeDtypeStruct((down.shape[0], piece, width), bf16),
-        ]
-    last = part == PARTS - 1
-    return pl.pallas_call(
-        functools.partial(gated_backward_kernel, part == 0, last, slots),
+        places = [jax.ShapeDtypeStruct(array.shape, bf16) for array in arrays]
+    return call_after(
+        after,
+        functools.partial(
+            gated_backward_kernel, first, last, masks, own_order, taken, block
+        ),
         grid=(inner,),
         in_specs=[
             pl.BlockSpec(memory_space=pltpu.SMEM),
@@ -599,10 +698,8 @@
             fixed_block(norm_pack.shape),
             column,
             column,
-            pl.BlockSpec(tile, lambda i: (i, 0, 0)),
-            pl.BlockSpec(tile, lambda i: (i + inner, 0, 0)),
-            pl.BlockSpec(tile, lambda i: (i, 0, 0)),
-        ],
+        ]
+        + specs,
         out_specs=[anywhere, anywhere, whole_block((length, width)), whole_block((8, width))],
         out_shape=places
         + [
@@ -616,11 +713,12 @@
             pltpu.VMEM((length, block), bf16),
             pltpu.VMEM((2, 3, block, width), bf16),
             pltpu.SemaphoreType.DMA((2, 3, count)),
-        ],
+        ]
+        + scratch,
         compiler_params=pltpu.CompilerParams(vmem_limit_bytes=VMEM),
         cost_estimate=cost(12 * length * width * hidden, 20 * 2**20),
         name="gated_backward",
-    )(me, grad, before, second, middle, norm_pack, gate, value, up, up, down)
+    )(me, grad, before, second, middle, norm_pack, gate, value, *arrays)
 
 
 def mixer_backward_kernel(
@@ -629,9 +727,7 @@
     split_ref,
     grad_ref,
     before_ref,
-    state_ref,
     normed_ref,
-    norm_ref,
     chan_ref,
     biased_ref,
     conv_ref,
@@ -641,13 +737,20 @@
     inv_ref,
     wout_ref,
     win_ref,
+    kernel_ref,
+    inner_t_ref,
+    slope_ref,
+    features_t_ref,
+    freq_out_ref,
+    inner_before_ref,
     win_g_ref,
     wout_g_ref,
+    chan_g_ref,
+    inner_g_ref,
+    freq_g_ref,
+    out_ref,
+    mlow_ref,
     kern_g_ref,
-    chan_g_ref,
-    out_ref,
-    small_ref,
-    mlow_ref,
     key_ref,
     val_ref,
     prod_ref,
@@ -662,7 +765,7 @@
     gram_ref,
 ):
     step = pl.program_id(0)
-    length, width = state_ref.shape
+    length, width = grad_ref.shape
     split = split_ref[0]
     boundary = split // BLK
     parts = length // BLK + 1
@@ -831,12 +934,38 @@
         got = loop_rows(length, rows, back, (zero, zero, zero, zero))
         for index in range(4):
             sums[3 * index + stream] = got[index]
-    chan_g_ref[...] = jnp.concatenate(
+    decay = chan_ref[15:16, :]
+    level = jnp.sqrt(2.0 * decay)
+    lead = 0.5 / decay
+
+    def profile(row, total):
+        here = pl.ds(row, rows)
+        position = row_mask(row, rows, CB).astype(f32)
+        change = kern_g_ref[here, :]
+        kern_g_ref[here, :] = change * (jnp.exp(-position * decay) * level)
+        return total + fold(change * kernel_ref[here, :] * (lead - position))
+
+    decay_sum = loop_rows(length, rows, profile, zero)
+    chan_g_ref[0:16, :] = jnp.concatenate(
         [jnp.sum(part, axis=0, keepdims=True) for part in sums]
         + [factor * jnp.sum(part, axis=0, keepdims=True) for part in cond_sums]
-        + [jnp.zeros((1, CB), f32)],
+        + [jnp.sum(decay_sum, axis=0, keepdims=True)],
         axis=0,
     )
+    chan_g_ref[16:, :] = dot_fine(inner_t_ref[...], kern_g_ref[...], NN)
+    inner_g = dot_fine(kern_g_ref[...], freq_out_ref[...], NT)
+
+    @pl.when(step == 0)
+    def _():
+        if first:
+            inner_g_ref[...] = inner_g
+        else:
+            inner_g_ref[...] = inner_before_ref[...] + inner_g
+
+    @pl.when(step > 0)
+    def _():
+        inner_g_ref[...] += inner_g
+
     wout_g_ref[...] = dot(mixed_ref[...], mlow_ref[...], TN).astype(bf16)
     for stream in range(3):
         win_g_ref[stream] = dot(low_ref[stream], normed_ref[...], TN).astype(bf16)
@@ -854,37 +983,28 @@
         out_ref[...] += update
 
     if not last:
-        small_ref[...] = jnp.zeros_like(small_ref)
+        freq_g_ref[...] = jnp.zeros_like(freq_g_ref)
         return
 
     @pl.when(step == pl.num_programs(0) - 1)
     def _():
-        def finish(row, carry):
-            here = pl.ds(row, 32)
-            grad_out = out_ref[here, :]
-            change, gain_rows = norm_backward(state_ref[here, :], grad_out, norm_ref[0:1, :])
-            out_ref[here, :] = grad_ref[here, :] + change
-            return carry[0] + fold(gain_rows), carry[1] + fold(grad_out)
-
-        wide_zero = jnp.zeros((8, width), f32)
-        got = loop_rows(length, 32, finish, (wide_zero, wide_zero))
-        small_ref[...] = jnp.concatenate(
-            [jnp.sum(part, axis=0, keepdims=True) for part in got] + [jnp.zeros((6, width), f32)],
-            axis=0,
-        )
-
-
-def mixer_backward(start, steps, split, grad, before, state, normed, norm_pack, chan_pack, biased, conv, scale, khat, w_out, w_in):
-    length, width = state.shape
+        phase_g = inner_g_ref[...] * slope_ref[...]
+        freq_g_ref[0 : phase_g.shape[1], :] = dot_fine(features_t_ref[...], phase_g, NN)
+        freq_g_ref[phase_g.shape[1] :, :] = fold(phase_g)
+def mixer_backward(after, start, steps, split, grad, before, normed, chan_pack, biased, conv, scale, khat, w_out, w_in, filtered, freq_out, inner_before):
+    length, width = grad.shape
     last = (start + steps) * CB == width
     parts = length // BLK + 1
     forward = jnp.asarray(FORWARD, bf16)
     inverse = jnp.asarray(INVERSE, bf16)
+    kernel, inner_t, slope, features_t = filtered
+    hidden = freq_out.shape[0]
     full = fixed_block((length, width))
     tall = pltpu.VMEM((length, CB), f32)
     tall_pad = pltpu.VMEM((length + PAD, CB), f32)
     spectrum = pltpu.VMEM((parts, BINS, CB), f32)
-    return pl.pallas_call(
+    return call_after(
+        after,
         functools.partial(mixer_backward_kernel, start == 0, last),
         grid=(steps,),
         in_specs=[
@@ -892,8 +1012,6 @@
             full,
             fixed_block(before.shape),
             full,
-            full,
-            fixed_block(norm_pack.shape),
             pl.BlockSpec((16, CB), lambda i: (0, i + start)),
             pl.BlockSpec((3, length + PAD, CB), lambda i: (0, 0, i + start)),
             pl.BlockSpec((length, CB), lambda i: (0, i + start)),
@@ -903,25 +1021,32 @@
             fixed_block(inverse.shape),
             pl.BlockSpec((CB, width), lambda i: (i + start, 0)),
             pl.BlockSpec((3, CB, width), lambda i: (0, i + start, 0)),
+            pl.BlockSpec((length, CB), lambda i: (0, i + start)),
+            fixed_block(inner_t.shape),
+            fixed_block(slope.shape),
+            fixed_block(features_t.shape),
+            pl.BlockSpec((freq_out.shape[0], CB), lambda i: (0, i + start)),
+            fixed_block(inner_before.shape),
         ],
         out_specs=[
             pl.BlockSpec((3, CB, width), lambda i: (0, i, 0)),
             pl.BlockSpec((CB, width), lambda i: (i, 0)),
-            pl.BlockSpec((length, CB), lambda i: (0, i)),
-            pl.BlockSpec((16, CB), lambda i: (0, i)),
+            pl.BlockSpec((16 + hidden, CB), lambda i: (0, i)),
+            whole_block((length, hidden)),
+            whole_block((hidden + 8, hidden)),
             whole_block((length, width)),
-            whole_block((8, width)),
         ],
         out_shape=[
             jax.ShapeDtypeStruct((3, steps * CB, width), bf16),
             jax.ShapeDtypeStruct((steps * CB, width), bf16),
-            jax.ShapeDtypeStruct((length, steps * CB), f32),
-            jax.ShapeDtypeStruct((16, steps * CB), f32),
+            jax.ShapeDtypeStruct((16 + hidden, steps * CB), f32),
+            jax.ShapeDtypeStruct((length, hidden), f32),
+            jax.ShapeDtypeStruct((hidden + 8, hidden), f32),
             jax.ShapeDtypeStruct((length, width), f32),
-            jax.ShapeDtypeStruct((8, width), f32),
         ],
         scratch_shapes=[
             pltpu.VMEM((length, width), bf16),
+            tall,
             tall,
             tall_pad,
             tall,
@@ -942,9 +1067,7 @@
         split,
         grad,
         before,
-        state,
         normed,
-        norm_pack,
         chan_pack,
         biased,
         conv,
@@ -954,7 +1077,53 @@
         inverse,
         w_out,
         w_in.reshape(3, width, width),
+        kernel,
+        inner_t,
+        slope,
+        features_t,
+        freq_out,
+        inner_before,
     )
+
+
+def norm_finish_kernel(acc_ref, state_ref, grad_ref, norm_ref, out_ref, small_ref):
+    length, width = state_ref.shape
+
+    def finish(row, carry):
+        here = pl.ds(row, 32)
+        grad_out = acc_ref[here, :]
+        change, gain_rows = norm_backward(state_ref[here, :], grad_out, norm_ref[0:1, :])
+        out_ref[here, :] = grad_ref[here, :] + change
+        return carry[0] + fold(gain_rows), carry[1] + fold(grad_out)
+
+    @pl.when(pl.program_id(0) == 0)
+    def _():
+        small_ref[...] = jnp.zeros_like(small_ref)
+
+    zero = jnp.zeros((8, width), f32)
+    got = loop_rows(length, 32, finish, (zero, zero))
+    small_ref[...] += jnp.concatenate(
+        [jnp.sum(part, axis=0, keepdims=True) for part in got] + [jnp.zeros((6, width), f32)], axis=0
+    )
+
+
+def norm_finish(after, acc, state, grad, norm_pack, block=256):
+    length, width = state.shape
+    tile = pl.BlockSpec((block, width), lambda i: (i, 0))
+    return call_after(
+        after,
+        norm_finish_kernel,
+        grid=(length // block,),
+        in_specs=[tile, tile, tile, whole_block(norm_pack.shape)],
+        out_specs=[tile, whole_block((8, width))],
+        out_shape=[
+            jax.ShapeDtypeStruct((length, width), f32),
+            jax.ShapeDtypeStruct((8, width), f32),
+        ],
+        compiler_params=pltpu.CompilerParams(vmem_limit_bytes=VMEM),
+        cost_estimate=cost(3e9, 16 * 2**20),
+        name="norm_finish",
+    )(acc, state, grad, norm_pack)
 
 
 def filter_features(length, count):
@@ -969,21 +1138,15 @@
     return lax.dot_general(left, right, dims, precision=lax.Precision.HIGHEST)
 
 
-def filter_kernel_body(inner_ref, out_ref, decay_ref, fwd_ref, kernel_ref, khat_ref):
+def filter_kernel_body(inner_ref, out_ref, chan_ref, fwd_ref, kernel_ref, khat_ref):
     length = inner_ref.shape[0]
-    decay = decay_ref[0:1, :]
+    decay = chan_ref[15:16, :]
     level = jnp.sqrt(2.0 * decay)
     sign = jnp.where(lax.broadcasted_iota(jnp.int32, (BINS, CB), 0) % 2 == 0, 1.0, -1.0)
     before = None
     for block in range(length // BLK):
         here = slice(block * BLK, (block + 1) * BLK)
-        profile = lax.dot_general(
-            inner_ref[here, :],
-            out_ref[...],
-            NN,
-            precision=lax.Precision.HIGHEST,
-            preferred_element_type=f32,
-        )
+        profile = dot_fine(inner_ref[here, :], out_ref[...], NN)
         position = row_mask(block * BLK, BLK, CB).astype(f32)
         kernel = profile * (jnp.exp(-position * decay) * level)
         kernel_ref[here, :] = kernel
@@ -992,13 +1155,14 @@
         before = spectrum
 
 
-def filter_forward(length, decay, freq_in, freq_bias, freq_out):
-    features = jnp.asarray(filter_features(length, freq_in.shape[0]))
+def filter_forward(length, chan_pack, freq_in, freq_bias, freq_out):
+    table = filter_features(length, freq_in.shape[0])
+    features = jnp.asarray(table)
     phase = highest(features, freq_in, NN) + freq_bias
     inner = jnp.sin(phase)
-    width = decay.shape[0]
+    width = freq_out.shape[1]
     hidden = inner.shape[1]
-    table = jnp.asarray(split_low(FORWARD))
+    forward = jnp.asarray(split_low(FORWARD))
     blocks = length // BLK
     kernel, khat = pl.pallas_call(
         filter_kernel_body,
@@ -1006,8 +1170,8 @@
         in_specs=[
             fixed_block((length, hidden)),
             pl.BlockSpec((hidden, CB), lambda i: (0, i)),
-            pl.BlockSpec((8, CB), lambda i: (0, i)),
-            fixed_block(table.shape),
+            pl.BlockSpec((16, CB), lambda i: (0, i)),
+            fixed_block(forward.shape),
         ],
         out_specs=[
             pl.BlockSpec((length, CB), lambda i: (0, i)),
@@ -1020,21 +1184,8 @@
         compiler_params=pltpu.CompilerParams(vmem_limit_bytes=VMEM),
         cost_estimate=cost(6e9, 10 * 2**20),
         name="filter_forward",
-    )(inner, freq_out, jnp.broadcast_to(decay[None], (8, width)), table)
-    positions = jnp.arange(length, dtype=f32)[:, None]
-    window = jnp.exp(-positions * decay[None, :]) * jnp.sqrt(2.0 * decay)[None, :]
-    return khat, (features, phase, inner, window, kernel, positions)
-
-
-def filter_backward(grad_kernel, kept, decay, freq_out):
-    features, phase, inner, window, kernel, positions = kept
-    grad_profile = grad_kernel * window
-    grad_freq_out = highest(inner, grad_profile, TN)
-    grad_phase = highest(grad_profile, freq_out, NT) * jnp.cos(phase)
-    grad_freq_in = highest(features, grad_phase, TN)
-    grad_freq_bias = jnp.sum(grad_phase, axis=0)
-    grad_decay = jnp.sum(grad_kernel * kernel * (0.5 / decay[None, :] - positions), axis=0)
-    return grad_decay, grad_freq_in, grad_freq_bias, grad_freq_out
+    )(inner, freq_out, chan_pack, forward)
+    return khat, (kernel, inner.T, jnp.cos(phase), jnp.asarray(table.T.copy()))
 
 
 def cube_orders(size):
@@ -1105,34 +1256,49 @@
     return jnp.concatenate([one, two], axis=0)
 
 
-def tie(value, *others):
-    return lax.optimization_barrier((value,) + others)[0]
-
-
-def gather_pieces(block, start_after=(), spread_after=()):
+def hold(value, *others):
+    for other in others:
+        value = value + (other[(0,) * other.ndim] * 0).astype(value.dtype)
+    return value
+
+
+def hold_place(value, *others):
+    if not others:
+        return value
+    anywhere = pl.BlockSpec(memory_space=pl.ANY)
+
+    def nothing(*refs):
+        pass
+
+    return pl.pallas_call(
+        nothing,
+        in_specs=[anywhere] * (1 + len(others)),
+        out_specs=anywhere,
+        out_shape=jax.ShapeDtypeStruct(value.shape, value.dtype),
+        input_output_aliases={0: 0},
+        cost_estimate=cost(0, 0),
+        name="hold_place",
+    )(value, *others)
+
+
+def gather_steps(block, after, clock, done):
     size = 32
-    if start_after:
-        block = tie(block, *start_after)
-    line = jnp.stack([block] + [swap(block, bit, size) for bit in (2, 4, 6)])
-    if spread_after:
-        line = tie(line, *spread_after)
-    along_x = swap(line, 8, size)
-    along_y = swap(line, 16, size)
-    corner_one = swap(along_x[:2], 16, size)
-    corner_two = swap(along_y[2:], 8, size)
-    places = (0, 2, 4, 6)
-    held = [
-        (line, places),
-        (along_x, tuple(8 + place for place in places)),
-        (along_y, tuple(16 + place for place in places)),
-        (corner_one, (24, 26)),
-        (corner_two, (28, 30)),
-    ]
+    block = hold(block, *after)
+    came = [swap(block, bit, size) for bit in (2, 4, 6)]
+    yield [block]
+    line = hold(jnp.stack([block] + came), *clock)
+    others = [swap(line, bit, size) for bit in (8, 16, 24)]
+    own = swap(line, 1, size)
+    yield [line]
+    others = [hold_place(other, *clock) for other in others]
     pieces = []
-    for piece, masks in held:
+    for bit, piece in zip((0, 8, 16, 24), [line] + others):
+        masks = tuple(bit + place for place in (0, 2, 4, 6))
         pieces.append((piece, masks))
-        pieces.append((swap(piece, 1, size), tuple(mask + 1 for mask in masks)))
-    return pieces, (line,), (along_x, along_y)
+        other = swap(piece, 1, size) if bit else own
+        pieces.append((other, tuple(mask + 1 for mask in masks)))
+    yield others
+    done(pieces)
 
 
 def place_kernel(masks, cuts, me_ref, *refs):
@@ -1187,7 +1353,7 @@
     )(me, *arrays)
 
 
-def scatter_steps(keep, send, done):
+def scatter_steps(keep, send, clock, done):
     size = 32
     shape = (4, 4) + keep.shape[1:]
     keep = keep.reshape(shape)
@@ -1197,53 +1363,30 @@
     def both(group):
         return keep[group].astype(f32) + got[group].astype(f32)
 
-    corner = both(3).astype(bf16)
-    from_y = swap(corner[:2], 16, size)
-    from_x = swap(corner[2:], 8, size)
-    yield [corner]
-    to_x = both(1)
-    to_x = jnp.concatenate([to_x[:2] + from_y.astype(f32), to_x[2:]], axis=0).astype(bf16)
-    to_y = both(2)
-    to_y = jnp.concatenate([to_y[:2], to_y[2:] + from_x.astype(f32)], axis=0).astype(bf16)
-    got_x, got_y = swap(to_x, 8, size), swap(to_y, 16, size)
-    yield [to_x, to_y]
-    line = both(0) + got_x.astype(f32) + got_y.astype(f32)
+    out = [hold(both(group), *clock).astype(bf16) for group in (3, 1, 2)]
+    came = [swap(piece, bit, size) for piece, bit in zip(out, (24, 8, 16))]
+    yield out
+    line = hold(sum_terms([both(0)] + [piece.astype(f32) for piece in came]), *clock)
     low = [line[place].astype(bf16) for place in (1, 2, 3)]
     came = [swap(piece, 2 * place + 2, size) for place, piece in enumerate(low)]
     yield low
-    done(sum_terms([line[0]] + [piece.astype(f32) for piece in came]))
-
-
-def sum_steps(values, size, done):
-    for place in range(size.bit_length() - 1):
-        came = swap(values, 1 << place, size)
-        yield [values]
-        values = values + came
-    done(values)
-
-
-class Flight:
-    def __init__(self):
-        self.running = []
-
-    def add(self, steps):
-        self.running.append(steps)
-
-    def advance(self):
-        sent = []
-        still = []
-        for steps in self.running:
-            try:
-                sent.extend(next(steps))
-                still.append(steps)
-            except StopIteration:
-                pass
-        self.running = still
-        return sent
-
-    def finish(self):
-        while self.running:
-            self.advance()
+    done(hold(sum_terms([line[0]] + [piece.astype(f32) for piece in came]), *clock))
+
+
+def sum_steps(values, size, me, done, after=()):
+    halved = values.reshape((2, -1) + values.shape[1:])
+    core = me % 2
+    send = jnp.take(halved, 1 - core, axis=0, mode="clip")
+    part = jnp.take(halved, core, axis=0, mode="clip") + swap(send, 1, size)
+    yield [send]
+    part = hold(part, *after)
+    for place in reversed(range(1, size.bit_length() - 1)):
+        came = swap(part, 1 << place, size)
+        yield [part]
+        part = part + came
+    other = swap(part, 1, size)
+    yield [part]
+    done(jnp.concatenate([jnp.where(core == 0, part, other), jnp.where(core == 0, other, part)], axis=0))
 
 
 def body(
@@ -1291,7 +1434,7 @@
                 in_bias[layer].reshape(3, width),
                 short_taps[layer].reshape(9, width),
                 cond_taps[layer],
-                jnp.zeros((1, width), f32),
+                decay_rate[layer][None],
             ]
         )
         packs.append((norm_pack, chan_pack))
@@ -1300,71 +1443,152 @@
     up_rows = up_weight.shape[2]
     down_rows = down_weight.shape[1]
     special = size == 32
+    clock = []
     mixer_w = [None] * layers
-    gated_w = [None] * layers
-    lines = {}
-    after_start, after_spread = (), ()
+    gated_w = [[None] * PARTS for _ in range(layers)]
+    hidden = size * down_rows // PARTS
+
+    def mixer_block(layer):
+        return jnp.concatenate([in_weight[layer].T, out_weight[layer]], axis=0)
+
+    def mixer_weights(layer, rows):
+        mixer_w[layer] = (
+            rows[:, :in_rows].reshape(3 * width, width),
+            rows[:, in_rows:].reshape(width, width),
+        )
+
+    def gather_mixer(layer, after):
+        def done(pieces):
+            (rows,) = place_pieces(pieces, (in_rows + out_rows,), mine)
+            mixer_weights(layer, rows)
+
+        return gather_steps(mixer_block(layer), after, clock, done)
+
+    def gated_weights(layer, pieces):
+        gated_w[layer] = {"pieces": pieces, "rows": down_rows // PARTS}
+
+    def gather_gated(layer, after):
+        return gather_steps(all_parts(layer), after, clock, functools.partial(gated_weights, layer))
+
+    def whole_gather(block, *after):
+        return lax.all_gather(hold(block, *after), AXES, axis=0)
+
+    def all_parts(layer):
+        halved = up_weight[layer].T.reshape(2, PARTS, -1, width)
+        own = down_weight[layer].reshape(PARTS, -1, width)
+        rows = []
+        for part in range(PARTS):
+            rows += [halved[0, part], halved[1, part], own[part]]
+        return jnp.concatenate(rows, axis=0)
+
+    def go(*names):
+        sent = []
+        for name in names:
+            sent.extend(next(steps[name], ()))
+        return sent
+
+    filters = [None] * layers
+
+    def make_filter(layer, *after):
+        filters[layer] = filter_forward(
+            length,
+            packs[layer][1],
+            hold(freq_in[layer], *after),
+            freq_bias[layer],
+            freq_out[layer],
+        )
+
     for layer in range(layers):
-        mixer_block = jnp.concatenate([in_weight[layer].T, out_weight[layer]], axis=0)
-        up_own, down_own = up_weight[layer].T, down_weight[layer]
-        if special:
-            pieces, after_start, after_spread = gather_pieces(mixer_block, after_start, after_spread)
-            lines[layer, "mixer"] = after_start + after_spread
-            (mixer_rows,) = place_pieces(pieces, (in_rows + out_rows,), mine)
-            gated_w[layer] = []
-            halved = up_own.reshape(2, PARTS, -1, width)
-            for part in range(PARTS):
-                block = jnp.concatenate(
-                    [halved[0, part], halved[1, part], down_own.reshape(PARTS, -1, width)[part]], axis=0
-                )
-                pieces, after_start, after_spread = gather_pieces(block, after_start, after_spread)
-                lines[layer, part] = after_start + after_spread
-                up, down = place_pieces(pieces, (up_rows // PARTS, down_rows // PARTS), mine)
-                gated_w[layer].append((up.reshape(-1, down_rows // PARTS, width), down))
-        else:
-            mixer_rows = gather_rows(mixer_block, size, me)
-            gated_rows = gather_rows(jnp.concatenate([up_own, down_own], axis=0), size, me)
+        make_filter(layer)
+    steps = {}
+    if special:
+        steps[0, "mixer"] = gather_mixer(0, ())
+    else:
+        for layer in range(layers):
+            mixer_weights(layer, gather_rows(mixer_block(layer), size, me))
+            gated_block = jnp.concatenate([up_weight[layer].T, down_weight[layer]], axis=0)
+            gated_rows = gather_rows(gated_block, size, me)
             ups = pieces_of(gated_rows[:, :up_rows].reshape(-1, width), 96)
             downs = pieces_of(gated_rows[:, up_rows:].reshape(-1, width), 96)
             gated_w[layer] = list(zip(ups, downs))
-        mixer_w[layer] = (
-            mixer_rows[:, :in_rows].reshape(3 * width, width),
-            mixer_rows[:, in_rows:].reshape(width, width),
-        )
-
-    filters = [
-        filter_forward(length, decay_rate[layer], freq_in[layer], freq_bias[layer], freq_out[layer])
-        for layer in range(layers)
-    ]
 
     saved = []
     outputs = []
     for layer in range(layers):
+        norm_pack, chan_pack = packs[layer]
+        waits = []
+        ahead = (layer + 1, "mixer"), (layer + 1, "gated")
+        more = special and layer + 1 < layers
+        gated, ahead = (layer, "gated"), (layer + 1, "mixer")
+        if special:
+            if layer == 0:
+                go((0, "mixer"))
+                line = go((0, "mixer"))
+                steps[gated] = gather_gated(0, line)
+                go(gated)
+                clock[:] = go((0, "mixer"))[:1]
+            else:
+                go((layer, "mixer"))
+            waits = go(gated)
+            if more:
+                steps[ahead] = gather_mixer(layer + 1, waits)
+                go(ahead)
+            go((layer, "mixer"))
         w_in, w_out = mixer_w[layer]
-        norm_pack, chan_pack = packs[layer]
+        middle, second, normed, biased, conv, scale = mixer_forward(
+            waits, split, state, norm_pack, chan_pack, w_in, filters[layer][0], w_out
+        )
+        waits = ()
+        clock[:] = [middle]
+        waits = []
         if special:
-            state = tie(state, *lines[layer, 0][:1])
-        middle, second, normed, biased, conv, scale = mixer_forward(
-            split, state, norm_pack, chan_pack, w_in, filters[layer][0], w_out
-        )
+            go(gated)
+            if more:
+                waits = go(ahead)
+                steps[layer + 1, "gated"] = gather_gated(layer + 1, [middle])
+                go((layer + 1, "gated"))
+            go(gated)
         total = middle
         kept = []
-        for part in range(PARTS):
-            up, down = gated_w[layer][part]
-            if special and part + 1 < PARTS:
-                second = tie(second, *lines[layer, part + 1])
-            elif special and layer + 1 < layers:
-                second = tie(second, *lines[layer + 1, "mixer"][:1])
-            gate, value, total = gated_forward(second, up, down, total, norm_pack, part == 0)
-            kept.append((gate, value))
+        if special:
+            gate, value, total = gated_forward(
+                waits,
+                mine,
+                second,
+                gated_w[layer],
+                total,
+                norm_pack,
+                PARTS * hidden,
+                True,
+                tuple(range(PARTS)),
+            )
+            clock[:] = [total]
+            kept = [(gate, value)]
+        else:
+            for part in range(PARTS):
+                gate, value, total = gated_forward(
+                    [], mine, second, gated_w[layer][part], total, norm_pack, hidden, part == 0
+                )
+                kept.append((gate, value))
         saved.append((state, normed, biased, conv, scale, middle, second, kept))
         outputs.append(total)
         state = total
 
     gradient = cotangent[0].astype(f32)
-    big = [[None] * 4 for _ in range(layers)]
+    big = [None] * layers
     small = [None] * layers
-    flight = Flight()
+    moving = {}
+
+    def forward_on(*names):
+        sent = []
+        for name in names:
+            if name in moving:
+                sent.extend(next(moving[name], ()))
+        return sent
+
+    def whole_scatter(values):
+        return lax.psum_scatter(values, AXES, scatter_dimension=0)
+
     nothing = jnp.zeros((8, width), f32)
     for layer in reversed(range(layers)):
         w_in, w_out = mixer_w[layer]
@@ -1372,42 +1596,66 @@
         state_in, normed, biased, conv, scale, middle, second, kept = saved[layer]
         passed = nothing
         gated_g = []
+        by_steps = special and layer == 0
         owned = [None] * PARTS
-        for part in range(PARTS):
-            gate, value = kept[part]
-            up, down = gated_w[layer][part]
+        calls = [(part,) for part in range(PARTS)]
+        if special and not by_steps:
+            calls = [tuple(range(PARTS))]
+        for index, taken in enumerate(calls):
+            waits = []
+            if by_steps:
+                waits = forward_on("mixer", "part0")
+            elif layer == layers - 1 and index == 0:
+                waits = [state]
+            if special:
+                gate, value = kept[0]
+                own = gated_w[layer]
+            else:
+                gate, value = kept[index]
+                own = gated_w[layer][index]
             one, two, passed, sums_two = gated_backward(
-                part,
+                waits,
                 mine,
-                tie(gradient, *flight.advance()),
+                gradient,
                 passed,
                 second,
                 middle,
                 norm_pack,
                 gate,
                 value,
-                up,
-                down,
-                size,
+                own,
+                index == 0,
+                index == len(calls) - 1,
+                by_steps,
+                taken,
             )
+            clock[:] = [sums_two]
             gated_g.append((one, two))
-            if special:
-                flight.add(scatter_steps(one, two, functools.partial(owned.__setitem__, part)))
+            if by_steps:
+                moving[f"part{index}"] = scatter_steps(
+                    one, two, clock, functools.partial(owned.__setitem__, index)
+                )
+        if special and not by_steps:
+            rows = whole_scatter(gated_g[0][0])
+            owned = [rows[part * rows.shape[0] // PARTS :][: rows.shape[0] // PARTS] for part in range(PARTS)]
         grad_middle = passed
-        passed = nothing
+        passed, inner_g = nothing, nothing
         found = []
-        splits = [3] if layer else [1, 1, 1]
+        splits = [1] * (width // CB) if by_steps else [width // CB]
         start = 0
-        for steps in splits:
-            *got, passed, sums_one = mixer_backward(
+        for index, count in enumerate(splits):
+            waits = []
+            if by_steps:
+                names = [("mixer", "part0", "part1"), (), ("part0", "part1")]
+                waits = forward_on(*names[min(index, 2)])
+            *got, inner_g, freq_g, passed = mixer_backward(
+                waits,
                 start,
-                steps,
+                count,
                 split,
-                tie(grad_middle, *flight.advance()),
+                grad_middle,
                 passed,
-                state_in,
                 normed,
-                norm_pack,
                 chan_pack,
                 biased,
                 conv,
@@ -1415,53 +1663,92 @@
                 filters[layer][0],
                 w_out,
                 w_in,
+                filters[layer][1],
+                freq_out[layer],
+                inner_g,
             )
+            clock[:] = [freq_g]
             found.append(got)
-            start += steps
-        gradient = passed
+            start += count
         in_g = jnp.concatenate([got[0] for got in found], axis=1)
         out_g = jnp.concatenate([got[1] for got in found], axis=0)
-        kernel_g = jnp.concatenate([got[2] for got in found], axis=1)
-        chan_g = jnp.concatenate([got[3] for got in found], axis=1)
+        chan_g = jnp.concatenate([got[2] for got in found], axis=1)
         mixer_g = jnp.concatenate(
             [in_g.reshape(size, in_rows, width), out_g.reshape(size, out_rows, width)], axis=1
         )
 
         mixer_own = [None]
+        waits = []
         if special:
             order = jnp.arange(size // 2, dtype=jnp.int32) * 2 ^ me
+            if by_steps:
+                forward_on("part0")
+                order = hold(order, *forward_on("part1"))
             keep, send = [
                 mixer_g.at[places].get(mode="promise_in_bounds") for places in (order, order ^ 1)
             ]
-            flight.add(scatter_steps(keep, send, functools.partial(mixer_own.__setitem__, 0)))
+            while forward_on("mixer"):
+                pass
+            waits = [send]
+            moving["mixer"] = scatter_steps(
+                keep, send, clock, functools.partial(mixer_own.__setitem__, 0)
+            )
         else:
             up_g = jnp.stack([one for one, _ in gated_g], axis=1).reshape(size, -1, width)
             down_g = jnp.stack([two for _, two in gated_g], axis=1).reshape(size, -1, width)
             owned = (scatter_rows(up_g, size, me), scatter_rows(down_g, size, me))
             mixer_own[0] = scatter_rows(mixer_g, size, me)
-        grad_decay, grad_freq_in, grad_freq_bias, grad_freq_out = filter_backward(
-            kernel_g, filters[layer][1], decay_rate[layer], freq_out[layer]
-        )
-        pieces = [
-            jnp.stack([sums_one[0], sums_two[0]]),
-            jnp.stack([sums_one[1], sums_two[1]]),
-            chan_g[0:3].reshape(3 * width),
-            chan_g[3:12].reshape(3, 3 * width),
-            chan_g[12:15],
-            grad_decay,
-            grad_freq_in,
-            grad_freq_bias,
-            grad_freq_out,
-            sums_two[2],
-            sums_two[3],
-        ]
-        vector = jnp.concatenate([piece.reshape(-1) for piece in pieces])
-        vector = jnp.pad(vector, (0, -vector.size % 1024)).reshape(-1, 128)
-        summed = [None]
-        flight.add(sum_steps(vector, size, functools.partial(summed.__setitem__, 0)))
-        small[layer] = (pieces, summed)
+        gradient, sums_one = norm_finish(waits, passed, state_in, grad_middle, norm_pack)
+        small[layer] = (chan_g, freq_g, sums_one, sums_two)
         big[layer] = (owned, mixer_own)
-    flight.finish()
+
+    def lines_of(values):
+        return -(-values.size // (8 * width)) * 8
+
+    def lined(values):
+        lines = lines_of(values)
+        flat_values = jnp.pad(values.reshape(-1), (0, lines * width - values.size))
+        return flat_values.reshape(lines, width)
+
+    vector = jnp.concatenate([lined(piece) for pieces in small for piece in pieces], axis=0)
+    vector = jnp.pad(vector, ((0, -vector.shape[0] % 16), (0, 0)))
+    if special:
+        vector = hold(vector, send)
+    summed = [None]
+    sent = []
+    moving["small"] = sum_steps(vector, size, me, functools.partial(summed.__setitem__, 0), sent)
+    forward_on("mixer", "small")
+    sent.extend(forward_on("mixer"))
+    clock[:] = sent[:1]
+    while forward_on("mixer", "small", "part1", "part0"):
+        pass
+    vector = summed[0]
+    count = sum(lines_of(piece) for piece in small[0])
+    vector = vector[: layers * count].reshape(layers, count, width)
+    found = []
+    start = 0
+    for piece in small[0]:
+        lines = lines_of(piece)
+        part = vector[:, start : start + lines]
+        if piece.shape[1] != width:
+            part = part.reshape(layers, -1)[:, : piece.size]
+        found.append(part.reshape((layers,) + piece.shape))
+        start += lines
+    chan_g, freq_g, sums_one, sums_two = found
+    count = freq_in.shape[1]
+    small = [
+        jnp.stack([sums_one[:, 0], sums_two[:, 0]], axis=1),
+        jnp.stack([sums_one[:, 1], sums_two[:, 1]], axis=1),
+        chan_g[:, 0:3].reshape(layers, 3 * width),
+        chan_g[:, 3:12].reshape(layers, 3, 3 * width),
+        chan_g[:, 12:15],
+        chan_g[:, 15],
+        freq_g[:, :count],
+        jnp.sum(freq_g[:, count:], axis=1),
+        chan_g[:, 16:],
+        sums_two[:, 2],
+        sums_two[:, 3],
+    ]
 
     for layer in range(layers):
         owned, mixer_own = big[layer]
@@ -1469,21 +1756,12 @@
             piece = down_rows // PARTS
             up_own = jnp.concatenate(
                 [part[at * piece : (at + 1) * piece] for at in range(2) for part in owned], axis=0
-            )
-            down_own = jnp.concatenate([part[2 * piece :] for part in owned], axis=0)
+            ).astype(f32)
+            down_own = jnp.concatenate([part[2 * piece :] for part in owned], axis=0).astype(f32)
         else:
             up_own, down_own = owned
-        big[layer] = (mixer_own[0][:in_rows].T, mixer_own[0][in_rows:], up_own.T, down_own)
-        pieces, summed = small[layer]
-        vector = summed[0].reshape(-1)
-        taken = []
-        start = 0
-        for piece in pieces:
-            taken.append(vector[start : start + piece.size].reshape(piece.shape))
-            start += piece.size
-        small[layer] = taken
-
-    small = [jnp.stack([small[layer][index] for layer in range(layers)]) for index in range(11)]
+        mixer_rows = mixer_own[0].astype(f32)
+        big[layer] = (mixer_rows[:in_rows].T, mixer_rows[in_rows:], up_own.T, down_own)
     big = [jnp.stack([big[layer][index] for layer in range(layers)]) for index in range(4)]
     return (
         jnp.stack(outputs)[:, None],

time: 1040 us -> 892 us (0.86)
  waiting for transfers between devices: 192 us -> 128 us
  starting transfers between devices: 122 us -> 90.1 us
  other arithmetic: 98.2 us -> 67.4 us
  between operations: 3.84 us -> 26.9 us
  matrix products: 28.5 us -> 7.62 us
  Pallas kernels: 483 us -> 467 us
    ppermute x130 -> x74, waiting for transfers between devices: 192 us -> 128 us  [swap(): lax.ppermute(values, AXES, [(index, index ^ bit) for index in range(size)])]
    ppermute x130 -> x74, starting transfers between devices: 122 us -> 90.1 us  [swap(): lax.ppermute(values, AXES, [(index, index ^ bit) for index in range(size)])]
    pallas_call x6 -> x2, Pallas kernels: 34 us -> 8.66 us  [place_pieces(): pl.pallas_call(functools.partial(place_kernel, masks, cuts), in_specs=[pl...]
    dot_general x8 -> x2, matrix products: 28.5 us -> 7.62 us  [highest(): return lax.dot_general(left, right, dims, precision=lax.Precision.HIGHEST)]
    another operation x40 -> x7, other arithmetic: 33.2 us -> 13.9 us
    convert_element_type x0 -> x5, other arithmetic: none -> 12.5 us  [the longest x4 12.5 us: scatter_steps(): out = [hold(both(group), *clock).astype(bf16) for group in (3, 1, 2)]]
    add x22 -> x19, other arithmetic: 25 us -> 14.1 us  [the longest x15 14 us: hold(): value = value + (other[(0,) * other.ndim] * 0).astype(value.dtype)]
    pallas_call x14 -> x22, Pallas kernels: 428 us -> 438 us  [the longest x3 144 us: gated_backward(): call_after(after, functools.partial(gated_backward_kernel, first, last, m...]
  transfers between devices with their start and end apart: 130 -> 75, of which waited for: 43 -> 16; matrix products, arithmetic and copies ran while one was open for 21% -> 17% of each run, Pallas kernels for 47% -> 42%
where the time goes in v2:
time: 892 us; the launch traced here: 880 us
  Pallas kernels  467 us (52%)
  waiting for transfers between devices  128 us (14%)
  local copies, waits for them, and re-layouts  93 us (10%)
  starting transfers between devices  90.1 us (10%)
  other arithmetic  67.4 us (8%)
  between operations  26.9 us (3%)
    pallas_call x3, Pallas kernels, gated_backward(): call_after(after, functools.partial(gated_backward_kernel, first, last, m...  144 us
    pallas_call x4, Pallas kernels, mixer_backward(): call_after(after, functools.partial(mixer_backward_kernel, start == 0, la...  134 us
    ppermute x74, waiting for transfers between devices, swap(): lax.ppermute(values, AXES, [(index, index ^ bit) for index in range(size)])  128 us
    ppermute x74, starting transfers between devices, swap(): lax.ppermute(values, AXES, [(index, index ^ bit) for index in range(size)])  90.1 us
    pallas_call x2, Pallas kernels, mixer_forward(): call_after(after, mixer_forward_kernel, grid=(steps,), in_specs=[pl.Block...  80.3 us
    pallas_call x2, Pallas kernels, gated_forward(): call_after(after, functools.partial(gated_forward_kernel, first, masks, t...  56 us
    pallas_call x2, Pallas kernels, norm_finish(): call_after(after, norm_finish_kernel, grid=(length // block,), in_specs=[...  23.6 us
    pallas_call x2, Pallas kernels, filter_forward(): pl.pallas_call(filter_kernel_body, grid=(width // CB,), in_specs=[fixed_b...  20.4 us
  transfers between devices with their start and end apart: 75, of which 16 were waited for; matrix products, arithmetic and copies ran while one was open for 17% of the time, Pallas kernels for 42%

profile of v2, /device:TPU:0, one launch (start us, length us, event | category | flops | bytes accessed | tf_op | source)
XLA Modules:
  0.0 880.1 jit_solution(15807794810018868720)
XLA Ops:
  10.4 4.1 collective-permute-start.4
  21.2 3.8 collective-permute-start.2
  31.7 3.8 fusion.35
  40.4 10.3 %filter_forward.2 = (f32[1024,768]{1,0:T(8,128)}, f32[4,512,768]{2,1,0:T(8,128)}) custom-call(f32[1024,64]{1,0:T(8,128)} %get-tuple-element.258.inner_ref, f32[64,768]{1,0:T(8,128)} %get-tuple-element.274.out_ref.refs_24_.refs_17_.refs_23_, f32[16,768]{1,0:T(8,128)} %pad_maximum_fusion.11.chan_ref.refs_4_.refs_11_.refs_10_, ...), custom_call_target="tpu_custom_call" | custom-call | flops 6000000000 | bytes 10485760 | tf_op jit(solution)/shard_map/filter_forward/pallas_call | solution.py:1167
  50.6 12.1 %collective-permute-start = (bf16[288,768]{1,0:T(8,128)(2,1)}, bf16[288,768]{1,0:T(8,128)(2,1)}, u32[]{:S(2)}, u32[]{:S(2)}) collective-permute-start(bf16[288,768]{1,0:T(8,128)(2,1)} %broadcast_add_fusion.3), channel_id=1, source_target_pairs={{0,2},{1,3},{2,0},{3,1},{4,6},{5,7},{6,4},{7,5},{8,10},{9,11},{10,... | collective-permute-start | bytes 1327112 | tf_op jit(solution)/shard_map/ppermute | solution.py:1207
  62.8 3.2 collective-permute-done.1
  81.6 4.3 place_pieces.2
  88.3 4.0 slice.722
  92.2 40.0 %mixer_forward.2 = (f32[1024,768]{1,0:T(8,128)}, bf16[1024,768]{1,0:T(8,128)(2,1)}, bf16[1024,768]{1,0:T(8,128)(2,1)}, f32[3,1032,768]{2,1,0:T(8,128)}, f32[1024,768]{1,0:T(8,128)}, /*index=5*/f32[8,768]{1,0:T(8,128)}) custom-call(bf16[4,288,768]{2,1,0:T(8,128)(2,1)} %maximum_add_fusion.refs_0_.refs_5_.refs_9_.refs_12_, ...), custom_call_target="tpu_custom_call" | custom-call | flops 20000000000 | bytes 41943040 | tf_op jit(solution)/shard_map/mixer_forward/pallas_call | solution.py:297
  132.3 25.6 %collective-permute-done.17.refs_0_ = bf16[4,288,768]{2,1,0:T(8,128)(2,1)} collective-permute-done((bf16[4,288,768]{2,1,0:T(8,128)(2,1)}, bf16[4,288,768]{2,1,0:T(8,128)(2,1)}, u32[]{:S(2)}, u32[]{:S(2)}) %collective-permute-start.17) | collective-permute-done | bytes 1769504 | tf_op jit(solution)/shard_map/ppermute | solution.py:1207
  161.2 3.9 fusion.36
  166.9 3.6 collective-permute-start.9
  172.0 3.0 collective-permute-done.9
  175.0 7.4 collective-permute-start.8
  185.0 4.3 collective-permute-done.8
  190.4 4.1 collective-permute-done.7
  200.3 27.9 %gated_forward.2 = (bf16[1024,3072]{1,0:T(8,128)(2,1)}, bf16[1024,3072]{1,0:T(8,128)(2,1)}, f32[1024,768]{1,0:T(8,128)}) custom-call(bf16[4,96,768]{2,1,0:T(8,128)(2,1)} %maximum_add_fusion.2.refs_0_, s32[1]{0:T(128)} %bitcast.42.me_ref.refs_1_.refs_0_.refs_4_, bf16[1024,768]{1,0:T(8,128)(2,1)} %get-tuple-element.77.refs_2_.refs_4_.refs_7_, ...), custom_call_target="tpu_custom_call" | custom-call | flops 14495514624 | bytes 20971520 | tf_op jit(solution)/shard_map/gated_forward/pallas_call | solution.py:463
  233.4 10.1 %filter_forward.3 = (f32[1024,768]{1,0:T(8,128)}, f32[4,512,768]{2,1,0:T(8,128)}) custom-call(f32[1024,64]{1,0:T(8,128)} %get-tuple-element.260.inner_ref, f32[64,768]{1,0:T(8,128)} %get-tuple-element.273.out_ref.refs_17_, f32[16,768]{1,0:T(8,128)} %pad_maximum_fusion.12.chan_ref.refs_4_, bf16[512,768]{1,0:T(8,128)(2,1)} %constant.68.clone.fwd_ref.refs_7_), custom_call_target="tpu_custom_call" | custom-call | flops 6000000000 | bytes 10485760 | tf_op jit(solution)/shard_map/filter_forward/pallas_call | solution.py:1167
  252.2 4.3 place_pieces.3
  258.9 4.0 slice.728
  262.9 40.3 %mixer_forward.3 = (f32[1024,768]{1,0:T(8,128)}, bf16[1024,768]{1,0:T(8,128)(2,1)}, bf16[1024,768]{1,0:T(8,128)(2,1)}, f32[3,1032,768]{2,1,0:T(8,128)}, f32[1024,768]{1,0:T(8,128)}, /*index=5*/f32[8,768]{1,0:T(8,128)}) custom-call(bf16[4,288,768]{2,1,0:T(8,128)(2,1)} %maximum_add_fusion.1.refs_0_.refs_4_.refs_9_, ...), custom_call_target="tpu_custom_call" | custom-call | flops 20000000000 | bytes 41943040 | tf_op jit(solution)/shard_map/mixer_forward/pallas_call | solution.py:297
  303.2 24.6 %collective-permute-done.34.refs_0_ = bf16[4,288,768]{2,1,0:T(8,128)(2,1)} collective-permute-done((bf16[4,288,768]{2,1,0:T(8,128)(2,1)}, bf16[4,288,768]{2,1,0:T(8,128)(2,1)}, u32[]{:S(2)}, u32[]{:S(2)}) %collective-permute-start.34) | collective-permute-done | bytes 1769504 | tf_op jit(solution)/shard_map/ppermute | solution.py:1207
  331.4 3.3 bitcast_convert_fusion.refs_2_
  338.1 28.1 %gated_forward.3 = (bf16[1024,3072]{1,0:T(8,128)(2,1)}, bf16[1024,3072]{1,0:T(8,128)(2,1)}, f32[1024,768]{1,0:T(8,128)}) custom-call(s32[1]{0:T(128)} %bitcast.42.me_ref.refs_1_.refs_0_.refs_4_, bf16[1024,768]{1,0:T(8,128)(2,1)} %get-tuple-element.80.refs_1_.refs_4_, f32[1024,768]{1,0:T(8,128)} %get-tuple-element.81.refs_1_.refs_2_.refs_5_, ...), custom_call_target="tpu_custom_call" | custom-call | flops 14495514624 | bytes 20971520 | tf_op jit(solution)/shard_map/gated_forward/pallas_call | solution.py:463
  366.8 66.4 %gated_backward.3 = (bf16[32,288,768]{2,1,0:T(8,128)(2,1)}, bf16[16,768]{1,0:T(8,128)(2,1)}, f32[1024,768]{1,0:T(8,128)}, f32[8,768]{1,0:T(8,128)}) custom-call(f32[1024,768]{1,0:T(8,128)} %get-tuple-element.82.refs_0_, s32[1]{0:T(128)} %bitcast.42.me_ref.refs_1_.refs_0_.refs_4_, f32[1024,768]{1,0:T(8,128)} %bitcast_convert_fusion.refs_2_, ...), custom_call_target="tpu_custom_call" | custom-call | flops 28991029248 | bytes 20971520 | tf_op jit(solution)/shard_map/gated_backward/pallas_call | solution.py:686
  433.2 61.7 %mixer_backward.4 = (bf16[3,768,768]{2,1,0:T(8,128)(2,1)}, bf16[768,768]{1,0:T(8,128)(2,1)}, f32[80,768]{1,0:T(8,128)}, f32[1024,64]{1,0:T(8,128)}, f32[72,64]{1,0:T(8,128)}, /*index=5*/f32[1024,768]{1,0:T(8,128)}) custom-call(s32[1]{0:T(128)S(6)} %copy.151.refs_1_.refs_0_.refs_7_.refs_6_, f32[1024,768]{1,0:T(8,128)} %get-tuple-element.85.refs_1_.refs_3_, ...), custom_call_target="tpu_custom_call" | custom-call | flops 35999997952 | bytes 44040192 | tf_op jit(solution)/shard_map/mixer_backward/pallas_call | solution.py:1006
  495.0 5.1 pad_maximum_fusion
  500.1 4.5 gather_fusion.1
  504.8 11.8 %norm_finish.2 = (f32[1024,768]{1,0:T(8,128)}, f32[8,768]{1,0:T(8,128)}) custom-call(bf16[16,96,768]{2,1,0:T(8,128)(2,1)} %gather_fusion.1, f32[1024,768]{1,0:T(8,128)} %get-tuple-element.93.refs_1_, f32[1024,768]{1,0:T(8,128)} %get-tuple-element.78.refs_1_.refs_2_, f32[1024,768]{1,0:T(8,128)} %get-tuple-element.85.refs_1_.refs_3_, ...), custom_call_target="tpu_custom_call" | custom-call | flops 3000000000 | bytes 16777216 | tf_op jit(solution)/shard_map/norm_finish/pallas_call | solution.py:1113
  516.6 33.8 %gated_backward.4 = (bf16[16,144,768]{2,1,0:T(8,128)(2,1)}, bf16[16,144,768]{2,1,0:T(8,128)(2,1)}, f32[1024,768]{1,0:T(8,128)}, f32[8,768]{1,0:T(8,128)}) custom-call(bf16[16,96,768]{2,1,0:T(8,128)(2,1)} %gather_fusion.1, s32[1]{0:T(128)} %bitcast.42.me_ref.refs_1_.refs_0_.refs_4_, f32[1024,768]{1,0:T(8,128)} %get-tuple-element.94.refs_2_.refs_5_, ...), custom_call_target="tpu_custom_call" | custom-call | flops 14495514624 | bytes 20971520 | tf_op jit(solution)/shard_map/gated_backward/pallas_call | solution.py:686
  552.4 4.6 gather_fusion
  558.8 5.1 maximum_bitcast_fusion
  570.4 43.3 %gated_backward.5 = (bf16[16,144,768]{2,1,0:T(8,128)(2,1)}, bf16[16,144,768]{2,1,0:T(8,128)(2,1)}, f32[1024,768]{1,0:T(8,128)}, f32[8,768]{1,0:T(8,128)}) custom-call(bf16[4,96,768]{2,1,0:T(8,128)(2,1)} %copy-done.27, bf16[4,96,768]{2,1,0:T(8,128)(2,1)} %copy-done.28, bf16[4,96,768]{2,1,0:T(8,128)(2,1)} %copy-done.29, ...), custom_call_target="tpu_custom_call" | custom-call | flops 14495514624 | bytes 20971520 | tf_op jit(solution)/shard_map/gated_backward/pallas_call | solution.py:686
  621.3 3.7 add_convert_fusion.3
  628.5 23.4 %mixer_backward.5 = (bf16[3,256,768]{2,1,0:T(8,128)(2,1)}, bf16[256,768]{1,0:T(8,128)(2,1)}, f32[80,256]{1,0:T(8,128)}, f32[1024,64]{1,0:T(8,128)}, f32[72,64]{1,0:T(8,128)}, /*index=5*/f32[1024,768]{1,0:T(8,128)}) custom-call(bf16[96,768]{1,0:T(8,128)(2,1)} %get-tuple-element.254.refs_0_, bf16[96,768]{1,0:T(8,128)(2,1)} %get-tuple-element.253.refs_1_, ...), custom_call_target="tpu_custom_call" | custom-call | flops 12000000000 | bytes 14680064 | tf_op jit(solution)/shard_map/mixer_backward/pallas_call | solution.py:1006
  651.9 24.4 %mixer_backward.6 = (bf16[3,256,768]{2,1,0:T(8,128)(2,1)}, bf16[256,768]{1,0:T(8,128)(2,1)}, f32[80,256]{1,0:T(8,128)}, f32[1024,64]{1,0:T(8,128)}, f32[72,64]{1,0:T(8,128)}, /*index=5*/f32[1024,768]{1,0:T(8,128)}) custom-call(s32[1]{0:T(128)S(6)} %copy.151.refs_1_.refs_0_.refs_7_.refs_6_, f32[1024,768]{1,0:T(8,128)} %get-tuple-element.103.refs_8_.refs_1_.refs_7_.refs_3_, ...), custom_call_target="tpu_custom_call" | custom-call | flops 12000000000 | bytes 14680064 | tf_op jit(solution)/shard_map/mixer_backward/pallas_call | solution.py:1006
  680.8 4.2 fusion.30
  685.9 3.7 add_convert_fusion
  693.1 24.8 %mixer_backward.7 = (bf16[3,256,768]{2,1,0:T(8,128)(2,1)}, bf16[256,768]{1,0:T(8,128)(2,1)}, f32[80,256]{1,0:T(8,128)}, f32[1024,64]{1,0:T(8,128)}, f32[72,64]{1,0:T(8,128)}, /*index=5*/f32[1024,768]{1,0:T(8,128)}) custom-call(bf16[144,768]{1,0:T(8,128)(2,1)} %get-tuple-element.237.refs_0_, bf16[144,768]{1,0:T(8,128)(2,1)} %get-tuple-element.236.refs_1_, ...), custom_call_target="tpu_custom_call" | custom-call | flops 12000000000 | bytes 14680064 | tf_op jit(solution)/shard_map/mixer_backward/pallas_call | solution.py:1006
  739.7 3.9 fusion.29
  750.0 4.5 gather_fusion.2
  762.7 11.8 %norm_finish.3 = (f32[1024,768]{1,0:T(8,128)}, f32[8,768]{1,0:T(8,128)}) custom-call(bf16[16,96,768]{2,1,0:T(8,128)(2,1)} %gather_fusion.2, f32[1024,768]{1,0:T(8,128)} %get-tuple-element.122.refs_1_, f32[1024,768]{1,0:T(8,128)} %bitcast_convert_fusion.1.refs_2_, f32[1024,768]{1,0:T(8,128)} %get-tuple-element.103.refs_8_.refs_1_.refs_7_.refs_3_, ...), custom_call_target="tpu_custom_call" | custom-call | flops 3000000000 | bytes 16777216 | tf_op jit(solution)/shard_map/norm_finish/pallas_call | solution.py:1113
  776.2 3.0 gather_fusion.3
  795.1 24.6 %collective-permute-done.54 = f32[104,768]{1,0:T(8,128)S(1)} collective-permute-done((f32[104,768]{1,0:T(8,128)S(1)}, f32[104,768]{1,0:T(8,128)S(1)}, u32[]{:S(2)}, u32[]{:S(2)}) %collective-permute-start.54) | collective-permute-done | bytes 319520 | tf_op jit(solution)/shard_map/ppermute | solution.py:1207
  826.2 3.1 collective-permute-done.55
  833.2 13.9 %collective-permute-done.63 = bf16[96,768]{1,0:T(8,128)(2,1)S(1)} collective-permute-done((bf16[96,768]{1,0:T(8,128)(2,1)S(1)}, bf16[96,768]{1,0:T(8,128)(2,1)S(1)}, u32[]{:S(2)}, u32[]{:S(2)}) %collective-permute-start.63) | collective-permute-done | bytes 147488 | tf_op jit(solution)/shard_map/ppermute | solution.py:1207
  847.2 5.3 collective-permute-done.56
  853.3 7.4 collective-permute-done.57
  (429 shorter events, 174.9 us)
Async XLA Ops:
  7.2 862.5 %reduce-scatter.2.cloned.1.call-start = ((), (), s32[]{:S(2)}) async-start(), calls=%async_computation.1 | async-start | bytes 14598144 | tf_op jit(solution)/shard_map/reduce_scatter | solution.py:1590
  10.4 25.7 %collective-permute-start.4 = (bf16[96,768]{1,0:T(8,128)(2,1)S(1)}, bf16[96,768]{1,0:T(8,128)(2,1)S(1)}, u32[]{:S(2)}, u32[]{:S(2)}) collective-permute-start(bf16[96,768]{1,0:T(8,128)(2,1)S(1)} %get-tuple-element.284), channel_id=1, source_target_pairs={{0,4},{1,5},{2,6},{3,7},{4,0},{5,1},{6,2},{7,3},{8,12},{9,13},{10,... | collective-permute-start | bytes 442376 | tf_op jit(solution)/shard_map/ppermute | solution.py:1207
  21.2 29.5 %collective-permute-start.2 = (bf16[288,768]{1,0:T(8,128)(2,1)}, bf16[288,768]{1,0:T(8,128)(2,1)}, u32[]{:S(2)}, u32[]{:S(2)}) collective-permute-start(bf16[288,768]{1,0:T(8,128)(2,1)} %broadcast_add_fusion.3), channel_id=1, source_target_pairs={{0,6},{1,7},{2,4},{3,5},{4,2},{5,3},{6,0},{7,1},{8,14},{9,15},{10,... | collective-permute-start | bytes 1327112 | tf_op jit(solution)/shard_map/ppermute | solution.py:1207
  25.0 41.0 %collective-permute-start.1 = (bf16[288,768]{1,0:T(8,128)(2,1)}, bf16[288,768]{1,0:T(8,128)(2,1)}, u32[]{:S(2)}, u32[]{:S(2)}) collective-permute-start(bf16[288,768]{1,0:T(8,128)(2,1)} %broadcast_add_fusion.3), channel_id=1, source_target_pairs={{0,4},{1,5},{2,6},{3,7},{4,0},{5,1},{6,2},{7,3},{8,12},{9,13},{10,... | collective-permute-start | bytes 1327112 | tf_op jit(solution)/shard_map/ppermute | solution.py:1207
  36.2 29.8 %collective-permute-start.14 = (bf16[4,96,768]{2,1,0:T(8,128)(2,1)S(1)}, bf16[4,96,768]{2,1,0:T(8,128)(2,1)}, u32[]{:S(2)}, u32[]{:S(2)}) collective-permute-start(bf16[4,96,768]{2,1,0:T(8,128)(2,1)S(1)} %pad_maximum_fusion.6.refs_0_), channel_id=1, source_target_pairs={{0,24},{1,25},{2,26},{3,27},{4,28},{5,29},{6,30},{7,31},{8,16},{9,... | collective-permute-start | bytes 1769480 | tf_op jit(solution)/shard_map/ppermute | solution.py:1207
  38.7 27.8 %collective-permute-start.12 = (bf16[4,96,768]{2,1,0:T(8,128)(2,1)S(1)}, bf16[4,96,768]{2,1,0:T(8,128)(2,1)}, u32[]{:S(2)}, u32[]{:S(2)}) collective-permute-start(bf16[4,96,768]{2,1,0:T(8,128)(2,1)S(1)} %pad_maximum_fusion.6.refs_0_), channel_id=1, source_target_pairs={{0,16},{1,17},{2,18},{3,19},{4,20},{5,21},{6,22},{7,23},{8,24},{9,... | collective-permute-start | bytes 1769480 | tf_op jit(solution)/shard_map/ppermute | solution.py:1207
  39.2 27.4 %collective-permute-start.6 = (bf16[4,96,768]{2,1,0:T(8,128)(2,1)S(1)}, bf16[4,96,768]{2,1,0:T(8,128)(2,1)}, u32[]{:S(2)}, u32[]{:S(2)}) collective-permute-start(bf16[4,96,768]{2,1,0:T(8,128)(2,1)S(1)} %pad_maximum_fusion.6.refs_0_), channel_id=1, source_target_pairs={{0,8},{1,9},{2,10},{3,11},{4,12},{5,13},{6,14},{7,15},{8,0},{9,1},... | collective-permute-start | bytes 1769480 | tf_op jit(solution)/shard_map/ppermute | solution.py:1207
  50.6 24.7 %collective-permute-start = (bf16[288,768]{1,0:T(8,128)(2,1)}, bf16[288,768]{1,0:T(8,128)(2,1)}, u32[]{:S(2)}, u32[]{:S(2)}) collective-permute-start(bf16[288,768]{1,0:T(8,128)(2,1)} %broadcast_add_fusion.3), channel_id=1, source_target_pairs={{0,2},{1,3},{2,0},{3,1},{4,6},{5,7},{6,4},{7,5},{8,10},{9,11},{10,... | collective-permute-start | bytes 1327112 | tf_op jit(solution)/shard_map/ppermute | solution.py:1207
  78.1 80.4 %collective-permute-start.21 = (bf16[4,288,768]{2,1,0:T(8,128)(2,1)}, bf16[4,288,768]{2,1,0:T(8,128)(2,1)S(1)}, u32[]{:S(2)}, u32[]{:S(2)}) collective-permute-start(bf16[4,288,768]{2,1,0:T(8,128)(2,1)} %maximum_add_fusion.refs_0_.refs_5_.refs_9_.refs_12_), channel_id=1, source_target_pairs={{0,24},{1,25},{2,26},{3,27},{4,28},{5,29},{6,30},{7,31},{8,16},{9,... | collective-permute-start | bytes 5308424 | tf_op jit(solution)/shard_map/ppermute | solution.py:1207
  80.6 77.3 %collective-permute-start.19 = (bf16[4,288,768]{2,1,0:T(8,128)(2,1)}, bf16[4,288,768]{2,1,0:T(8,128)(2,1)}, u32[]{:S(2)}, u32[]{:S(2)}) collective-permute-start(bf16[4,288,768]{2,1,0:T(8,128)(2,1)} %maximum_add_fusion.refs_0_.refs_5_.refs_9_.refs_12_), channel_id=1, source_target_pairs={{0,16},{1,17},{2,18},{3,19},{4,20},{5,21},{6,22},{7,23},{8,24},{9,... | collective-permute-start | bytes 5308424 | tf_op jit(solution)/shard_map/ppermute | solution.py:1207
  81.1 76.8 %collective-permute-start.17 = (bf16[4,288,768]{2,1,0:T(8,128)(2,1)}, bf16[4,288,768]{2,1,0:T(8,128)(2,1)}, u32[]{:S(2)}, u32[]{:S(2)}) collective-permute-start(bf16[4,288,768]{2,1,0:T(8,128)(2,1)} %maximum_add_fusion.refs_0_.refs_5_.refs_9_.refs_12_), channel_id=1, source_target_pairs={{0,8},{1,9},{2,10},{3,11},{4,12},{5,13},{6,14},{7,15},{8,0},{9,1},... | collective-permute-start | bytes 5308424 | tf_op jit(solution)/shard_map/ppermute | solution.py:1207
  81.6 115.2 %collective-permute-start.16 = (bf16[4,288,768]{2,1,0:T(8,128)(2,1)}, bf16[4,288,768]{2,1,0:T(8,128)(2,1)}, u32[]{:S(2)}, u32[]{:S(2)}) collective-permute-start(bf16[4,288,768]{2,1,0:T(8,128)(2,1)} %maximum_add_fusion.refs_0_.refs_5_.refs_9_.refs_12_), channel_id=1, source_target_pairs={{0,1},{1,0},{2,3},{3,2},{4,5},{5,4},{6,7},{7,6},{8,9},{9,8},{10,11... | collective-permute-start | bytes 5308424 | tf_op jit(solution)/shard_map/ppermute | solution.py:1207
  157.9 39.0 %collective-permute-start.18 = (bf16[4,288,768]{2,1,0:T(8,128)(2,1)}, bf16[4,288,768]{2,1,0:T(8,128)(2,1)}, u32[]{:S(2)}, u32[]{:S(2)}) collective-permute-start(bf16[4,288,768]{2,1,0:T(8,128)(2,1)} %hold_place.9.refs_7_.refs_11_.refs_14_), channel_id=1, source_target_pairs={{0,1},{1,0},{2,3},{3,2},{4,5},{5,4},{6,7},{7,6},{8,9},{9,8},{10,11... | collective-permute-start | bytes 5308424 | tf_op jit(solution)/shard_map/ppermute | solution.py:1207
  157.9 40.4 %collective-permute-start.20 = (bf16[4,288,768]{2,1,0:T(8,128)(2,1)}, bf16[4,288,768]{2,1,0:T(8,128)(2,1)}, u32[]{:S(2)}, u32[]{:S(2)}) collective-permute-start(bf16[4,288,768]{2,1,0:T(8,128)(2,1)} %hold_place.10.refs_9_.refs_13_.refs_16_), channel_id=1, source_target_pairs={{0,1},{1,0},{2,3},{3,2},{4,5},{5,4},{6,7},{7,6},{8,9},{9,8},{10,11... | collective-permute-start | bytes 5308424 | tf_op jit(solution)/shard_map/ppermute | solution.py:1207
  159.8 39.2 %collective-permute-start.22 = (bf16[4,288,768]{2,1,0:T(8,128)(2,1)}, bf16[4,288,768]{2,1,0:T(8,128)(2,1)}, u32[]{:S(2)}, u32[]{:S(2)}) collective-permute-start(bf16[4,288,768]{2,1,0:T(8,128)(2,1)} %hold_place.11.refs_11_.refs_15_.refs_18_), channel_id=1, source_target_pairs={{0,1},{1,0},{2,3},{3,2},{4,5},{5,4},{6,7},{7,6},{8,9},{9,8},{10,11... | collective-permute-start | bytes 5308424 | tf_op jit(solution)/shard_map/ppermute | solution.py:1207
  194.5 38.4 %collective-permute-start.25 = (bf16[288,768]{1,0:T(8,128)(2,1)S(1)}, bf16[288,768]{1,0:T(8,128)(2,1)S(1)}, u32[]{:S(2)}, u32[]{:S(2)}) collective-permute-start(bf16[288,768]{1,0:T(8,128)(2,1)S(1)} %broadcast_add_fusion.1), channel_id=1, source_target_pairs={{0,6},{1,7},{2,4},{3,5},{4,2},{5,3},{6,0},{7,1},{8,14},{9,15},{10,... | collective-permute-start | bytes 1327112 | tf_op jit(solution)/shard_map/ppermute | solution.py:1207
  196.7 36.1 %collective-permute-start.24 = (bf16[288,768]{1,0:T(8,128)(2,1)S(1)}, bf16[288,768]{1,0:T(8,128)(2,1)}, u32[]{:S(2)}, u32[]{:S(2)}) collective-permute-start(bf16[288,768]{1,0:T(8,128)(2,1)S(1)} %broadcast_add_fusion.1), channel_id=1, source_target_pairs={{0,4},{1,5},{2,6},{3,7},{4,0},{5,1},{6,2},{7,3},{8,12},{9,13},{10,... | collective-permute-start | bytes 1327112 | tf_op jit(solution)/shard_map/ppermute | solution.py:1207
  196.8 31.4 %collective-permute-start.31 = (bf16[4,96,768]{2,1,0:T(8,128)(2,1)}, bf16[4,96,768]{2,1,0:T(8,128)(2,1)S(1)}, u32[]{:S(2)}, u32[]{:S(2)}) collective-permute-start(bf16[4,96,768]{2,1,0:T(8,128)(2,1)} %maximum_add_fusion.2.refs_0_), channel_id=1, source_target_pairs={{0,24},{1,25},{2,26},{3,27},{4,28},{5,29},{6,30},{7,31},{8,16},{9,... | collective-permute-start | bytes 1769480 | tf_op jit(solution)/shard_map/ppermute | solution.py:1207
  198.3 33.8 %collective-permute-start.29 = (bf16[4,96,768]{2,1,0:T(8,128)(2,1)}, bf16[4,96,768]{2,1,0:T(8,128)(2,1)S(1)}, u32[]{:S(2)}, u32[]{:S(2)}) collective-permute-start(bf16[4,96,768]{2,1,0:T(8,128)(2,1)} %maximum_add_fusion.2.refs_0_), channel_id=1, source_target_pairs={{0,16},{1,17},{2,18},{3,19},{4,20},{5,21},{6,22},{7,23},{8,24},{9,... | collective-permute-start | bytes 1769480 | tf_op jit(solution)/shard_map/ppermute | solution.py:1207
  199.0 32.2 %collective-permute-start.27 = (bf16[4,96,768]{2,1,0:T(8,128)(2,1)}, bf16[4,96,768]{2,1,0:T(8,128)(2,1)S(1)}, u32[]{:S(2)}, u32[]{:S(2)}) collective-permute-start(bf16[4,96,768]{2,1,0:T(8,128)(2,1)} %maximum_add_fusion.2.refs_0_), channel_id=1, source_target_pairs={{0,8},{1,9},{2,10},{3,11},{4,12},{5,13},{6,14},{7,15},{8,0},{9,1},... | collective-permute-start | bytes 1769480 | tf_op jit(solution)/shard_map/ppermute | solution.py:1207
  248.7 80.2 %collective-permute-start.38 = (bf16[4,288,768]{2,1,0:T(8,128)(2,1)}, bf16[4,288,768]{2,1,0:T(8,128)(2,1)S(1)}, u32[]{:S(2)}, u32[]{:S(2)}) collective-permute-start(bf16[4,288,768]{2,1,0:T(8,128)(2,1)} %maximum_add_fusion.1.refs_0_.refs_4_.refs_9_), channel_id=1, source_target_pairs={{0,24},{1,25},{2,26},{3,27},{4,28},{5,29},{6,30},{7,31},{8,16},{9,... | collective-permute-start | bytes 5308424 | tf_op jit(solution)/shard_map/ppermute | solution.py:1207
  250.1 78.6 %collective-permute-start.36 = (bf16[4,288,768]{2,1,0:T(8,128)(2,1)}, bf16[4,288,768]{2,1,0:T(8,128)(2,1)}, u32[]{:S(2)}, u32[]{:S(2)}) collective-permute-start(bf16[4,288,768]{2,1,0:T(8,128)(2,1)} %maximum_add_fusion.1.refs_0_.refs_4_.refs_9_), channel_id=1, source_target_pairs={{0,16},{1,17},{2,18},{3,19},{4,20},{5,21},{6,22},{7,23},{8,24},{9,... | collective-permute-start | bytes 5308424 | tf_op jit(solution)/shard_map/ppermute | solution.py:1207
  250.6 77.1 %collective-permute-start.34 = (bf16[4,288,768]{2,1,0:T(8,128)(2,1)}, bf16[4,288,768]{2,1,0:T(8,128)(2,1)}, u32[]{:S(2)}, u32[]{:S(2)}) collective-permute-start(bf16[4,288,768]{2,1,0:T(8,128)(2,1)} %maximum_add_fusion.1.refs_0_.refs_4_.refs_9_), channel_id=1, source_target_pairs={{0,8},{1,9},{2,10},{3,11},{4,12},{5,13},{6,14},{7,15},{8,0},{9,1},... | collective-permute-start | bytes 5308424 | tf_op jit(solution)/shard_map/ppermute | solution.py:1207
  252.2 82.5 %collective-permute-start.33 = (bf16[4,288,768]{2,1,0:T(8,128)(2,1)}, bf16[4,288,768]{2,1,0:T(8,128)(2,1)}, u32[]{:S(2)}, u32[]{:S(2)}) collective-permute-start(bf16[4,288,768]{2,1,0:T(8,128)(2,1)} %maximum_add_fusion.1.refs_0_.refs_4_.refs_9_), channel_id=1, source_target_pairs={{0,1},{1,0},{2,3},{3,2},{4,5},{5,4},{6,7},{7,6},{8,9},{9,8},{10,11... | collective-permute-start | bytes 5308424 | tf_op jit(solution)/shard_map/ppermute | solution.py:1207
  504.6 59.3 %collective-permute-start.40 = (bf16[16,96,768]{2,1,0:T(8,128)(2,1)}, bf16[16,96,768]{2,1,0:T(8,128)(2,1)}, u32[]{:S(2)}, u32[]{:S(2)}) collective-permute-start(bf16[16,96,768]{2,1,0:T(8,128)(2,1)} %gather_fusion.1), channel_id=1, source_target_pairs={{0,1},{1,0},{2,3},{3,2},{4,5},{5,4},{6,7},{7,6},{8,9},{9,8},{10,11... | collective-permute-start | bytes 7077896 | tf_op jit(solution)/shard_map/ppermute | solution.py:1207
  550.4 70.9 %collective-permute-start.44 = (bf16[16,144,768]{2,1,0:T(8,128)(2,1)}, bf16[16,144,768]{2,1,0:T(8,128)(2,1)}, u32[]{:S(2)}, u32[]{:S(2)}) collective-permute-start(bf16[16,144,768]{2,1,0:T(8,128)(2,1)} %get-tuple-element.98.refs_3_), channel_id=1, source_target_pairs={{0,1},{1,0},{2,3},{3,2},{4,5},{5,4},{6,7},{7,6},{8,9},{9,8},{10,11... | collective-permute-start | bytes 10616840 | tf_op jit(solution)/shard_map/ppermute | solution.py:1207
  566.1 49.5 %collective-permute-start.43 = (bf16[4,96,768]{2,1,0:T(8,128)(2,1)S(1)}, bf16[4,96,768]{2,1,0:T(8,128)(2,1)S(1)}, u32[]{:S(2)}, u32[]{:S(2)}) collective-permute-start(bf16[4,96,768]{2,1,0:T(8,128)(2,1)S(1)} %get-tuple-element.229.refs_2_), channel_id=1, source_target_pairs={{0,16},{1,17},{2,18},{3,19},{4,20},{5,21},{6,22},{7,23},{8,24},{9,... | collective-permute-start | bytes 1769480 | tf_op jit(solution)/shard_map/ppermute | solution.py:1207
  568.8 46.8 %collective-permute-start.42 = (bf16[4,96,768]{2,1,0:T(8,128)(2,1)S(1)}, bf16[4,96,768]{2,1,0:T(8,128)(2,1)S(1)}, u32[]{:S(2)}, u32[]{:S(2)}) collective-permute-start(bf16[4,96,768]{2,1,0:T(8,128)(2,1)S(1)} %get-tuple-element.230.refs_1_), channel_id=1, source_target_pairs={{0,8},{1,9},{2,10},{3,11},{4,12},{5,13},{6,14},{7,15},{8,0},{9,1},... | collective-permute-start | bytes 1769480 | tf_op jit(solution)/shard_map/ppermute | solution.py:1207
  569.3 46.3 %collective-permute-start.41 = (bf16[4,96,768]{2,1,0:T(8,128)(2,1)S(1)}, bf16[4,96,768]{2,1,0:T(8,128)(2,1)S(1)}, u32[]{:S(2)}, u32[]{:S(2)}) collective-permute-start(bf16[4,96,768]{2,1,0:T(8,128)(2,1)S(1)} %get-tuple-element.231.refs_0_), channel_id=1, source_target_pairs={{0,24},{1,25},{2,26},{3,27},{4,28},{5,29},{6,30},{7,31},{8,16},{9,... | collective-permute-start | bytes 1769480 | tf_op jit(solution)/shard_map/ppermute | solution.py:1207
  615.5 70.3 %collective-permute-start.48 = (bf16[16,144,768]{2,1,0:T(8,128)(2,1)}, bf16[16,144,768]{2,1,0:T(8,128)(2,1)}, u32[]{:S(2)}, u32[]{:S(2)}) collective-permute-start(bf16[16,144,768]{2,1,0:T(8,128)(2,1)} %get-tuple-element.102.refs_6_), channel_id=1, source_target_pairs={{0,1},{1,0},{2,3},{3,2},{4,5},{5,4},{6,7},{7,6},{8,9},{9,8},{10,11... | collective-permute-start | bytes 10616840 | tf_op jit(solution)/shard_map/ppermute | solution.py:1207
  619.2 103.8 %collective-permute-start.67 = (bf16[96,768]{1,0:T(8,128)(2,1)}, bf16[96,768]{1,0:T(8,128)(2,1)}, u32[]{:S(2)}, u32[]{:S(2)}) collective-permute-start(bf16[96,768]{1,0:T(8,128)(2,1)} %get-tuple-element.252.refs_2_), channel_id=1, source_target_pairs={{0,6},{1,7},{2,4},{3,5},{4,2},{5,3},{6,0},{7,1},{8,14},{9,15},{10,... | collective-permute-start | bytes 442376 | tf_op jit(solution)/shard_map/ppermute | solution.py:1207
  625.0 53.2 %collective-permute-start.47 = (bf16[4,144,768]{2,1,0:T(8,128)(2,1)}, bf16[4,144,768]{2,1,0:T(8,128)(2,1)S(1)}, u32[]{:S(2)}, u32[]{:S(2)}) collective-permute-start(bf16[4,144,768]{2,1,0:T(8,128)(2,1)} %get-tuple-element.223.refs_5_), channel_id=1, source_target_pairs={{0,16},{1,17},{2,18},{3,19},{4,20},{5,21},{6,22},{7,23},{8,24},{9,... | collective-permute-start | bytes 2654216 | tf_op jit(solution)/shard_map/ppermute | solution.py:1207
  626.7 52.3 %collective-permute-start.46 = (bf16[4,144,768]{2,1,0:T(8,128)(2,1)}, bf16[4,144,768]{2,1,0:T(8,128)(2,1)S(1)}, u32[]{:S(2)}, u32[]{:S(2)}) collective-permute-start(bf16[4,144,768]{2,1,0:T(8,128)(2,1)} %get-tuple-element.224.refs_4_), channel_id=1, source_target_pairs={{0,8},{1,9},{2,10},{3,11},{4,12},{5,13},{6,14},{7,15},{8,0},{9,1},... | collective-permute-start | bytes 2654216 | tf_op jit(solution)/shard_map/ppermute | solution.py:1207
  626.7 52.2 %collective-permute-start.45 = (bf16[4,144,768]{2,1,0:T(8,128)(2,1)S(1)}, bf16[4,144,768]{2,1,0:T(8,128)(2,1)S(1)}, u32[]{:S(2)}, u32[]{:S(2)}) collective-permute-start(bf16[4,144,768]{2,1,0:T(8,128)(2,1)S(1)} %get-tuple-element.225.refs_3_), channel_id=1, source_target_pairs={{0,24},{1,25},{2,26},{3,27},{4,28},{5,29},{6,30},{7,31},{8,16},{9,... | collective-permute-start | bytes 2654216 | tf_op jit(solution)/shard_map/ppermute | solution.py:1207
  678.2 55.2 %collective-permute-start.66 = (bf16[96,768]{1,0:T(8,128)(2,1)}, bf16[96,768]{1,0:T(8,128)(2,1)}, u32[]{:S(2)}, u32[]{:S(2)}) collective-permute-start(bf16[96,768]{1,0:T(8,128)(2,1)} %get-tuple-element.253.refs_1_), channel_id=1, source_target_pairs={{0,4},{1,5},{2,6},{3,7},{4,0},{5,1},{6,2},{7,3},{8,12},{9,13},{10,... | collective-permute-start | bytes 442376 | tf_op jit(solution)/shard_map/ppermute | solution.py:1207
  689.6 47.8 %collective-permute-start.51 = (bf16[4,144,768]{2,1,0:T(8,128)(2,1)}, bf16[4,144,768]{2,1,0:T(8,128)(2,1)}, u32[]{:S(2)}, u32[]{:S(2)}) collective-permute-start(bf16[4,144,768]{2,1,0:T(8,128)(2,1)} %get-tuple-element.220.refs_5_), channel_id=1, source_target_pairs={{0,16},{1,17},{2,18},{3,19},{4,20},{5,21},{6,22},{7,23},{8,24},{9,... | collective-permute-start | bytes 2654216 | tf_op jit(solution)/shard_map/ppermute | solution.py:1207
  691.5 48.3 %collective-permute-start.50 = (bf16[4,144,768]{2,1,0:T(8,128)(2,1)}, bf16[4,144,768]{2,1,0:T(8,128)(2,1)}, u32[]{:S(2)}, u32[]{:S(2)}) collective-permute-start(bf16[4,144,768]{2,1,0:T(8,128)(2,1)} %get-tuple-element.221.refs_4_), channel_id=1, source_target_pairs={{0,8},{1,9},{2,10},{3,11},{4,12},{5,13},{6,14},{7,15},{8,0},{9,1},... | collective-permute-start | bytes 2654216 | tf_op jit(solution)/shard_map/ppermute | solution.py:1207
  691.5 48.3 %collective-permute-start.49 = (bf16[4,144,768]{2,1,0:T(8,128)(2,1)}, bf16[4,144,768]{2,1,0:T(8,128)(2,1)}, u32[]{:S(2)}, u32[]{:S(2)}) collective-permute-start(bf16[4,144,768]{2,1,0:T(8,128)(2,1)} %get-tuple-element.222.refs_3_), channel_id=1, source_target_pairs={{0,24},{1,25},{2,26},{3,27},{4,28},{5,29},{6,30},{7,31},{8,16},{9,... | collective-permute-start | bytes 2654216 | tf_op jit(solution)/shard_map/ppermute | solution.py:1207
  754.5 24.7 %collective-permute-start.53 = (bf16[16,96,768]{2,1,0:T(8,128)(2,1)}, bf16[16,96,768]{2,1,0:T(8,128)(2,1)}, u32[]{:S(2)}, u32[]{:S(2)}) collective-permute-start(bf16[16,96,768]{2,1,0:T(8,128)(2,1)} %gather_fusion.2), channel_id=1, source_target_pairs={{0,1},{1,0},{2,3},{3,2},{4,5},{5,4},{6,7},{7,6},{8,9},{9,8},{10,11... | collective-permute-start | bytes 7077896 | tf_op jit(solution)/shard_map/ppermute | solution.py:1207
  757.3 31.7 %collective-permute-start.71 = (bf16[144,768]{1,0:T(8,128)(2,1)}, bf16[144,768]{1,0:T(8,128)(2,1)}, u32[]{:S(2)}, u32[]{:S(2)}) collective-permute-start(bf16[144,768]{1,0:T(8,128)(2,1)} %get-tuple-element.232), channel_id=1, source_target_pairs={{0,2},{1,3},{2,0},{3,1},{4,6},{5,7},{6,4},{7,5},{8,10},{9,11},{10,... | collective-permute-start | bytes 663560 | tf_op jit(solution)/shard_map/ppermute | solution.py:1207
  757.3 34.4 %collective-permute-start.73 = (bf16[144,768]{1,0:T(8,128)(2,1)}, bf16[144,768]{1,0:T(8,128)(2,1)}, u32[]{:S(2)}, u32[]{:S(2)}) collective-permute-start(bf16[144,768]{1,0:T(8,128)(2,1)} %get-tuple-element.233), channel_id=1, source_target_pairs={{0,6},{1,7},{2,4},{3,5},{4,2},{5,3},{6,0},{7,1},{8,14},{9,15},{10,... | collective-permute-start | bytes 663560 | tf_op jit(solution)/shard_map/ppermute | solution.py:1207
  759.3 34.4 %collective-permute-start.72 = (bf16[144,768]{1,0:T(8,128)(2,1)}, bf16[144,768]{1,0:T(8,128)(2,1)}, u32[]{:S(2)}, u32[]{:S(2)}) collective-permute-start(bf16[144,768]{1,0:T(8,128)(2,1)} %get-tuple-element.234), channel_id=1, source_target_pairs={{0,4},{1,5},{2,6},{3,7},{4,0},{5,1},{6,2},{7,3},{8,12},{9,13},{10,... | collective-permute-start | bytes 663560 | tf_op jit(solution)/shard_map/ppermute | solution.py:1207
  783.4 37.4 %collective-permute-start.59 = (bf16[4,96,768]{2,1,0:T(8,128)(2,1)}, bf16[4,96,768]{2,1,0:T(8,128)(2,1)}, u32[]{:S(2)}, u32[]{:S(2)}) collective-permute-start(bf16[4,96,768]{2,1,0:T(8,128)(2,1)} %get-tuple-element.226), channel_id=1, source_target_pairs={{0,24},{1,25},{2,26},{3,27},{4,28},{5,29},{6,30},{7,31},{8,16},{9,... | collective-permute-start | bytes 1769480 | tf_op jit(solution)/shard_map/ppermute | solution.py:1207
  789.0 31.8 %collective-permute-start.61 = (bf16[4,96,768]{2,1,0:T(8,128)(2,1)}, bf16[4,96,768]{2,1,0:T(8,128)(2,1)S(1)}, u32[]{:S(2)}, u32[]{:S(2)}) collective-permute-start(bf16[4,96,768]{2,1,0:T(8,128)(2,1)} %get-tuple-element.227), channel_id=1, source_target_pairs={{0,16},{1,17},{2,18},{3,19},{4,20},{5,21},{6,22},{7,23},{8,24},{9,... | collective-permute-start | bytes 1769480 | tf_op jit(solution)/shard_map/ppermute | solution.py:1207
  789.6 31.2 %collective-permute-start.60 = (bf16[4,96,768]{2,1,0:T(8,128)(2,1)}, bf16[4,96,768]{2,1,0:T(8,128)(2,1)S(1)}, u32[]{:S(2)}, u32[]{:S(2)}) collective-permute-start(bf16[4,96,768]{2,1,0:T(8,128)(2,1)} %copy-done.26), channel_id=1, source_target_pairs={{0,8},{1,9},{2,10},{3,11},{4,12},{5,13},{6,14},{7,15},{8,0},{9,1},... | collective-permute-start | bytes 1769480 | tf_op jit(solution)/shard_map/ppermute | solution.py:1207
  791.7 28.0 %collective-permute-start.54 = (f32[104,768]{1,0:T(8,128)S(1)}, f32[104,768]{1,0:T(8,128)S(1)}, u32[]{:S(2)}, u32[]{:S(2)}) collective-permute-start(f32[104,768]{1,0:T(8,128)S(1)} %fusion.10), channel_id=1, source_target_pairs={{0,16},{1,17},{2,18},{3,19},{4,20},{5,21},{6,22},{7,23},{8,24},{9,... | collective-permute-start | bytes 958472 | tf_op jit(solution)/shard_map/ppermute | solution.py:1207
  825.2 21.9 %collective-permute-start.63 = (bf16[96,768]{1,0:T(8,128)(2,1)S(1)}, bf16[96,768]{1,0:T(8,128)(2,1)S(1)}, u32[]{:S(2)}, u32[]{:S(2)}) collective-permute-start(bf16[96,768]{1,0:T(8,128)(2,1)S(1)} %get-tuple-element.251), channel_id=1, source_target_pairs={{0,4},{1,5},{2,6},{3,7},{4,0},{5,1},{6,2},{7,3},{8,12},{9,13},{10,... | collective-permute-start | bytes 442376 | tf_op jit(solution)/shard_map/ppermute | solution.py:1207
  829.4 23.1 %collective-permute-start.56 = (f32[104,768]{1,0:T(8,128)S(1)}, f32[104,768]{1,0:T(8,128)S(1)}, u32[]{:S(2)}, u32[]{:S(2)}) collective-permute-start(f32[104,768]{1,0:T(8,128)S(1)} %add.554), channel_id=1, source_target_pairs={{0,4},{1,5},{2,6},{3,7},{4,0},{5,1},{6,2},{7,3},{8,12},{9,13},{10,... | collective-permute-start | bytes 958472 | tf_op jit(solution)/shard_map/ppermute | solution.py:1207
  (93 other events, 956.3 us)
Sparse Core Ops, SparseCore 0:
  433.4 164.1 reduce-scatter.1

commit v3 on v2

--- a/solution.py
+++ b/solution.py
@@ -174,11 +174,11 @@
     @pl.when(step == 0)
     def _():
         def norm(row, carry):
-            hat, _ = norm_parts(state_ref[pl.ds(row, 64), :])
-            normed_ref[pl.ds(row, 64), :] = (hat * norm_ref[0:1, :] + norm_ref[1:2, :]).astype(bf16)
+            hat, _ = norm_parts(state_ref[pl.ds(row, 256), :].astype(f32))
+            normed_ref[pl.ds(row, 256), :] = (hat * norm_ref[0:1, :] + norm_ref[1:2, :]).astype(bf16)
             return carry
 
-        loop_rows(length, 64, norm, 0)
+        loop_rows(length, 256, norm, 0)
         val_ref[0:PAD, :] = jnp.zeros((PAD, CB), f32)
 
     biased_ref[:, 0:PAD, :] = jnp.zeros((3, PAD, CB), f32)
@@ -186,7 +186,7 @@
         biased = dot(normed_ref[...], win_ref[stream], NT) + chan_ref[stream : stream + 1, :]
         biased_ref[stream, PAD:, :] = biased
 
-    rows = 32
+    rows = 64
 
     def shorten(row, carry):
         out = []
@@ -270,14 +270,14 @@
     @pl.when(step == pl.num_programs(0) - 1)
     def _():
         def finish(row, carry):
-            here = pl.ds(row, 64)
-            middle = state_ref[here, :] + middle_ref[here, :] + norm_ref[4:5, :]
+            here = pl.ds(row, 256)
+            middle = state_ref[here, :].astype(f32) + middle_ref[here, :] + norm_ref[4:5, :]
             middle_ref[here, :] = middle
             hat, _ = norm_parts(middle)
             second_ref[here, :] = (hat * norm_ref[2:3, :] + norm_ref[3:4, :]).astype(bf16)
             return carry
 
-        loop_rows(length, 64, finish, 0)
+        loop_rows(length, 256, finish, 0)
 
 
 def whole_block(shape):
@@ -362,13 +362,15 @@
 
 
 def load_weights(masks, taken, me_ref, refs, up_ref, down_ref, sems):
-    moves = []
     size, piece = down_ref.shape[0] // len(taken), down_ref.shape[1]
-    for array, own in zip(refs, masks):
-        for slot, mask in enumerate(own):
-            device = slot if mask is None else me_ref[0] ^ mask
-            for part, source in enumerate(taken):
-                start = 3 * piece * source
+    found = []
+    count = 0
+    for part, source in enumerate(taken):
+        moves = []
+        start = 3 * piece * source
+        for array, own in zip(refs, masks):
+            for slot, mask in enumerate(own):
+                device = slot if mask is None else me_ref[0] ^ mask
                 targets = [
                     up_ref.at[2 * (size * part + device)],
                     up_ref.at[2 * (size * part + device) + 1],
@@ -377,11 +379,20 @@
                 for place, target in enumerate(targets):
                     rows = slice(start + place * piece, start + (place + 1) * piece)
                     moves.append(
-                        pltpu.make_async_copy(array.at[slot, rows, :], target, sems.at[len(moves)])
+                        pltpu.make_async_copy(array.at[slot, rows, :], target, sems.at[count])
                     )
-    for move in moves:
-        move.start()
-    return moves
+                    count += 1
+        found.append(moves)
+    return found
+
+
+def wait_weights(step, inner, found):
+    for part, moves in enumerate(found):
+
+        @pl.when(step == part * inner)
+        def _():
+            for move in moves:
+                move.wait()
 
 
 def weight_blocks(up_ref, down_ref, parts, inner, count, step):
@@ -404,9 +415,15 @@
 
         @pl.when(step == 0)
         def _():
-            moves = load_weights(masks, taken, me_ref, refs[: len(masks)], up_ref, down_ref, sems)
-            for move in moves:
-                move.wait()
+            for moves in load_weights(masks, taken, me_ref, refs[: len(masks)], up_ref, down_ref, sems):
+                for move in moves:
+                    move.start()
+
+        wait_weights(
+            step,
+            pl.num_programs(0) // len(taken),
+            load_weights(masks, taken, me_ref, refs[: len(masks)], up_ref, down_ref, sems),
+        )
 
     else:
         up_ref, down_ref, gate_ref, value_ref, out_ref = refs
@@ -504,6 +521,7 @@
     taken,
     block,
     me_ref,
+    glow_ref,
     grad_ref,
     before_ref,
     second_ref,
@@ -515,7 +533,7 @@
 ):
     step = pl.program_id(0)
     steps = pl.num_programs(0)
-    length, width = grad_ref.shape
+    length, width = glow_ref.shape
     rows = 256
     slots = bool(masks)
     if slots:
@@ -523,7 +541,7 @@
     else:
         up_ref, down_ref = refs[:2]
         refs = refs[2:]
-    one_ref, two_ref, out_ref, small_ref, glow_ref, hidden_ref, dgate_ref, dvalue_ref, stage_ref, sems = refs[:10]
+    one_ref, two_ref, out_ref, mlow_ref, small_ref, hidden_ref, dgate_ref, dvalue_ref, stage_ref, sems = refs[:10]
     if slots:
         up_ref, down_ref, load_sems = refs[10:]
     piece = down_ref.shape[1]
@@ -532,68 +550,62 @@
 
     @pl.when(step == 0)
     def _():
-        moves = []
         if slots:
-            moves = load_weights(masks, taken, me_ref, pieces, up_ref, down_ref, load_sems)
-        glow_ref[...] = grad_ref[...].astype(bf16)
+            for moves in load_weights(masks, taken, me_ref, pieces, up_ref, down_ref, load_sems):
+                for move in moves:
+                    move.start()
         if first:
             out_ref[...] = jnp.zeros_like(out_ref)
         else:
             out_ref[...] = before_ref[...]
-        for move in moves:
-            move.wait()
 
     parts = len(taken)
     inner = steps // parts
+    if slots:
+        wait_weights(step, inner, load_weights(masks, taken, me_ref, pieces, up_ref, down_ref, load_sems))
     gate_w, value_w, down_w = weight_blocks(up_ref, down_ref, parts, inner, count, step)
 
-    def copies(at_step, kind, item):
-        source = stage_ref.at[at_step % 2, kind, pl.ds(item * piece, piece), :]
-        half = at_step % inner * count + item
+    def copies(at_step, kind):
+        group = 2 if slots and kind < 2 else 1
+        span = group * piece
+        base = at_step % inner * count // group
         start = at_step // inner * 3 * piece
-        if not slots:
-            if kind == 2:
-                return source, [(None, two_ref.at[half])]
-            return source, [(None, one_ref.at[half + kind * inner * count])]
-        if kind == 2:
-            device = half
-            rows_at = pl.ds(start + 2 * piece, piece)
-        else:
-            device = (half >> 1) + kind * (inner * count >> 1)
-            rows_at = pl.ds(start + (half & 1) * piece, piece)
-        if not own_order:
-            return source, [(None, one_ref.at[device, rows_at, :])]
-        mask = device ^ me_ref[0]
-        place = mask >> 1
-        core = mask & 1
-        return source, [
-            (core == 0, one_ref.at[place, rows_at, :]),
-            (core == 1, two_ref.at[place, rows_at, :]),
-        ]
+        found = []
+        for item in range(count // group):
+            source = stage_ref.at[at_step % 2, kind, item * span : (item + 1) * span, :]
+            sem = sems.at[at_step % 2, kind, item]
+            if not slots:
+                place = base + item + (kind * inner * count if kind < 2 else 0)
+                found.append((source, sem, [(None, (two_ref if kind == 2 else one_ref).at[place])]))
+                continue
+            device = base + item + (kind * inner * count // 2 if kind < 2 else 0)
+            rows_at = pl.ds(start + (2 * piece if kind == 2 else 0), span)
+            if not own_order:
+                found.append((source, sem, [(None, one_ref.at[device, rows_at, :])]))
+                continue
+            mask = device ^ me_ref[0]
+            place = mask >> 1
+            core = mask & 1
+            targets = [
+                (core == 0, one_ref.at[place, rows_at, :]),
+                (core == 1, two_ref.at[place, rows_at, :]),
+            ]
+            found.append((source, sem, targets))
+        return found
 
     def send(kind):
-        def go(item, carry):
-            source, targets = copies(step, kind, item)
+        for source, sem, targets in copies(step, kind):
             for condition, target in targets:
-                move = pltpu.make_async_copy(source, target, sems.at[side, kind, item])
+                move = pltpu.make_async_copy(source, target, sem)
                 if condition is None:
                     move.start()
                 else:
                     pl.when(condition)(move.start)
-            return carry
-
-        lax.fori_loop(0, count, go, 0)
 
     def drain(at_step):
-        def go(item, carry):
-            for kind in range(3):
-                source, targets = copies(at_step, kind, item)
-                pltpu.make_async_copy(
-                    source, targets[0][1], sems.at[at_step % 2, kind, item]
-                ).wait()
-            return carry
-
-        lax.fori_loop(0, count, go, 0)
+        for kind in range(3):
+            for source, sem, targets in copies(at_step, kind):
+                pltpu.make_async_copy(source, targets[0][1], sem).wait()
 
     for row in range(0, length, rows):
         here = slice(row, row + rows)
@@ -627,15 +639,17 @@
     def _():
         if not last:
             small_ref[...] = jnp.zeros_like(small_ref)
+            mlow_ref[...] = jnp.zeros_like(mlow_ref)
         else:
 
             def finish(row, carry):
-                here = pl.ds(row, 32)
+                here = pl.ds(row, 128)
                 grad_out = out_ref[here, :]
-                grad = grad_ref[here, :]
+                grad = grad_ref[here, :].astype(f32)
                 change, gain_rows = norm_backward(middle_ref[here, :], grad_out, norm_ref[2:3, :])
                 total = grad + change
                 out_ref[here, :] = total
+                mlow_ref[here, :] = total.astype(bf16)
                 return (
                     carry[0] + fold(gain_rows),
                     carry[1] + fold(grad_out),
@@ -644,7 +658,7 @@
                 )
 
             zero = jnp.zeros((8, width), f32)
-            sums = loop_rows(length, 32, finish, (zero, zero, zero, zero))
+            sums = loop_rows(length, 128, finish, (zero, zero, zero, zero))
             small_ref[...] = jnp.concatenate(
                 [jnp.sum(part, axis=0, keepdims=True) for part in sums]
                 + [jnp.zeros((4, width), f32)],
@@ -659,7 +673,7 @@
 
 
 def gated_backward(after,
-    me, grad, before, second, middle, norm_pack, gate, value, weights, first, last, own_order, taken=(0,), block=768
+    me, glow, grad, before, second, middle, norm_pack, gate, value, weights, first, last, own_order, taken=(0,), block=768
 ):
     length, width = second.shape
     parts = len(taken)
@@ -692,22 +706,29 @@
         in_specs=[
             pl.BlockSpec(memory_space=pltpu.SMEM),
             fixed_block((length, width)),
+            fixed_block(grad.shape),
             fixed_block(before.shape),
             fixed_block((length, width)),
-            fixed_block((length, width)),
+            fixed_block(middle.shape),
             fixed_block(norm_pack.shape),
             column,
             column,
         ]
         + specs,
-        out_specs=[anywhere, anywhere, whole_block((length, width)), whole_block((8, width))],
+        out_specs=[
+            anywhere,
+            anywhere,
+            whole_block((length, width)),
+            whole_block((length if last else 16, width)),
+            whole_block((8, width)),
+        ],
         out_shape=places
         + [
             jax.ShapeDtypeStruct((length, width), f32),
+            jax.ShapeDtypeStruct((length if last else 16, width), bf16),
             jax.ShapeDtypeStruct((8, width), f32),
         ],
         scratch_shapes=[
-            pltpu.VMEM((length, width), bf16),
             pltpu.VMEM((length, block), bf16),
             pltpu.VMEM((length, block), bf16),
             pltpu.VMEM((length, block), bf16),
@@ -718,15 +739,14 @@
         compiler_params=pltpu.CompilerParams(vmem_limit_bytes=VMEM),
         cost_estimate=cost(12 * length * width * hidden, 20 * 2**20),
         name="gated_backward",
-    )(me, grad, before, second, middle, norm_pack, gate, value, *arrays)
+    )(me, glow, grad, before, second, middle, norm_pack, gate, value, *arrays)
 
 
 def mixer_backward_kernel(
     first,
     last,
     split_ref,
-    grad_ref,
-    before_ref,
+    mlow_ref,
     normed_ref,
     chan_ref,
     biased_ref,
@@ -736,7 +756,6 @@
     fwd_ref,
     inv_ref,
     wout_ref,
-    win_ref,
     kernel_ref,
     inner_t_ref,
     slope_ref,
@@ -748,8 +767,7 @@
     chan_g_ref,
     inner_g_ref,
     freq_g_ref,
-    out_ref,
-    mlow_ref,
+    low_ref,
     kern_g_ref,
     key_ref,
     val_ref,
@@ -758,22 +776,20 @@
     mixed_ref,
     cond_ref,
     dpad_ref,
-    low_ref,
     spec_ref,
     dspec_ref,
     res_ref,
     gram_ref,
 ):
     step = pl.program_id(0)
-    length, width = grad_ref.shape
+    length, width = mlow_ref.shape
     split = split_ref[0]
     boundary = split // BLK
     parts = length // BLK + 1
-    rows = 32
+    rows = 64
 
     @pl.when(step == 0)
     def _():
-        mlow_ref[...] = grad_ref[...].astype(bf16)
         val_ref[0:PAD, :] = jnp.zeros((PAD, CB), f32)
         cond_ref[length:, :] = jnp.zeros((PAD, CB), f32)
         dpad_ref[:, length:, :] = jnp.zeros((3, PAD, CB), f32)
@@ -969,19 +985,6 @@
     wout_g_ref[...] = dot(mixed_ref[...], mlow_ref[...], TN).astype(bf16)
     for stream in range(3):
         win_g_ref[stream] = dot(low_ref[stream], normed_ref[...], TN).astype(bf16)
-    update = sum_terms([dot(low_ref[stream], win_ref[stream], NN) for stream in range(3)])
-
-    @pl.when(step == 0)
-    def _():
-        if first:
-            out_ref[...] = update
-        else:
-            out_ref[...] = before_ref[...] + update
-
-    @pl.when(step > 0)
-    def _():
-        out_ref[...] += update
-
     if not last:
         freq_g_ref[...] = jnp.zeros_like(freq_g_ref)
         return
@@ -991,8 +994,8 @@
         phase_g = inner_g_ref[...] * slope_ref[...]
         freq_g_ref[0 : phase_g.shape[1], :] = dot_fine(features_t_ref[...], phase_g, NN)
         freq_g_ref[phase_g.shape[1] :, :] = fold(phase_g)
-def mixer_backward(after, start, steps, split, grad, before, normed, chan_pack, biased, conv, scale, khat, w_out, w_in, filtered, freq_out, inner_before):
-    length, width = grad.shape
+def mixer_backward(after, start, steps, split, mlow, normed, chan_pack, biased, conv, scale, khat, w_out, filtered, freq_out, inner_before):
+    length, width = mlow.shape
     last = (start + steps) * CB == width
     parts = length // BLK + 1
     forward = jnp.asarray(FORWARD, bf16)
@@ -1010,7 +1013,6 @@
         in_specs=[
             pl.BlockSpec(memory_space=pltpu.SMEM),
             full,
-            fixed_block(before.shape),
             full,
             pl.BlockSpec((16, CB), lambda i: (0, i + start)),
             pl.BlockSpec((3, length + PAD, CB), lambda i: (0, 0, i + start)),
@@ -1020,7 +1022,6 @@
             fixed_block(forward.shape),
             fixed_block(inverse.shape),
             pl.BlockSpec((CB, width), lambda i: (i + start, 0)),
-            pl.BlockSpec((3, CB, width), lambda i: (0, i + start, 0)),
             pl.BlockSpec((length, CB), lambda i: (0, i + start)),
             fixed_block(inner_t.shape),
             fixed_block(slope.shape),
@@ -1034,7 +1035,7 @@
             pl.BlockSpec((16 + hidden, CB), lambda i: (0, i)),
             whole_block((length, hidden)),
             whole_block((hidden + 8, hidden)),
-            whole_block((length, width)),
+            pl.BlockSpec((3, length, CB), lambda i: (0, 0, i)),
         ],
         out_shape=[
             jax.ShapeDtypeStruct((3, steps * CB, width), bf16),
@@ -1042,10 +1043,9 @@
             jax.ShapeDtypeStruct((16 + hidden, steps * CB), f32),
             jax.ShapeDtypeStruct((length, hidden), f32),
             jax.ShapeDtypeStruct((hidden + 8, hidden), f32),
-            jax.ShapeDtypeStruct((length, width), f32),
+            jax.ShapeDtypeStruct((3, length, steps * CB), bf16),
         ],
         scratch_shapes=[
-            pltpu.VMEM((length, width), bf16),
             tall,
             tall,
             tall_pad,
@@ -1054,7 +1054,6 @@
             pltpu.VMEM((length, CB), bf16),
             tall_pad,
             pltpu.VMEM((3, length + PAD, CB), f32),
-            pltpu.VMEM((3, length, CB), bf16),
             spectrum,
             spectrum,
             spectrum,
@@ -1065,8 +1064,7 @@
         name="mixer_backward",
     )(
         split,
-        grad,
-        before,
+        mlow,
         normed,
         chan_pack,
         biased,
@@ -1076,7 +1074,6 @@
         forward,
         inverse,
         w_out,
-        w_in.reshape(3, width, width),
         kernel,
         inner_t,
         slope,
@@ -1086,44 +1083,49 @@
     )
 
 
-def norm_finish_kernel(acc_ref, state_ref, grad_ref, norm_ref, out_ref, small_ref):
-    length, width = state_ref.shape
-
-    def finish(row, carry):
-        here = pl.ds(row, 32)
-        grad_out = acc_ref[here, :]
-        change, gain_rows = norm_backward(state_ref[here, :], grad_out, norm_ref[0:1, :])
-        out_ref[here, :] = grad_ref[here, :] + change
-        return carry[0] + fold(gain_rows), carry[1] + fold(grad_out)
+def norm_finish_kernel(state_ref, grad_ref, norm_ref, win_ref, *refs):
+    *low_refs, out_ref, low_out_ref, small_ref = refs
+    rows, width = state_ref.shape
+    update = None
+    start = 0
+    for low_ref in low_refs:
+        count = low_ref.shape[2]
+        for stream in range(3):
+            term = dot(low_ref[stream], win_ref[stream, start : start + count, :], NN)
+            update = term if update is None else update + term
+        start += count
+    change, gain_rows = norm_backward(state_ref[...].astype(f32), update, norm_ref[0:1, :])
+    total = grad_ref[...] + change
+    out_ref[...] = total
+    low_out_ref[...] = total.astype(bf16)
 
     @pl.when(pl.program_id(0) == 0)
     def _():
         small_ref[...] = jnp.zeros_like(small_ref)
 
-    zero = jnp.zeros((8, width), f32)
-    got = loop_rows(length, 32, finish, (zero, zero))
-    small_ref[...] += jnp.concatenate(
-        [jnp.sum(part, axis=0, keepdims=True) for part in got] + [jnp.zeros((6, width), f32)], axis=0
-    )
-
-
-def norm_finish(after, acc, state, grad, norm_pack, block=256):
+    sums = [jnp.sum(part, axis=0, keepdims=True) for part in (gain_rows, update)]
+    small_ref[...] += jnp.concatenate(sums + [jnp.zeros((6, width), f32)], axis=0)
+
+
+def norm_finish(after, lows, w_in, state, grad, norm_pack, block=256):
     length, width = state.shape
     tile = pl.BlockSpec((block, width), lambda i: (i, 0))
     return call_after(
         after,
         norm_finish_kernel,
         grid=(length // block,),
-        in_specs=[tile, tile, tile, whole_block(norm_pack.shape)],
-        out_specs=[tile, whole_block((8, width))],
+        in_specs=[tile, tile, whole_block(norm_pack.shape), fixed_block((3, width, width))]
+        + [pl.BlockSpec((3, block, low.shape[2]), lambda i: (0, i, 0)) for low in lows],
+        out_specs=[tile, tile, whole_block((8, width))],
         out_shape=[
             jax.ShapeDtypeStruct((length, width), f32),
+            jax.ShapeDtypeStruct((length, width), bf16),
             jax.ShapeDtypeStruct((8, width), f32),
         ],
         compiler_params=pltpu.CompilerParams(vmem_limit_bytes=VMEM),
-        cost_estimate=cost(3e9, 16 * 2**20),
+        cost_estimate=cost(6 * length * width * width, 20 * 2**20),
         name="norm_finish",
-    )(acc, state, grad, norm_pack)
+    )(state, grad, norm_pack, w_in.reshape(3, width, width), *lows)
 
 
 def filter_features(length, count):
@@ -1414,7 +1416,7 @@
     length, width = tokens.shape[1:]
     me = lax.axis_index(AXES)
     split = split_point.astype(jnp.int32)
-    state = tokens[0].astype(f32)
+    state = tokens[0]
     in_rows = in_weight.shape[2]
     out_rows = out_weight.shape[1]
 
@@ -1502,7 +1504,9 @@
         make_filter(layer)
     steps = {}
     if special:
-        steps[0, "mixer"] = gather_mixer(0, ())
+        rows = whole_gather(jnp.concatenate([all_parts(0), mixer_block(0)], axis=0))
+        gated_weights(0, [(rows, (None,) * size)])
+        mixer_weights(0, rows[:, -in_rows - out_rows :])
     else:
         for layer in range(layers):
             mixer_weights(layer, gather_rows(mixer_block(layer), size, me))
@@ -1519,21 +1523,14 @@
         waits = []
         ahead = (layer + 1, "mixer"), (layer + 1, "gated")
         more = special and layer + 1 < layers
-        gated, ahead = (layer, "gated"), (layer + 1, "mixer")
-        if special:
-            if layer == 0:
-                go((0, "mixer"))
-                line = go((0, "mixer"))
-                steps[gated] = gather_gated(0, line)
-                go(gated)
-                clock[:] = go((0, "mixer"))[:1]
-            else:
-                go((layer, "mixer"))
-            waits = go(gated)
-            if more:
-                steps[ahead] = gather_mixer(layer + 1, waits)
-                go(ahead)
-            go((layer, "mixer"))
+        ahead = (layer + 1, "mixer"), (layer + 1, "gated")
+        if more:
+            steps[ahead[0]] = gather_mixer(layer + 1, [filters[layer][0]])
+            go(ahead[0])
+            steps[ahead[1]] = gather_gated(layer + 1, [mixer_w[layer][1]])
+            go(ahead[1])
+            clock[:] = [mixer_w[layer][1]]
+            waits = go(ahead[0])
         w_in, w_out = mixer_w[layer]
         middle, second, normed, biased, conv, scale = mixer_forward(
             waits, split, state, norm_pack, chan_pack, w_in, filters[layer][0], w_out
@@ -1541,13 +1538,13 @@
         waits = ()
         clock[:] = [middle]
         waits = []
-        if special:
-            go(gated)
-            if more:
-                waits = go(ahead)
-                steps[layer + 1, "gated"] = gather_gated(layer + 1, [middle])
-                go((layer + 1, "gated"))
-            go(gated)
+        if more:
+            go(ahead[0])
+            go(ahead[0])
+            waits = go(ahead[1])
+        elif special:
+            go((layer, "gated"))
+            go((layer, "gated"))
         total = middle
         kept = []
         if special:
@@ -1574,7 +1571,7 @@
         outputs.append(total)
         state = total
 
-    gradient = cotangent[0].astype(f32)
+    gradient = glow = cotangent[0]
     big = [None] * layers
     small = [None] * layers
     moving = {}
@@ -1589,6 +1586,7 @@
     def whole_scatter(values):
         return lax.psum_scatter(values, AXES, scatter_dimension=0)
 
+    early = []
     nothing = jnp.zeros((8, width), f32)
     for layer in reversed(range(layers)):
         w_in, w_out = mixer_w[layer]
@@ -1613,19 +1611,21 @@
             else:
                 gate, value = kept[index]
                 own = gated_w[layer][index]
-            one, two, passed, sums_two = gated_backward(
+            final = index == len(calls) - 1
+            one, two, passed, mlow, sums_two = gated_backward(
                 waits,
                 mine,
-                gradient,
+                glow,
+                gradient if final else nothing,
                 passed,
                 second,
-                middle,
+                middle if final else nothing,
                 norm_pack,
                 gate,
                 value,
                 own,
                 index == 0,
-                index == len(calls) - 1,
+                final,
                 by_steps,
                 taken,
             )
@@ -1637,24 +1637,27 @@
                 )
         if special and not by_steps:
             rows = whole_scatter(gated_g[0][0])
+            early.append(rows)
             owned = [rows[part * rows.shape[0] // PARTS :][: rows.shape[0] // PARTS] for part in range(PARTS)]
         grad_middle = passed
-        passed, inner_g = nothing, nothing
+        inner_g = nothing
+        lows = []
         found = []
         splits = [1] * (width // CB) if by_steps else [width // CB]
         start = 0
         for index, count in enumerate(splits):
             waits = []
             if by_steps:
-                names = [("mixer", "part0", "part1"), (), ("part0", "part1")]
+                names = [("part0", "part1"), ("mixer", "part1"), ("part0",)]
                 waits = forward_on(*names[min(index, 2)])
-            *got, inner_g, freq_g, passed = mixer_backward(
+                if index == 1:
+                    waits += early
+            *got, inner_g, freq_g, low = mixer_backward(
                 waits,
                 start,
                 count,
                 split,
-                grad_middle,
-                passed,
+                mlow,
                 normed,
                 chan_pack,
                 biased,
@@ -1662,11 +1665,11 @@
                 scale,
                 filters[layer][0],
                 w_out,
-                w_in,
                 filters[layer][1],
                 freq_out[layer],
                 inner_g,
             )
+            lows.append(low)
             clock[:] = [freq_g]
             found.append(got)
             start += count
@@ -1681,15 +1684,12 @@
         waits = []
         if special:
             order = jnp.arange(size // 2, dtype=jnp.int32) * 2 ^ me
-            if by_steps:
-                forward_on("part0")
-                order = hold(order, *forward_on("part1"))
             keep, send = [
                 mixer_g.at[places].get(mode="promise_in_bounds") for places in (order, order ^ 1)
             ]
             while forward_on("mixer"):
                 pass
-            waits = [send]
+            waits = [send, keep]
             moving["mixer"] = scatter_steps(
                 keep, send, clock, functools.partial(mixer_own.__setitem__, 0)
             )
@@ -1698,7 +1698,9 @@
             down_g = jnp.stack([two for _, two in gated_g], axis=1).reshape(size, -1, width)
             owned = (scatter_rows(up_g, size, me), scatter_rows(down_g, size, me))
             mixer_own[0] = scatter_rows(mixer_g, size, me)
-        gradient, sums_one = norm_finish(waits, passed, state_in, grad_middle, norm_pack)
+        gradient, glow, sums_one = norm_finish(
+            waits, lows, w_in, state_in, grad_middle, norm_pack
+        )
         small[layer] = (chan_g, freq_g, sums_one, sums_two)
         big[layer] = (owned, mixer_own)
 

time: 892 us -> 832 us (0.933)
  Pallas kernels: 467 us -> 404 us
  waiting for transfers between devices: 128 us -> 171 us
  local copies, waits for them, and re-layouts: 93 us -> 75.6 us
    all_gather x0 -> x1, waiting for transfers between devices: none -> 99.6 us  [whole_gather(): return lax.all_gather(hold(block, *after), AXES, axis=0)]
    ppermute x74 -> x54, waiting for transfers between devices: 128 us -> 71.7 us  [swap(): lax.ppermute(values, AXES, [(index, index ^ bit) for index in range(size)])]
    pallas_call x3, Pallas kernels: 144 us -> 117 us  [gated_backward(): call_after(after, functools.partial(gated_backward_kernel, first, last, m...]
    pallas_call x4, Pallas kernels: 134 us -> 117 us  [mixer_backward(): call_after(after, functools.partial(mixer_backward_kernel, start == 0, la...]
    pallas_call x2, Pallas kernels: 80.3 us -> 71.2 us  [mixer_forward(): call_after(after, mixer_forward_kernel, grid=(steps,), in_specs=[pl.Block...]
    ppermute x74 -> x54, starting transfers between devices: 90.1 us -> 81.3 us  [swap(): lax.ppermute(values, AXES, [(index, index ^ bit) for index in range(size)])]
    unnamed x164 -> x151, local copies, waits for them, and re-layouts: 16.9 us -> 19.2 us
  transfers between devices with their start and end apart: 75 -> 56, of which waited for: 16 -> 15; matrix products, arithmetic and copies ran while one was open for 17% -> 15% of each run, Pallas kernels for 42% -> 39%
where the time goes in v3:
time: 832 us; the launch traced here: 825 us
  Pallas kernels  404 us (49%)
  waiting for transfers between devices  171 us (21%)
  starting transfers between devices  81.4 us (10%)
  local copies, waits for them, and re-layouts  75.6 us (9%)
  other arithmetic  60.7 us (7%)
  between operations  24.2 us (3%)
    pallas_call x3, Pallas kernels, gated_backward(): call_after(after, functools.partial(gated_backward_kernel, first, last, m...  117 us
    pallas_call x4, Pallas kernels, mixer_backward(): call_after(after, functools.partial(mixer_backward_kernel, start == 0, la...  117 us
    all_gather x1, waiting for transfers between devices, whole_gather(): return lax.all_gather(hold(block, *after), AXES, axis=0)  99.6 us
    ppermute x54, starting transfers between devices, swap(): lax.ppermute(values, AXES, [(index, index ^ bit) for index in range(size)])  81.3 us
    ppermute x54, waiting for transfers between devices, swap(): lax.ppermute(values, AXES, [(index, index ^ bit) for index in range(size)])  71.7 us
    pallas_call x2, Pallas kernels, mixer_forward(): call_after(after, mixer_forward_kernel, grid=(steps,), in_specs=[pl.Block...  71.2 us
    pallas_call x2, Pallas kernels, gated_forward(): call_after(after, functools.partial(gated_forward_kernel, first, masks, t...  53.7 us
    pallas_call x2, Pallas kernels, norm_finish(): call_after(after, norm_finish_kernel, grid=(length // block,), in_specs=[...  21.3 us
  transfers between devices with their start and end apart: 56, of which 15 were waited for; matrix products, arithmetic and copies ran while one was open for 15% of the time, Pallas kernels for 39%

profile of v3, /device:TPU:0, one launch (start us, length us, event | category | flops | bytes accessed | tf_op | source)
XLA Modules:
  0.0 824.8 jit_solution(8210773630470379176)
XLA Ops:
  12.4 3.7 fusion.36
  16.1 10.1 %filter_forward.2 = (f32[1024,768]{1,0:T(8,128)}, f32[4,512,768]{2,1,0:T(8,128)}) custom-call(f32[1024,64]{1,0:T(8,128)} %get-tuple-element.264.inner_ref, f32[64,768]{1,0:T(8,128)} %get-tuple-element.280.out_ref.refs_19_.refs_22_.refs_18_, f32[16,768]{1,0:T(8,128)} %pad_maximum_fusion.9.chan_ref.refs_4_.refs_7_.refs_10_.refs_6_, ...), custom_call_target="tpu_custom_call" | custom-call | flops 6000000000 | bytes 10485760 | tf_op jit(solution)/shard_map/filter_forward/pallas_call | solution.py:1169
  28.2 5.1 collective-permute-start.5
  34.8 3.7 fusion.37
  38.5 10.1 %filter_forward.3 = (f32[1024,768]{1,0:T(8,128)}, f32[4,512,768]{2,1,0:T(8,128)}) custom-call(f32[1024,64]{1,0:T(8,128)} %get-tuple-element.266.inner_ref, f32[64,768]{1,0:T(8,128)} %get-tuple-element.279.out_ref.refs_15_, f32[16,768]{1,0:T(8,128)} %pad_maximum_fusion.10.chan_ref.refs_3_, bf16[512,768]{1,0:T(8,128)(2,1)} %constant.65.clone.fwd_ref.refs_7_.refs_6_), custom_call_target="tpu_custom_call" | custom-call | flops 6000000000 | bytes 10485760 | tf_op jit(solution)/shard_map/filter_forward/pallas_call | solution.py:1169
  48.7 99.6 %all-gather.3.cloned.1.call-done = bf16[12288,768]{1,0:T(8,128)(2,1)} async-done(((bf16[384,768]{1,0:T(8,128)(2,1)}), bf16[12288,768]{1,0:T(8,128)(2,1)}) %all-gather.3.cloned.1.call-update) | async-done | bytes 18874384 | tf_op jit(solution)/shard_map/all_gather | solution.py:1476
  155.3 4.1 slice.711
  168.3 35.6 %mixer_forward.2 = (f32[1024,768]{1,0:T(8,128)}, bf16[1024,768]{1,0:T(8,128)(2,1)}, bf16[1024,768]{1,0:T(8,128)(2,1)}, f32[3,1032,768]{2,1,0:T(8,128)}, f32[1024,768]{1,0:T(8,128)}, /*index=5*/f32[8,768]{1,0:T(8,128)}) custom-call(bf16[4,96,768]{2,1,0:T(8,128)(2,1)} %copy-done.5, s32[1]{0:T(128)S(6)} %copy.142.refs_1_.refs_0_.refs_4_.refs_7_.refs_3_, ...), custom_call_target="tpu_custom_call" | custom-call | flops 20000000000 | bytes 41943040 | tf_op jit(solution)/shard_map/mixer_forward/pallas_call | solution.py:297
  213.6 26.4 %gated_forward.2 = (bf16[1024,3072]{1,0:T(8,128)(2,1)}, bf16[1024,3072]{1,0:T(8,128)(2,1)}, f32[1024,768]{1,0:T(8,128)}) custom-call(bf16[4,288,768]{2,1,0:T(8,128)(2,1)} %maximum_add_fusion.refs_0_.refs_4_.refs_10_, s32[1]{0:T(128)} %bitcast.55.refs_1_.me_ref.refs_0_.refs_4_, bf16[1024,768]{1,0:T(8,128)(2,1)} %get-tuple-element.81.refs_2_.refs_5_.refs_8_, ...), custom_call_target="tpu_custom_call" | custom-call | flops 14495514624 | bytes 20971520 | tf_op jit(solution)/shard_map/gated_forward/pallas_call | solution.py:480
  241.7 4.3 place_pieces.1
  248.4 4.0 slice.712
  252.4 35.7 %mixer_forward.3 = (f32[1024,768]{1,0:T(8,128)}, bf16[1024,768]{1,0:T(8,128)(2,1)}, bf16[1024,768]{1,0:T(8,128)(2,1)}, f32[3,1032,768]{2,1,0:T(8,128)}, f32[1024,768]{1,0:T(8,128)}, /*index=5*/f32[8,768]{1,0:T(8,128)}) custom-call(s32[1]{0:T(128)S(6)} %copy.142.refs_1_.refs_0_.refs_4_.refs_7_.refs_3_, f32[1024,768]{1,0:T(8,128)} %get-tuple-element.82.refs_1_.refs_2_, ...), custom_call_target="tpu_custom_call" | custom-call | flops 20000000000 | bytes 41943040 | tf_op jit(solution)/shard_map/mixer_forward/pallas_call | solution.py:297
  293.3 5.1 collective-permute-done.17.refs_9_.refs_15_
  299.6 27.3 %gated_forward.3 = (bf16[1024,3072]{1,0:T(8,128)(2,1)}, bf16[1024,3072]{1,0:T(8,128)(2,1)}, f32[1024,768]{1,0:T(8,128)}) custom-call(s32[1]{0:T(128)} %bitcast.55.refs_1_.me_ref.refs_0_.refs_4_, bf16[1024,768]{1,0:T(8,128)(2,1)} %get-tuple-element.84.refs_1_.refs_5_, f32[1024,768]{1,0:T(8,128)} %get-tuple-element.85.refs_1_.refs_2_.refs_6_, ...), custom_call_target="tpu_custom_call" | custom-call | flops 14495514624 | bytes 20971520 | tf_op jit(solution)/shard_map/gated_forward/pallas_call | solution.py:480
  327.5 52.9 %gated_backward.3 = (bf16[32,288,768]{2,1,0:T(8,128)(2,1)}, bf16[16,768]{1,0:T(8,128)(2,1)}, f32[1024,768]{1,0:T(8,128)}, bf16[1024,768]{1,0:T(8,128)(2,1)}, f32[8,768]{1,0:T(8,128)}) custom-call(f32[1024,768]{1,0:T(8,128)} %get-tuple-element.86.refs_0_, s32[1]{0:T(128)} %bitcast.55.refs_1_.me_ref.refs_0_.refs_4_, bf16[1024,768]{1,0:T(8,128)(2,1)} %bitcast.331, ...), custom_call_target="tpu_custom_call" | custom-call | flops 28991029248 | bytes 20971520 | tf_op jit(solution)/shard_map/gated_backward/pallas_call | solution.py:700
  382.3 54.7 %mixer_backward.4 = (bf16[3,768,768]{2,1,0:T(8,128)(2,1)}, bf16[768,768]{1,0:T(8,128)(2,1)}, f32[80,768]{1,0:T(8,128)}, f32[1024,64]{1,0:T(8,128)}, f32[72,64]{1,0:T(8,128)}, /*index=5*/bf16[3,1024,768]{2,1,0:T(8,128)(2,1)}) custom-call(s32[1]{0:T(128)S(6)} %copy.142.refs_1_.refs_0_.refs_4_.refs_7_.refs_3_, bf16[1024,768]{1,0:T(8,128)(2,1)} %get-tuple-element.89.refs_1_, ...), custom_call_target="tpu_custom_call" | custom-call | flops 35999997952 | bytes 44040192 | tf_op jit(solution)/shard_map/mixer_backward/pallas_call | solution.py:1009
  437.1 5.4 pad_maximum_fusion
  442.4 4.5 gather_fusion
  447.3 4.5 gather_fusion.1
  451.8 11.0 %norm_finish.2 = (f32[1024,768]{1,0:T(8,128)}, bf16[1024,768]{1,0:T(8,128)(2,1)}, f32[8,768]{1,0:T(8,128)}) custom-call(bf16[16,96,768]{2,1,0:T(8,128)(2,1)} %gather_fusion, bf16[16,96,768]{2,1,0:T(8,128)(2,1)} %gather_fusion.1, f32[1024,768]{1,0:T(8,128)} %get-tuple-element.82.refs_1_.refs_2_, f32[1024,768]{1,0:T(8,128)} %get-tuple-element.97.refs_3_, ...), custom_call_target="tpu_custom_call" | custom-call | flops 3623878656 | bytes 20971520 | tf_op jit(solution)/shard_map/norm_finish/pallas_call | solution.py:1113
  462.8 29.4 %gated_backward.4 = (bf16[16,144,768]{2,1,0:T(8,128)(2,1)}, bf16[16,144,768]{2,1,0:T(8,128)(2,1)}, f32[1024,768]{1,0:T(8,128)}, bf16[16,768]{1,0:T(8,128)(2,1)}, f32[8,768]{1,0:T(8,128)}) custom-call(bf16[16,96,768]{2,1,0:T(8,128)(2,1)} %gather_fusion, s32[1]{0:T(128)} %bitcast.55.refs_1_.me_ref.refs_0_.refs_4_, ...), custom_call_target="tpu_custom_call" | custom-call | flops 14495514624 | bytes 20971520 | tf_op jit(solution)/shard_map/gated_backward/pallas_call | solution.py:700
  494.6 3.1 add_convert_fusion.9
  497.7 34.6 %gated_backward.5 = (bf16[16,144,768]{2,1,0:T(8,128)(2,1)}, bf16[16,144,768]{2,1,0:T(8,128)(2,1)}, f32[1024,768]{1,0:T(8,128)}, bf16[1024,768]{1,0:T(8,128)(2,1)}, f32[8,768]{1,0:T(8,128)}) custom-call(bf16[4,96,768]{2,1,0:T(8,128)(2,1)} %get-tuple-element.237.refs_0_, bf16[4,96,768]{2,1,0:T(8,128)(2,1)} %get-tuple-element.236.refs_1_, ...), custom_call_target="tpu_custom_call" | custom-call | flops 14495514624 | bytes 20971520 | tf_op jit(solution)/shard_map/gated_backward/pallas_call | solution.py:700
  534.1 6.1 maximum_bitcast_fusion
  545.9 3.7 add_convert_fusion.3
  551.4 20.4 %mixer_backward.5 = (bf16[3,256,768]{2,1,0:T(8,128)(2,1)}, bf16[256,768]{1,0:T(8,128)(2,1)}, f32[80,256]{1,0:T(8,128)}, f32[1024,64]{1,0:T(8,128)}, f32[72,64]{1,0:T(8,128)}, /*index=5*/bf16[3,1024,256]{2,1,0:T(8,128)(2,1)}) custom-call(bf16[4,144,768]{2,1,0:T(8,128)(2,1)} %get-tuple-element.231.refs_0_, bf16[4,144,768]{2,1,0:T(8,128)(2,1)} %get-tuple-element.230.refs_1_, ...), custom_call_target="tpu_custom_call" | custom-call | flops 12000000000 | bytes 14680064 | tf_op jit(solution)/shard_map/mixer_backward/pallas_call | solution.py:1009
  580.8 17.1 %collective-permute-start.43 = (bf16[96,768]{1,0:T(8,128)(2,1)}, bf16[96,768]{1,0:T(8,128)(2,1)}, u32[]{:S(2)}, u32[]{:S(2)}) collective-permute-start(bf16[96,768]{1,0:T(8,128)(2,1)} %get-tuple-element.259.refs_1_), channel_id=1, source_target_pairs={{0,4},{1,5},{2,6},{3,7},{4,0},{5,1},{6,2},{7,3},{8,12},{9,13},{10,... | collective-permute-start | bytes 442376 | tf_op jit(solution)/shard_map/ppermute | solution.py:1209
  597.9 3.7 add_convert_fusion
  601.6 20.3 %mixer_backward.6 = (bf16[3,256,768]{2,1,0:T(8,128)(2,1)}, bf16[256,768]{1,0:T(8,128)(2,1)}, f32[80,256]{1,0:T(8,128)}, f32[1024,64]{1,0:T(8,128)}, f32[72,64]{1,0:T(8,128)}, /*index=5*/bf16[3,1024,256]{2,1,0:T(8,128)(2,1)}) custom-call(bf16[96,768]{1,0:T(8,128)(2,1)} %get-tuple-element.260.refs_0_, bf16[96,768]{1,0:T(8,128)(2,1)} %get-tuple-element.259.refs_1_, ...), custom_call_target="tpu_custom_call" | custom-call | flops 12000000000 | bytes 14680064 | tf_op jit(solution)/shard_map/mixer_backward/pallas_call | solution.py:1009
  625.3 4.0 fusion.31
  630.2 21.1 %mixer_backward.7 = (bf16[3,256,768]{2,1,0:T(8,128)(2,1)}, bf16[256,768]{1,0:T(8,128)(2,1)}, f32[80,256]{1,0:T(8,128)}, f32[1024,64]{1,0:T(8,128)}, f32[72,64]{1,0:T(8,128)}, /*index=5*/bf16[3,1024,256]{2,1,0:T(8,128)(2,1)}) custom-call(bf16[144,768]{1,0:T(8,128)(2,1)} %get-tuple-element.243.refs_0_, bf16[144,768]{1,0:T(8,128)(2,1)} %get-tuple-element.242.refs_1_, ...), custom_call_target="tpu_custom_call" | custom-call | flops 12000000000 | bytes 14680064 | tf_op jit(solution)/shard_map/mixer_backward/pallas_call | solution.py:1009
  653.1 2.8 pad_maximum_fusion.1
  655.9 4.4 gather_fusion.3
  660.3 4.5 gather_fusion.2
  665.8 10.3 %norm_finish.3 = (f32[1024,768]{1,0:T(8,128)}, bf16[1024,768]{1,0:T(8,128)(2,1)}, f32[8,768]{1,0:T(8,128)}) custom-call(bf16[16,96,768]{2,1,0:T(8,128)(2,1)} %gather_fusion.2, bf16[16,96,768]{2,1,0:T(8,128)(2,1)} %gather_fusion.3, bf16[1024,768]{1,0:T(8,128)(2,1)} %bitcast.303, f32[1024,768]{1,0:T(8,128)} %get-tuple-element.127.refs_3_, ...), custom_call_target="tpu_custom_call" | custom-call | flops 3623878656 | bytes 20971520 | tf_op jit(solution)/shard_map/norm_finish/pallas_call | solution.py:1113
  696.3 5.0 collective-permute-start.46
  701.3 3.0 add_convert_fusion.8
  708.5 19.3 %collective-permute-done.48 = bf16[4,144,768]{2,1,0:T(8,128)(2,1)} collective-permute-done((bf16[4,144,768]{2,1,0:T(8,128)(2,1)}, bf16[4,144,768]{2,1,0:T(8,128)(2,1)}, u32[]{:S(2)}, u32[]{:S(2)}) %collective-permute-start.48) | collective-permute-done | bytes 884768 | tf_op jit(solution)/shard_map/ppermute | solution.py:1209
  729.2 4.0 fusion.29
  738.6 6.3 collective-permute-start.51
  751.6 7.0 collective-permute-done.53
  759.5 5.7 collective-permute-done.52
  772.6 3.3 collective-permute-start.41
  776.1 3.0 collective-permute-start.33
  779.9 4.0 collective-permute-done.41
  783.9 9.9 %collective-permute-done.40 = bf16[96,768]{1,0:T(8,128)(2,1)S(1)} collective-permute-done((bf16[96,768]{1,0:T(8,128)(2,1)S(1)}, bf16[96,768]{1,0:T(8,128)(2,1)S(1)}, u32[]{:S(2)}, u32[]{:S(2)}) %collective-permute-start.40) | collective-permute-done | bytes 147488 | tf_op jit(solution)/shard_map/ppermute | solution.py:1209
  793.8 5.9 collective-permute-done.33
  800.5 8.0 collective-permute-done.34
  (360 shorter events, 122.9 us)
Async XLA Ops:
  7.3 140.9 %all-gather.3.cloned.1.call-start = ((), (), s32[]{:S(2)}) async-start(), calls=%async_computation.2 | async-start | bytes 19464192 | tf_op jit(solution)/shard_map/all_gather | solution.py:1476
  10.5 591.1 %reduce-scatter.2.cloned.1.call-start = ((), (), s32[]{:S(2)}) async-start(), calls=%async_computation.1 | async-start | bytes 14598144 | tf_op jit(solution)/shard_map/reduce_scatter | solution.py:1587
  28.2 131.2 %collective-permute-start.5 = (bf16[96,768]{1,0:T(8,128)(2,1)S(1)}, bf16[96,768]{1,0:T(8,128)(2,1)}, u32[]{:S(2)}, u32[]{:S(2)}) collective-permute-start(bf16[96,768]{1,0:T(8,128)(2,1)S(1)} %maximum_add_fusion.3), channel_id=1, source_target_pairs={{0,6},{1,7},{2,4},{3,5},{4,2},{5,3},{6,0},{7,1},{8,14},{9,15},{10,... | collective-permute-start | bytes 442376 | tf_op jit(solution)/shard_map/ppermute | solution.py:1209
  33.3 128.9 %collective-permute-start.4 = (bf16[96,768]{1,0:T(8,128)(2,1)S(1)}, bf16[96,768]{1,0:T(8,128)(2,1)}, u32[]{:S(2)}, u32[]{:S(2)}) collective-permute-start(bf16[96,768]{1,0:T(8,128)(2,1)S(1)} %maximum_add_fusion.3), channel_id=1, source_target_pairs={{0,4},{1,5},{2,6},{3,7},{4,0},{5,1},{6,2},{7,3},{8,12},{9,13},{10,... | collective-permute-start | bytes 442376 | tf_op jit(solution)/shard_map/ppermute | solution.py:1209
  33.3 128.9 %collective-permute-start.3 = (bf16[96,768]{1,0:T(8,128)(2,1)S(1)}, bf16[96,768]{1,0:T(8,128)(2,1)}, u32[]{:S(2)}, u32[]{:S(2)}) collective-permute-start(bf16[96,768]{1,0:T(8,128)(2,1)S(1)} %maximum_add_fusion.3), channel_id=1, source_target_pairs={{0,2},{1,3},{2,0},{3,1},{4,6},{5,7},{6,4},{7,5},{8,10},{9,11},{10,... | collective-permute-start | bytes 442376 | tf_op jit(solution)/shard_map/ppermute | solution.py:1209
  151.6 15.3 %collective-permute-start.2 = (bf16[288,768]{1,0:T(8,128)(2,1)}, bf16[288,768]{1,0:T(8,128)(2,1)}, u32[]{:S(2)}, u32[]{:S(2)}) collective-permute-start(bf16[288,768]{1,0:T(8,128)(2,1)} %broadcast_add_fusion.1), channel_id=1, source_target_pairs={{0,6},{1,7},{2,4},{3,5},{4,2},{5,3},{6,0},{7,1},{8,14},{9,15},{10,... | collective-permute-start | bytes 1327112 | tf_op jit(solution)/shard_map/ppermute | solution.py:1209
  155.0 50.7 %collective-permute-start.1 = (bf16[288,768]{1,0:T(8,128)(2,1)}, bf16[288,768]{1,0:T(8,128)(2,1)}, u32[]{:S(2)}, u32[]{:S(2)}) collective-permute-start(bf16[288,768]{1,0:T(8,128)(2,1)} %broadcast_add_fusion.1), channel_id=1, source_target_pairs={{0,4},{1,5},{2,6},{3,7},{4,0},{5,1},{6,2},{7,3},{8,12},{9,13},{10,... | collective-permute-start | bytes 1327112 | tf_op jit(solution)/shard_map/ppermute | solution.py:1209
  159.4 46.5 %collective-permute-start = (bf16[288,768]{1,0:T(8,128)(2,1)}, bf16[288,768]{1,0:T(8,128)(2,1)S(1)}, u32[]{:S(2)}, u32[]{:S(2)}) collective-permute-start(bf16[288,768]{1,0:T(8,128)(2,1)} %broadcast_add_fusion.1), channel_id=1, source_target_pairs={{0,2},{1,3},{2,0},{3,1},{4,6},{5,7},{6,4},{7,5},{8,10},{9,11},{10,... | collective-permute-start | bytes 1327112 | tf_op jit(solution)/shard_map/ppermute | solution.py:1209
  163.3 49.3 %collective-permute-start.11 = (bf16[4,96,768]{2,1,0:T(8,128)(2,1)S(1)}, bf16[4,96,768]{2,1,0:T(8,128)(2,1)S(1)}, u32[]{:S(2)}, u32[]{:S(2)}) collective-permute-start(bf16[4,96,768]{2,1,0:T(8,128)(2,1)S(1)} %maximum_add_fusion.1.refs_0_), channel_id=1, source_target_pairs={{0,24},{1,25},{2,26},{3,27},{4,28},{5,29},{6,30},{7,31},{8,16},{9,... | collective-permute-start | bytes 1769480 | tf_op jit(solution)/shard_map/ppermute | solution.py:1209
  164.8 46.6 %collective-permute-start.9 = (bf16[4,96,768]{2,1,0:T(8,128)(2,1)S(1)}, bf16[4,96,768]{2,1,0:T(8,128)(2,1)S(1)}, u32[]{:S(2)}, u32[]{:S(2)}) collective-permute-start(bf16[4,96,768]{2,1,0:T(8,128)(2,1)S(1)} %maximum_add_fusion.1.refs_0_), channel_id=1, source_target_pairs={{0,16},{1,17},{2,18},{3,19},{4,20},{5,21},{6,22},{7,23},{8,24},{9,... | collective-permute-start | bytes 1769480 | tf_op jit(solution)/shard_map/ppermute | solution.py:1209
  166.8 43.5 %collective-permute-start.7 = (bf16[4,96,768]{2,1,0:T(8,128)(2,1)S(1)}, bf16[4,96,768]{2,1,0:T(8,128)(2,1)S(1)}, u32[]{:S(2)}, u32[]{:S(2)}) collective-permute-start(bf16[4,96,768]{2,1,0:T(8,128)(2,1)S(1)} %maximum_add_fusion.1.refs_0_), channel_id=1, source_target_pairs={{0,8},{1,9},{2,10},{3,11},{4,12},{5,13},{6,14},{7,15},{8,0},{9,1},... | collective-permute-start | bytes 1769480 | tf_op jit(solution)/shard_map/ppermute | solution.py:1209
  205.8 34.2 %collective-permute-start.6 = (bf16[4,96,768]{2,1,0:T(8,128)(2,1)}, bf16[4,96,768]{2,1,0:T(8,128)(2,1)S(1)}, u32[]{:S(2)}, u32[]{:S(2)}) collective-permute-start(bf16[4,96,768]{2,1,0:T(8,128)(2,1)} %copy-done.5), channel_id=1, source_target_pairs={{0,1},{1,0},{2,3},{3,2},{4,5},{5,4},{6,7},{7,6},{8,9},{9,8},{10,11... | collective-permute-start | bytes 1769480 | tf_op jit(solution)/shard_map/ppermute | solution.py:1209
  208.4 82.7 %collective-permute-start.18 = (bf16[4,288,768]{2,1,0:T(8,128)(2,1)}, bf16[4,288,768]{2,1,0:T(8,128)(2,1)}, u32[]{:S(2)}, u32[]{:S(2)}) collective-permute-start(bf16[4,288,768]{2,1,0:T(8,128)(2,1)} %maximum_add_fusion.refs_0_.refs_4_.refs_10_), channel_id=1, source_target_pairs={{0,24},{1,25},{2,26},{3,27},{4,28},{5,29},{6,30},{7,31},{8,16},{9,... | collective-permute-start | bytes 5308424 | tf_op jit(solution)/shard_map/ppermute | solution.py:1209
  211.2 29.6 %collective-permute-start.8 = (bf16[4,96,768]{2,1,0:T(8,128)(2,1)}, bf16[4,96,768]{2,1,0:T(8,128)(2,1)}, u32[]{:S(2)}, u32[]{:S(2)}) collective-permute-start(bf16[4,96,768]{2,1,0:T(8,128)(2,1)} %hold_place.6.refs_2_), channel_id=1, source_target_pairs={{0,1},{1,0},{2,3},{3,2},{4,5},{5,4},{6,7},{7,6},{8,9},{9,8},{10,11... | collective-permute-start | bytes 1769480 | tf_op jit(solution)/shard_map/ppermute | solution.py:1209
  212.3 29.4 %collective-permute-start.10 = (bf16[4,96,768]{2,1,0:T(8,128)(2,1)}, bf16[4,96,768]{2,1,0:T(8,128)(2,1)}, u32[]{:S(2)}, u32[]{:S(2)}) collective-permute-start(bf16[4,96,768]{2,1,0:T(8,128)(2,1)} %hold_place.7.refs_4_), channel_id=1, source_target_pairs={{0,1},{1,0},{2,3},{3,2},{4,5},{5,4},{6,7},{7,6},{8,9},{9,8},{10,11... | collective-permute-start | bytes 1769480 | tf_op jit(solution)/shard_map/ppermute | solution.py:1209
  213.4 28.3 %collective-permute-start.12 = (bf16[4,96,768]{2,1,0:T(8,128)(2,1)}, bf16[4,96,768]{2,1,0:T(8,128)(2,1)}, u32[]{:S(2)}, u32[]{:S(2)}) collective-permute-start(bf16[4,96,768]{2,1,0:T(8,128)(2,1)} %hold_place.8.refs_6_), channel_id=1, source_target_pairs={{0,1},{1,0},{2,3},{3,2},{4,5},{5,4},{6,7},{7,6},{8,9},{9,8},{10,11... | collective-permute-start | bytes 1769480 | tf_op jit(solution)/shard_map/ppermute | solution.py:1209
  240.0 49.8 %collective-permute-start.16 = (bf16[4,288,768]{2,1,0:T(8,128)(2,1)}, bf16[4,288,768]{2,1,0:T(8,128)(2,1)S(1)}, u32[]{:S(2)}, u32[]{:S(2)}) collective-permute-start(bf16[4,288,768]{2,1,0:T(8,128)(2,1)} %maximum_add_fusion.refs_0_.refs_4_.refs_10_), channel_id=1, source_target_pairs={{0,16},{1,17},{2,18},{3,19},{4,20},{5,21},{6,22},{7,23},{8,24},{9,... | collective-permute-start | bytes 5308424 | tf_op jit(solution)/shard_map/ppermute | solution.py:1209
  240.8 47.3 %collective-permute-start.14 = (bf16[4,288,768]{2,1,0:T(8,128)(2,1)}, bf16[4,288,768]{2,1,0:T(8,128)(2,1)S(1)}, u32[]{:S(2)}, u32[]{:S(2)}) collective-permute-start(bf16[4,288,768]{2,1,0:T(8,128)(2,1)} %maximum_add_fusion.refs_0_.refs_4_.refs_10_), channel_id=1, source_target_pairs={{0,8},{1,9},{2,10},{3,11},{4,12},{5,13},{6,14},{7,15},{8,0},{9,1},... | collective-permute-start | bytes 5308424 | tf_op jit(solution)/shard_map/ppermute | solution.py:1209
  241.7 50.0 %collective-permute-start.13 = (bf16[4,288,768]{2,1,0:T(8,128)(2,1)}, bf16[4,288,768]{2,1,0:T(8,128)(2,1)}, u32[]{:S(2)}, u32[]{:S(2)}) collective-permute-start(bf16[4,288,768]{2,1,0:T(8,128)(2,1)} %maximum_add_fusion.refs_0_.refs_4_.refs_10_), channel_id=1, source_target_pairs={{0,1},{1,0},{2,3},{3,2},{4,5},{5,4},{6,7},{7,6},{8,9},{9,8},{10,11... | collective-permute-start | bytes 5308424 | tf_op jit(solution)/shard_map/ppermute | solution.py:1209
  446.9 47.6 %collective-permute-start.21 = (bf16[16,96,768]{2,1,0:T(8,128)(2,1)}, bf16[16,96,768]{2,1,0:T(8,128)(2,1)}, u32[]{:S(2)}, u32[]{:S(2)}) collective-permute-start(bf16[16,96,768]{2,1,0:T(8,128)(2,1)} %gather_fusion), channel_id=1, source_target_pairs={{0,1},{1,0},{2,3},{3,2},{4,5},{5,4},{6,7},{7,6},{8,9},{9,8},{10,11... | collective-permute-start | bytes 7077896 | tf_op jit(solution)/shard_map/ppermute | solution.py:1209
  492.3 53.6 %collective-permute-start.20 = (bf16[16,144,768]{2,1,0:T(8,128)(2,1)}, bf16[16,144,768]{2,1,0:T(8,128)(2,1)}, u32[]{:S(2)}, u32[]{:S(2)}) collective-permute-start(bf16[16,144,768]{2,1,0:T(8,128)(2,1)} %get-tuple-element.103.refs_3_), channel_id=1, source_target_pairs={{0,1},{1,0},{2,3},{3,2},{4,5},{5,4},{6,7},{7,6},{8,9},{9,8},{10,11... | collective-permute-start | bytes 10616840 | tf_op jit(solution)/shard_map/ppermute | solution.py:1209
  532.3 48.5 %collective-permute-start.25 = (bf16[16,144,768]{2,1,0:T(8,128)(2,1)}, bf16[16,144,768]{2,1,0:T(8,128)(2,1)}, u32[]{:S(2)}, u32[]{:S(2)}) collective-permute-start(bf16[16,144,768]{2,1,0:T(8,128)(2,1)} %get-tuple-element.108.refs_3_), channel_id=1, source_target_pairs={{0,1},{1,0},{2,3},{3,2},{4,5},{5,4},{6,7},{7,6},{8,9},{9,8},{10,11... | collective-permute-start | bytes 10616840 | tf_op jit(solution)/shard_map/ppermute | solution.py:1209
  540.2 33.4 %collective-permute-start.24 = (bf16[4,96,768]{2,1,0:T(8,128)(2,1)}, bf16[4,96,768]{2,1,0:T(8,128)(2,1)S(1)}, u32[]{:S(2)}, u32[]{:S(2)}) collective-permute-start(bf16[4,96,768]{2,1,0:T(8,128)(2,1)} %get-tuple-element.235.refs_2_), channel_id=1, source_target_pairs={{0,16},{1,17},{2,18},{3,19},{4,20},{5,21},{6,22},{7,23},{8,24},{9,... | collective-permute-start | bytes 1769480 | tf_op jit(solution)/shard_map/ppermute | solution.py:1209
  542.3 33.5 %collective-permute-start.23 = (bf16[4,96,768]{2,1,0:T(8,128)(2,1)}, bf16[4,96,768]{2,1,0:T(8,128)(2,1)S(1)}, u32[]{:S(2)}, u32[]{:S(2)}) collective-permute-start(bf16[4,96,768]{2,1,0:T(8,128)(2,1)} %get-tuple-element.236.refs_1_), channel_id=1, source_target_pairs={{0,8},{1,9},{2,10},{3,11},{4,12},{5,13},{6,14},{7,15},{8,0},{9,1},... | collective-permute-start | bytes 1769480 | tf_op jit(solution)/shard_map/ppermute | solution.py:1209
  544.0 31.7 %collective-permute-start.22 = (bf16[4,96,768]{2,1,0:T(8,128)(2,1)}, bf16[4,96,768]{2,1,0:T(8,128)(2,1)}, u32[]{:S(2)}, u32[]{:S(2)}) collective-permute-start(bf16[4,96,768]{2,1,0:T(8,128)(2,1)} %get-tuple-element.237.refs_0_), channel_id=1, source_target_pairs={{0,24},{1,25},{2,26},{3,27},{4,28},{5,29},{6,30},{7,31},{8,16},{9,... | collective-permute-start | bytes 1769480 | tf_op jit(solution)/shard_map/ppermute | solution.py:1209
  549.6 74.2 %collective-permute-start.28 = (bf16[4,144,768]{2,1,0:T(8,128)(2,1)}, bf16[4,144,768]{2,1,0:T(8,128)(2,1)}, u32[]{:S(2)}, u32[]{:S(2)}) collective-permute-start(bf16[4,144,768]{2,1,0:T(8,128)(2,1)} %get-tuple-element.229.refs_2_), channel_id=1, source_target_pairs={{0,16},{1,17},{2,18},{3,19},{4,20},{5,21},{6,22},{7,23},{8,24},{9,... | collective-permute-start | bytes 2654216 | tf_op jit(solution)/shard_map/ppermute | solution.py:1209
  573.6 51.0 %collective-permute-start.27 = (bf16[4,144,768]{2,1,0:T(8,128)(2,1)}, bf16[4,144,768]{2,1,0:T(8,128)(2,1)}, u32[]{:S(2)}, u32[]{:S(2)}) collective-permute-start(bf16[4,144,768]{2,1,0:T(8,128)(2,1)} %get-tuple-element.230.refs_1_), channel_id=1, source_target_pairs={{0,8},{1,9},{2,10},{3,11},{4,12},{5,13},{6,14},{7,15},{8,0},{9,1},... | collective-permute-start | bytes 2654216 | tf_op jit(solution)/shard_map/ppermute | solution.py:1209
  575.7 49.6 %collective-permute-start.26 = (bf16[4,144,768]{2,1,0:T(8,128)(2,1)}, bf16[4,144,768]{2,1,0:T(8,128)(2,1)}, u32[]{:S(2)}, u32[]{:S(2)}) collective-permute-start(bf16[4,144,768]{2,1,0:T(8,128)(2,1)} %get-tuple-element.231.refs_0_), channel_id=1, source_target_pairs={{0,24},{1,25},{2,26},{3,27},{4,28},{5,29},{6,30},{7,31},{8,16},{9,... | collective-permute-start | bytes 2654216 | tf_op jit(solution)/shard_map/ppermute | solution.py:1209
  579.5 106.3 %collective-permute-start.44 = (bf16[96,768]{1,0:T(8,128)(2,1)}, bf16[96,768]{1,0:T(8,128)(2,1)S(1)}, u32[]{:S(2)}, u32[]{:S(2)}) collective-permute-start(bf16[96,768]{1,0:T(8,128)(2,1)} %get-tuple-element.258.refs_2_), channel_id=1, source_target_pairs={{0,6},{1,7},{2,4},{3,5},{4,2},{5,3},{6,0},{7,1},{8,14},{9,15},{10,... | collective-permute-start | bytes 442376 | tf_op jit(solution)/shard_map/ppermute | solution.py:1209
  580.8 106.2 %collective-permute-start.43 = (bf16[96,768]{1,0:T(8,128)(2,1)}, bf16[96,768]{1,0:T(8,128)(2,1)}, u32[]{:S(2)}, u32[]{:S(2)}) collective-permute-start(bf16[96,768]{1,0:T(8,128)(2,1)} %get-tuple-element.259.refs_1_), channel_id=1, source_target_pairs={{0,4},{1,5},{2,6},{3,7},{4,0},{5,1},{6,2},{7,3},{8,12},{9,13},{10,... | collective-permute-start | bytes 442376 | tf_op jit(solution)/shard_map/ppermute | solution.py:1209
  623.8 64.7 %collective-permute-start.42 = (bf16[96,768]{1,0:T(8,128)(2,1)}, bf16[96,768]{1,0:T(8,128)(2,1)}, u32[]{:S(2)}, u32[]{:S(2)}) collective-permute-start(bf16[96,768]{1,0:T(8,128)(2,1)} %get-tuple-element.260.refs_0_), channel_id=1, source_target_pairs={{0,2},{1,3},{2,0},{3,1},{4,6},{5,7},{6,4},{7,5},{8,10},{9,11},{10,... | collective-permute-start | bytes 442376 | tf_op jit(solution)/shard_map/ppermute | solution.py:1209
  624.6 81.5 %collective-permute-start.50 = (bf16[4,144,768]{2,1,0:T(8,128)(2,1)}, bf16[4,144,768]{2,1,0:T(8,128)(2,1)}, u32[]{:S(2)}, u32[]{:S(2)}) collective-permute-start(bf16[4,144,768]{2,1,0:T(8,128)(2,1)} %get-tuple-element.226.refs_5_), channel_id=1, source_target_pairs={{0,16},{1,17},{2,18},{3,19},{4,20},{5,21},{6,22},{7,23},{8,24},{9,... | collective-permute-start | bytes 2654216 | tf_op jit(solution)/shard_map/ppermute | solution.py:1209
  664.9 31.4 %collective-permute-start.30 = (bf16[16,96,768]{2,1,0:T(8,128)(2,1)}, bf16[16,96,768]{2,1,0:T(8,128)(2,1)}, u32[]{:S(2)}, u32[]{:S(2)}) collective-permute-start(bf16[16,96,768]{2,1,0:T(8,128)(2,1)} %gather_fusion.2), channel_id=1, source_target_pairs={{0,1},{1,0},{2,3},{3,2},{4,5},{5,4},{6,7},{7,6},{8,9},{9,8},{10,11... | collective-permute-start | bytes 7077896 | tf_op jit(solution)/shard_map/ppermute | solution.py:1209
  685.8 22.8 %collective-permute-start.49 = (bf16[4,144,768]{2,1,0:T(8,128)(2,1)}, bf16[4,144,768]{2,1,0:T(8,128)(2,1)}, u32[]{:S(2)}, u32[]{:S(2)}) collective-permute-start(bf16[4,144,768]{2,1,0:T(8,128)(2,1)} %get-tuple-element.227.refs_4_), channel_id=1, source_target_pairs={{0,8},{1,9},{2,10},{3,11},{4,12},{5,13},{6,14},{7,15},{8,0},{9,1},... | collective-permute-start | bytes 2654216 | tf_op jit(solution)/shard_map/ppermute | solution.py:1209
  687.0 40.8 %collective-permute-start.48 = (bf16[4,144,768]{2,1,0:T(8,128)(2,1)}, bf16[4,144,768]{2,1,0:T(8,128)(2,1)}, u32[]{:S(2)}, u32[]{:S(2)}) collective-permute-start(bf16[4,144,768]{2,1,0:T(8,128)(2,1)} %get-tuple-element.228.refs_3_), channel_id=1, source_target_pairs={{0,24},{1,25},{2,26},{3,27},{4,28},{5,29},{6,30},{7,31},{8,16},{9,... | collective-permute-start | bytes 2654216 | tf_op jit(solution)/shard_map/ppermute | solution.py:1209
  688.5 50.0 %collective-permute-start.47 = (bf16[144,768]{1,0:T(8,128)(2,1)}, bf16[144,768]{1,0:T(8,128)(2,1)}, u32[]{:S(2)}, u32[]{:S(2)}) collective-permute-start(bf16[144,768]{1,0:T(8,128)(2,1)} %get-tuple-element.241.refs_2_), channel_id=1, source_target_pairs={{0,6},{1,7},{2,4},{3,5},{4,2},{5,3},{6,0},{7,1},{8,14},{9,15},{10,... | collective-permute-start | bytes 663560 | tf_op jit(solution)/shard_map/ppermute | solution.py:1209
  696.3 48.6 %collective-permute-start.46 = (bf16[144,768]{1,0:T(8,128)(2,1)}, bf16[144,768]{1,0:T(8,128)(2,1)}, u32[]{:S(2)}, u32[]{:S(2)}) collective-permute-start(bf16[144,768]{1,0:T(8,128)(2,1)} %get-tuple-element.242.refs_1_), channel_id=1, source_target_pairs={{0,4},{1,5},{2,6},{3,7},{4,0},{5,1},{6,2},{7,3},{8,12},{9,13},{10,... | collective-permute-start | bytes 663560 | tf_op jit(solution)/shard_map/ppermute | solution.py:1209
  706.2 41.2 %collective-permute-start.45 = (bf16[144,768]{1,0:T(8,128)(2,1)}, bf16[144,768]{1,0:T(8,128)(2,1)}, u32[]{:S(2)}, u32[]{:S(2)}) collective-permute-start(bf16[144,768]{1,0:T(8,128)(2,1)} %get-tuple-element.243.refs_0_), channel_id=1, source_target_pairs={{0,2},{1,3},{2,0},{3,1},{4,6},{5,7},{6,4},{7,5},{8,10},{9,11},{10,... | collective-permute-start | bytes 663560 | tf_op jit(solution)/shard_map/ppermute | solution.py:1209
  708.5 28.4 %collective-permute-start.29 = (f32[104,768]{1,0:T(8,128)}, f32[104,768]{1,0:T(8,128)}, u32[]{:S(2)}, u32[]{:S(2)}) collective-permute-start(f32[104,768]{1,0:T(8,128)} %dynamic-slice_bitcast_fusion), channel_id=1, source_target_pairs={{0,1},{1,0},{2,3},{3,2},{4,5},{5,4},{6,7},{7,6},{8,9},{9,8},{10,11... | collective-permute-start | bytes 958472 | tf_op jit(solution)/shard_map/ppermute | solution.py:1209
  727.8 41.4 %collective-permute-start.36 = (bf16[4,96,768]{2,1,0:T(8,128)(2,1)}, bf16[4,96,768]{2,1,0:T(8,128)(2,1)}, u32[]{:S(2)}, u32[]{:S(2)}) collective-permute-start(bf16[4,96,768]{2,1,0:T(8,128)(2,1)} %get-tuple-element.232), channel_id=1, source_target_pairs={{0,24},{1,25},{2,26},{3,27},{4,28},{5,29},{6,30},{7,31},{8,16},{9,... | collective-permute-start | bytes 1769480 | tf_op jit(solution)/shard_map/ppermute | solution.py:1209
  737.0 32.2 %collective-permute-start.38 = (bf16[4,96,768]{2,1,0:T(8,128)(2,1)}, bf16[4,96,768]{2,1,0:T(8,128)(2,1)S(1)}, u32[]{:S(2)}, u32[]{:S(2)}) collective-permute-start(bf16[4,96,768]{2,1,0:T(8,128)(2,1)} %get-tuple-element.233), channel_id=1, source_target_pairs={{0,16},{1,17},{2,18},{3,19},{4,20},{5,21},{6,22},{7,23},{8,24},{9,... | collective-permute-start | bytes 1769480 | tf_op jit(solution)/shard_map/ppermute | solution.py:1209
  738.6 12.2 %collective-permute-start.51 = (bf16[144,768]{1,0:T(8,128)(2,1)S(1)}, bf16[144,768]{1,0:T(8,128)(2,1)S(1)}, u32[]{:S(2)}, u32[]{:S(2)}) collective-permute-start(bf16[144,768]{1,0:T(8,128)(2,1)S(1)} %get-tuple-element.238), channel_id=1, source_target_pairs={{0,2},{1,3},{2,0},{3,1},{4,6},{5,7},{6,4},{7,5},{8,10},{9,11},{10,... | collective-permute-start | bytes 663560 | tf_op jit(solution)/shard_map/ppermute | solution.py:1209
  744.9 13.7 %collective-permute-start.53 = (bf16[144,768]{1,0:T(8,128)(2,1)S(1)}, bf16[144,768]{1,0:T(8,128)(2,1)S(1)}, u32[]{:S(2)}, u32[]{:S(2)}) collective-permute-start(bf16[144,768]{1,0:T(8,128)(2,1)S(1)} %get-tuple-element.239), channel_id=1, source_target_pairs={{0,6},{1,7},{2,4},{3,5},{4,2},{5,3},{6,0},{7,1},{8,14},{9,15},{10,... | collective-permute-start | bytes 663560 | tf_op jit(solution)/shard_map/ppermute | solution.py:1209
  747.4 17.8 %collective-permute-start.52 = (bf16[144,768]{1,0:T(8,128)(2,1)S(1)}, bf16[144,768]{1,0:T(8,128)(2,1)S(1)}, u32[]{:S(2)}, u32[]{:S(2)}) collective-permute-start(bf16[144,768]{1,0:T(8,128)(2,1)S(1)} %get-tuple-element.240), channel_id=1, source_target_pairs={{0,4},{1,5},{2,6},{3,7},{4,0},{5,1},{6,2},{7,3},{8,12},{9,13},{10,... | collective-permute-start | bytes 663560 | tf_op jit(solution)/shard_map/ppermute | solution.py:1209
  750.8 18.4 %collective-permute-start.37 = (bf16[4,96,768]{2,1,0:T(8,128)(2,1)S(1)}, bf16[4,96,768]{2,1,0:T(8,128)(2,1)S(1)}, u32[]{:S(2)}, u32[]{:S(2)}) collective-permute-start(bf16[4,96,768]{2,1,0:T(8,128)(2,1)S(1)} %copy-done.26), channel_id=1, source_target_pairs={{0,8},{1,9},{2,10},{3,11},{4,12},{5,13},{6,14},{7,15},{8,0},{9,1},... | collective-permute-start | bytes 1769480 | tf_op jit(solution)/shard_map/ppermute | solution.py:1209
  772.6 11.2 %collective-permute-start.41 = (bf16[96,768]{1,0:T(8,128)(2,1)S(1)}, bf16[96,768]{1,0:T(8,128)(2,1)S(1)}, u32[]{:S(2)}, u32[]{:S(2)}) collective-permute-start(bf16[96,768]{1,0:T(8,128)(2,1)S(1)} %get-tuple-element.256), channel_id=1, source_target_pairs={{0,6},{1,7},{2,4},{3,5},{4,2},{5,3},{6,0},{7,1},{8,14},{9,15},{10,... | collective-permute-start | bytes 442376 | tf_op jit(solution)/shard_map/ppermute | solution.py:1209
  776.0 17.8 %collective-permute-start.40 = (bf16[96,768]{1,0:T(8,128)(2,1)S(1)}, bf16[96,768]{1,0:T(8,128)(2,1)S(1)}, u32[]{:S(2)}, u32[]{:S(2)}) collective-permute-start(bf16[96,768]{1,0:T(8,128)(2,1)S(1)} %get-tuple-element.257), channel_id=1, source_target_pairs={{0,4},{1,5},{2,6},{3,7},{4,0},{5,1},{6,2},{7,3},{8,12},{9,13},{10,... | collective-permute-start | bytes 442376 | tf_op jit(solution)/shard_map/ppermute | solution.py:1209
  776.1 23.7 %collective-permute-start.33 = (f32[104,768]{1,0:T(8,128)S(1)}, f32[104,768]{1,0:T(8,128)S(1)}, u32[]{:S(2)}, u32[]{:S(2)}) collective-permute-start(f32[104,768]{1,0:T(8,128)S(1)} %add.443), channel_id=1, source_target_pairs={{0,4},{1,5},{2,6},{3,7},{4,0},{5,1},{6,2},{7,3},{8,12},{9,13},{10,... | collective-permute-start | bytes 958472 | tf_op jit(solution)/shard_map/ppermute | solution.py:1209
  (68 other events, 793.6 us)
Sparse Core Ops, SparseCore 0:
  11.7 136.4 all-gather.2
  380.6 180.9 reduce-scatter.1

commit v4 on v3

--- a/solution.py
+++ b/solution.py
@@ -1382,7 +1382,7 @@
     part = jnp.take(halved, core, axis=0, mode="clip") + swap(send, 1, size)
     yield [send]
     part = hold(part, *after)
-    for place in reversed(range(1, size.bit_length() - 1)):
+    for place in range(1, size.bit_length() - 1):
         came = swap(part, 1 << place, size)
         yield [part]
         part = part + came
@@ -1626,12 +1626,14 @@
                 own,
                 index == 0,
                 final,
-                by_steps,
+                by_steps and not final,
                 taken,
             )
             clock[:] = [sums_two]
             gated_g.append((one, two))
-            if by_steps:
+            if by_steps and final:
+                owned[index] = whole_scatter(hold_place(one, *early))
+            elif by_steps:
                 moving[f"part{index}"] = scatter_steps(
                     one, two, clock, functools.partial(owned.__setitem__, index)
                 )
@@ -1648,7 +1650,7 @@
         for index, count in enumerate(splits):
             waits = []
             if by_steps:
-                names = [("part0", "part1"), ("mixer", "part1"), ("part0",)]
+                names = [("part0",), ("mixer",), ("part0",)]
                 waits = forward_on(*names[min(index, 2)])
                 if index == 1:
                     waits += early

time: 832 us -> 783 us (0.941)
  starting transfers between devices: 81.4 us -> 59 us
  waiting for transfers between devices: 171 us -> 154 us
    ppermute x54 -> x47, starting transfers between devices: 81.3 us -> 58.9 us  [swap(): lax.ppermute(values, AXES, [(index, index ^ bit) for index in range(size)])]
    ppermute x54 -> x47, waiting for transfers between devices: 71.7 us -> 54.5 us  [swap(): lax.ppermute(values, AXES, [(index, index ^ bit) for index in range(size)])]
    unnamed x151 -> x135, local copies, waits for them, and re-layouts: 19.2 us -> 14.6 us
  transfers between devices with their start and end apart: 56 -> 50, of which waited for: 15 -> 13; matrix products, arithmetic and copies ran while one was open for 15% -> 15% of each run, Pallas kernels for 39% -> 42%
where the time goes in v4:
time: 783 us; the launch traced here: 774 us
  Pallas kernels  407 us (52%)
  waiting for transfers between devices  154 us (20%)
  local copies, waits for them, and re-layouts  68.5 us (9%)
  starting transfers between devices  59 us (8%)
  other arithmetic  54 us (7%)
  between operations  23.7 us (3%)
    pallas_call x4, Pallas kernels, mixer_backward(): call_after(after, functools.partial(mixer_backward_kernel, start == 0, la...  119 us
    pallas_call x3, Pallas kernels, gated_backward(): call_after(after, functools.partial(gated_backward_kernel, first, last, m...  117 us
    all_gather x1, waiting for transfers between devices, whole_gather(): return lax.all_gather(hold(block, *after), AXES, axis=0)  99.6 us
    pallas_call x2, Pallas kernels, mixer_forward(): call_after(after, mixer_forward_kernel, grid=(steps,), in_specs=[pl.Block...  72 us
    ppermute x47, starting transfers between devices, swap(): lax.ppermute(values, AXES, [(index, index ^ bit) for index in range(size)])  58.9 us
    ppermute x47, waiting for transfers between devices, swap(): lax.ppermute(values, AXES, [(index, index ^ bit) for index in range(size)])  54.5 us
    pallas_call x2, Pallas kernels, gated_forward(): call_after(after, functools.partial(gated_forward_kernel, first, masks, t...  53.7 us
    pallas_call x2, Pallas kernels, norm_finish(): call_after(after, norm_finish_kernel, grid=(length // block,), in_specs=[...  20.8 us
  transfers between devices with their start and end apart: 50, of which 13 were waited for; matrix products, arithmetic and copies ran while one was open for 15% of the time, Pallas kernels for 42%

profile of v4, /device:TPU:0, one launch (start us, length us, event | category | flops | bytes accessed | tf_op | source)
XLA Modules:
  0.0 773.8 jit_solution(10802870627661082385)
XLA Ops:
  12.4 3.7 fusion.34
  16.1 10.1 %filter_forward.2 = (f32[1024,768]{1,0:T(8,128)}, f32[4,512,768]{2,1,0:T(8,128)}) custom-call(f32[1024,64]{1,0:T(8,128)} %get-tuple-element.254.inner_ref, f32[64,768]{1,0:T(8,128)} %get-tuple-element.267.out_ref.refs_18_.refs_19_, f32[16,768]{1,0:T(8,128)} %pad_maximum_fusion.9.chan_ref.refs_4_.refs_6_.refs_7_, ...), custom_call_target="tpu_custom_call" | custom-call | flops 6000000000 | bytes 10485760 | tf_op jit(solution)/shard_map/filter_forward/pallas_call | solution.py:1169
  28.2 5.1 collective-permute-start.5
  34.8 3.7 fusion.35
  38.6 10.0 %filter_forward.3 = (f32[1024,768]{1,0:T(8,128)}, f32[4,512,768]{2,1,0:T(8,128)}) custom-call(f32[1024,64]{1,0:T(8,128)} %get-tuple-element.256.inner_ref, f32[64,768]{1,0:T(8,128)} %get-tuple-element.266.out_ref.refs_15_, f32[16,768]{1,0:T(8,128)} %pad_maximum_fusion.10.chan_ref.refs_3_, bf16[512,768]{1,0:T(8,128)(2,1)} %constant.65.clone.fwd_ref.refs_7_.refs_6_), custom_call_target="tpu_custom_call" | custom-call | flops 6000000000 | bytes 10485760 | tf_op jit(solution)/shard_map/filter_forward/pallas_call | solution.py:1169
  48.6 99.6 %all-gather.3.cloned.1.call-done = bf16[12288,768]{1,0:T(8,128)(2,1)} async-done(((bf16[384,768]{1,0:T(8,128)(2,1)}), bf16[12288,768]{1,0:T(8,128)(2,1)}) %all-gather.3.cloned.1.call-update) | async-done | bytes 18874384 | tf_op jit(solution)/shard_map/all_gather | solution.py:1476
  155.3 4.1 slice.650
  159.3 2.8 collective-permute-start
  168.3 35.9 %mixer_forward.2 = (f32[1024,768]{1,0:T(8,128)}, bf16[1024,768]{1,0:T(8,128)(2,1)}, bf16[1024,768]{1,0:T(8,128)(2,1)}, f32[3,1032,768]{2,1,0:T(8,128)}, f32[1024,768]{1,0:T(8,128)}, /*index=5*/f32[8,768]{1,0:T(8,128)}) custom-call(bf16[4,96,768]{2,1,0:T(8,128)(2,1)} %copy-done.2, s32[1]{0:T(128)S(6)} %copy.144.refs_1_.refs_0_.refs_3_.refs_4_, ...), custom_call_target="tpu_custom_call" | custom-call | flops 20000000000 | bytes 41943040 | tf_op jit(solution)/shard_map/mixer_forward/pallas_call | solution.py:297
  206.2 2.6 maximum_add_fusion.refs_0_.refs_4_.refs_10_
  213.5 26.5 %gated_forward.2 = (bf16[1024,3072]{1,0:T(8,128)(2,1)}, bf16[1024,3072]{1,0:T(8,128)(2,1)}, f32[1024,768]{1,0:T(8,128)}) custom-call(bf16[4,288,768]{2,1,0:T(8,128)(2,1)} %maximum_add_fusion.refs_0_.refs_4_.refs_10_, s32[1]{0:T(128)} %bitcast.55.refs_1_.me_ref.refs_0_.refs_4_, bf16[1024,768]{1,0:T(8,128)(2,1)} %get-tuple-element.80.refs_2_.refs_5_.refs_8_, ...), custom_call_target="tpu_custom_call" | custom-call | flops 14495514624 | bytes 20971520 | tf_op jit(solution)/shard_map/gated_forward/pallas_call | solution.py:480
  242.2 4.4 place_pieces.1
  246.5 2.4 slice.652
  248.9 4.0 slice.651
  252.9 36.1 %mixer_forward.3 = (f32[1024,768]{1,0:T(8,128)}, bf16[1024,768]{1,0:T(8,128)(2,1)}, bf16[1024,768]{1,0:T(8,128)(2,1)}, f32[3,1032,768]{2,1,0:T(8,128)}, f32[1024,768]{1,0:T(8,128)}, /*index=5*/f32[8,768]{1,0:T(8,128)}) custom-call(s32[1]{0:T(128)S(6)} %copy.144.refs_1_.refs_0_.refs_3_.refs_4_, f32[1024,768]{1,0:T(8,128)} %get-tuple-element.81.refs_1_.refs_2_, ...), custom_call_target="tpu_custom_call" | custom-call | flops 20000000000 | bytes 41943040 | tf_op jit(solution)/shard_map/mixer_forward/pallas_call | solution.py:297
  292.2 2.0 collective-permute-done.15.refs_7_.refs_13_
  294.2 5.1 collective-permute-done.17.refs_9_.refs_15_
  300.5 27.2 %gated_forward.3 = (bf16[1024,3072]{1,0:T(8,128)(2,1)}, bf16[1024,3072]{1,0:T(8,128)(2,1)}, f32[1024,768]{1,0:T(8,128)}) custom-call(s32[1]{0:T(128)} %bitcast.55.refs_1_.me_ref.refs_0_.refs_4_, bf16[1024,768]{1,0:T(8,128)(2,1)} %get-tuple-element.83.refs_1_.refs_5_, f32[1024,768]{1,0:T(8,128)} %get-tuple-element.84.refs_1_.refs_2_.refs_6_, ...), custom_call_target="tpu_custom_call" | custom-call | flops 14495514624 | bytes 20971520 | tf_op jit(solution)/shard_map/gated_forward/pallas_call | solution.py:480
  328.2 52.9 %gated_backward.3 = (bf16[32,288,768]{2,1,0:T(8,128)(2,1)}, bf16[16,768]{1,0:T(8,128)(2,1)}, f32[1024,768]{1,0:T(8,128)}, bf16[1024,768]{1,0:T(8,128)(2,1)}, f32[8,768]{1,0:T(8,128)}) custom-call(f32[1024,768]{1,0:T(8,128)} %get-tuple-element.85.refs_0_, s32[1]{0:T(128)} %bitcast.55.refs_1_.me_ref.refs_0_.refs_4_, bf16[1024,768]{1,0:T(8,128)(2,1)} %bitcast.331, ...), custom_call_target="tpu_custom_call" | custom-call | flops 28991029248 | bytes 20971520 | tf_op jit(solution)/shard_map/gated_backward/pallas_call | solution.py:700
  383.1 55.5 %mixer_backward.4 = (bf16[3,768,768]{2,1,0:T(8,128)(2,1)}, bf16[768,768]{1,0:T(8,128)(2,1)}, f32[80,768]{1,0:T(8,128)}, f32[1024,64]{1,0:T(8,128)}, f32[72,64]{1,0:T(8,128)}, /*index=5*/bf16[3,1024,768]{2,1,0:T(8,128)(2,1)}) custom-call(s32[1]{0:T(128)S(6)} %copy.144.refs_1_.refs_0_.refs_3_.refs_4_, bf16[1024,768]{1,0:T(8,128)(2,1)} %get-tuple-element.88.refs_1_, ...), custom_call_target="tpu_custom_call" | custom-call | flops 35999997952 | bytes 44040192 | tf_op jit(solution)/shard_map/mixer_backward/pallas_call | solution.py:1009
  438.6 5.4 pad_maximum_fusion
  444.0 4.5 gather_fusion.1
  448.5 4.6 gather_fusion
  453.1 10.5 %norm_finish.2 = (f32[1024,768]{1,0:T(8,128)}, bf16[1024,768]{1,0:T(8,128)(2,1)}, f32[8,768]{1,0:T(8,128)}) custom-call(bf16[16,96,768]{2,1,0:T(8,128)(2,1)} %gather_fusion, bf16[16,96,768]{2,1,0:T(8,128)(2,1)} %gather_fusion.1, f32[1024,768]{1,0:T(8,128)} %get-tuple-element.81.refs_1_.refs_2_, f32[1024,768]{1,0:T(8,128)} %get-tuple-element.96.refs_3_, ...), custom_call_target="tpu_custom_call" | custom-call | flops 3623878656 | bytes 20971520 | tf_op jit(solution)/shard_map/norm_finish/pallas_call | solution.py:1113
  463.7 29.3 %gated_backward.4 = (bf16[16,144,768]{2,1,0:T(8,128)(2,1)}, bf16[16,144,768]{2,1,0:T(8,128)(2,1)}, f32[1024,768]{1,0:T(8,128)}, bf16[16,768]{1,0:T(8,128)(2,1)}, f32[8,768]{1,0:T(8,128)}) custom-call(bf16[16,96,768]{2,1,0:T(8,128)(2,1)} %gather_fusion, s32[1]{0:T(128)} %bitcast.55.refs_1_.me_ref.refs_0_.refs_4_, ...), custom_call_target="tpu_custom_call" | custom-call | flops 14495514624 | bytes 20971520 | tf_op jit(solution)/shard_map/gated_backward/pallas_call | solution.py:700
  497.0 6.1 maximum_bitcast_fusion
  503.1 3.1 add_convert_fusion.6
  509.7 34.9 %gated_backward.5 = (bf16[32,144,768]{2,1,0:T(8,128)(2,1)}, bf16[16,768]{1,0:T(8,128)(2,1)}, f32[1024,768]{1,0:T(8,128)}, bf16[1024,768]{1,0:T(8,128)(2,1)}, f32[8,768]{1,0:T(8,128)}) custom-call(bf16[4,96,768]{2,1,0:T(8,128)(2,1)} %get-tuple-element.230.refs_0_, bf16[4,96,768]{2,1,0:T(8,128)(2,1)} %get-tuple-element.229.refs_1_, ...), custom_call_target="tpu_custom_call" | custom-call | flops 14495514624 | bytes 20971520 | tf_op jit(solution)/shard_map/gated_backward/pallas_call | solution.py:700
  546.5 4.6 add_convert_fusion
  553.3 20.6 %mixer_backward.5 = (bf16[3,256,768]{2,1,0:T(8,128)(2,1)}, bf16[256,768]{1,0:T(8,128)(2,1)}, f32[80,256]{1,0:T(8,128)}, f32[1024,64]{1,0:T(8,128)}, f32[72,64]{1,0:T(8,128)}, /*index=5*/bf16[3,1024,256]{2,1,0:T(8,128)(2,1)}) custom-call(bf16[4,144,768]{2,1,0:T(8,128)(2,1)} %get-tuple-element.224.refs_0_, bf16[4,144,768]{2,1,0:T(8,128)(2,1)} %get-tuple-element.223.refs_1_, ...), custom_call_target="tpu_custom_call" | custom-call | flops 12000000000 | bytes 14680064 | tf_op jit(solution)/shard_map/mixer_backward/pallas_call | solution.py:1009
  577.1 3.1 fusion.30
  582.2 17.0 %collective-permute-start.42 = (bf16[96,768]{1,0:T(8,128)(2,1)}, bf16[96,768]{1,0:T(8,128)(2,1)}, u32[]{:S(2)}, u32[]{:S(2)}) collective-permute-start(bf16[96,768]{1,0:T(8,128)(2,1)} %get-tuple-element.249.refs_1_), channel_id=1, source_target_pairs={{0,4},{1,5},{2,6},{3,7},{4,0},{5,1},{6,2},{7,3},{8,12},{9,13},{10,... | collective-permute-start | bytes 442376 | tf_op jit(solution)/shard_map/ppermute | solution.py:1209
  599.2 20.7 %mixer_backward.6 = (bf16[3,256,768]{2,1,0:T(8,128)(2,1)}, bf16[256,768]{1,0:T(8,128)(2,1)}, f32[80,256]{1,0:T(8,128)}, f32[1024,64]{1,0:T(8,128)}, f32[72,64]{1,0:T(8,128)}, /*index=5*/bf16[3,1024,256]{2,1,0:T(8,128)(2,1)}) custom-call(bf16[96,768]{1,0:T(8,128)(2,1)} %get-tuple-element.250.refs_0_, bf16[96,768]{1,0:T(8,128)(2,1)} %get-tuple-element.249.refs_1_, ...), custom_call_target="tpu_custom_call" | custom-call | flops 12000000000 | bytes 14680064 | tf_op jit(solution)/shard_map/mixer_backward/pallas_call | solution.py:1009
  622.1 3.6 fusion.29
  626.6 2.4 collective-permute-start.46
  629.0 22.0 %mixer_backward.7 = (bf16[3,256,768]{2,1,0:T(8,128)(2,1)}, bf16[256,768]{1,0:T(8,128)(2,1)}, f32[80,256]{1,0:T(8,128)}, f32[1024,64]{1,0:T(8,128)}, f32[72,64]{1,0:T(8,128)}, /*index=5*/bf16[3,1024,256]{2,1,0:T(8,128)(2,1)}) custom-call(bf16[144,768]{1,0:T(8,128)(2,1)} %get-tuple-element.233.refs_0_, bf16[144,768]{1,0:T(8,128)(2,1)} %get-tuple-element.232.refs_1_, ...), custom_call_target="tpu_custom_call" | custom-call | flops 12000000000 | bytes 14680064 | tf_op jit(solution)/shard_map/mixer_backward/pallas_call | solution.py:1009
  654.2 2.8 pad_maximum_fusion.1
  656.9 4.5 gather_fusion.3
  661.5 4.6 gather_fusion.2
  668.1 10.3 %norm_finish.3 = (f32[1024,768]{1,0:T(8,128)}, bf16[1024,768]{1,0:T(8,128)(2,1)}, f32[8,768]{1,0:T(8,128)}) custom-call(bf16[16,96,768]{2,1,0:T(8,128)(2,1)} %gather_fusion.2, bf16[16,96,768]{2,1,0:T(8,128)(2,1)} %gather_fusion.3, bf16[1024,768]{1,0:T(8,128)(2,1)} %bitcast.304, f32[1024,768]{1,0:T(8,128)} %get-tuple-element.124.refs_3_, ...), custom_call_target="tpu_custom_call" | custom-call | flops 3623878656 | bytes 20971520 | tf_op jit(solution)/shard_map/norm_finish/pallas_call | solution.py:1113
  686.2 3.0 add_convert_fusion.5
  698.6 4.1 collective-permute-done.45
  705.0 8.8 %collective-permute-done.30 = f32[104,768]{1,0:T(8,128)S(1)} collective-permute-done((f32[104,768]{1,0:T(8,128)S(1)}, f32[104,768]{1,0:T(8,128)S(1)}, u32[]{:S(2)}, u32[]{:S(2)}) %collective-permute-start.30) | collective-permute-done | bytes 319520 | tf_op jit(solution)/shard_map/ppermute | solution.py:1209
  713.9 7.5 collective-permute-done.37
  726.7 12.2 %collective-permute-done.31 = f32[104,768]{1,0:T(8,128)S(1)} collective-permute-done((f32[104,768]{1,0:T(8,128)S(1)}, f32[104,768]{1,0:T(8,128)S(1)}, u32[]{:S(2)}, u32[]{:S(2)}) %collective-permute-start.31) | collective-permute-done | bytes 319520 | tf_op jit(solution)/shard_map/ppermute | solution.py:1209
  739.5 5.0 collective-permute-done.39
  744.6 2.6 collective-permute-done.32
  749.3 5.7 collective-permute-done.33
  (330 shorter events, 93.1 us)
Async XLA Ops:
  7.3 140.9 %all-gather.3.cloned.1.call-start = ((), (), s32[]{:S(2)}) async-start(), calls=%async_computation.4 | async-start | bytes 19464192 | tf_op jit(solution)/shard_map/all_gather | solution.py:1476
  10.5 588.7 %reduce-scatter.3.cloned.1.call-start = ((), (), s32[]{:S(2)}) async-start(), calls=%async_computation.2 | async-start | bytes 14598144 | tf_op jit(solution)/shard_map/reduce_scatter | solution.py:1587
  28.2 131.1 %collective-permute-start.5 = (bf16[96,768]{1,0:T(8,128)(2,1)S(1)}, bf16[96,768]{1,0:T(8,128)(2,1)}, u32[]{:S(2)}, u32[]{:S(2)}) collective-permute-start(bf16[96,768]{1,0:T(8,128)(2,1)S(1)} %maximum_add_fusion.3), channel_id=1, source_target_pairs={{0,6},{1,7},{2,4},{3,5},{4,2},{5,3},{6,0},{7,1},{8,14},{9,15},{10,... | collective-permute-start | bytes 442376 | tf_op jit(solution)/shard_map/ppermute | solution.py:1209
  33.3 128.8 %collective-permute-start.4 = (bf16[96,768]{1,0:T(8,128)(2,1)S(1)}, bf16[96,768]{1,0:T(8,128)(2,1)}, u32[]{:S(2)}, u32[]{:S(2)}) collective-permute-start(bf16[96,768]{1,0:T(8,128)(2,1)S(1)} %maximum_add_fusion.3), channel_id=1, source_target_pairs={{0,4},{1,5},{2,6},{3,7},{4,0},{5,1},{6,2},{7,3},{8,12},{9,13},{10,... | collective-permute-start | bytes 442376 | tf_op jit(solution)/shard_map/ppermute | solution.py:1209
  33.3 128.8 %collective-permute-start.3 = (bf16[96,768]{1,0:T(8,128)(2,1)S(1)}, bf16[96,768]{1,0:T(8,128)(2,1)}, u32[]{:S(2)}, u32[]{:S(2)}) collective-permute-start(bf16[96,768]{1,0:T(8,128)(2,1)S(1)} %maximum_add_fusion.3), channel_id=1, source_target_pairs={{0,2},{1,3},{2,0},{3,1},{4,6},{5,7},{6,4},{7,5},{8,10},{9,11},{10,... | collective-permute-start | bytes 442376 | tf_op jit(solution)/shard_map/ppermute | solution.py:1209
  151.6 15.3 %collective-permute-start.2 = (bf16[288,768]{1,0:T(8,128)(2,1)}, bf16[288,768]{1,0:T(8,128)(2,1)}, u32[]{:S(2)}, u32[]{:S(2)}) collective-permute-start(bf16[288,768]{1,0:T(8,128)(2,1)} %broadcast_add_fusion.1), channel_id=1, source_target_pairs={{0,6},{1,7},{2,4},{3,5},{4,2},{5,3},{6,0},{7,1},{8,14},{9,15},{10,... | collective-permute-start | bytes 1327112 | tf_op jit(solution)/shard_map/ppermute | solution.py:1209
  155.0 51.1 %collective-permute-start.1 = (bf16[288,768]{1,0:T(8,128)(2,1)}, bf16[288,768]{1,0:T(8,128)(2,1)}, u32[]{:S(2)}, u32[]{:S(2)}) collective-permute-start(bf16[288,768]{1,0:T(8,128)(2,1)} %broadcast_add_fusion.1), channel_id=1, source_target_pairs={{0,4},{1,5},{2,6},{3,7},{4,0},{5,1},{6,2},{7,3},{8,12},{9,13},{10,... | collective-permute-start | bytes 1327112 | tf_op jit(solution)/shard_map/ppermute | solution.py:1209
  159.3 46.9 %collective-permute-start = (bf16[288,768]{1,0:T(8,128)(2,1)}, bf16[288,768]{1,0:T(8,128)(2,1)S(1)}, u32[]{:S(2)}, u32[]{:S(2)}) collective-permute-start(bf16[288,768]{1,0:T(8,128)(2,1)} %broadcast_add_fusion.1), channel_id=1, source_target_pairs={{0,2},{1,3},{2,0},{3,1},{4,6},{5,7},{6,4},{7,5},{8,10},{9,11},{10,... | collective-permute-start | bytes 1327112 | tf_op jit(solution)/shard_map/ppermute | solution.py:1209
  163.2 49.2 %collective-permute-start.11 = (bf16[4,96,768]{2,1,0:T(8,128)(2,1)S(1)}, bf16[4,96,768]{2,1,0:T(8,128)(2,1)S(1)}, u32[]{:S(2)}, u32[]{:S(2)}) collective-permute-start(bf16[4,96,768]{2,1,0:T(8,128)(2,1)S(1)} %maximum_add_fusion.1.refs_0_), channel_id=1, source_target_pairs={{0,24},{1,25},{2,26},{3,27},{4,28},{5,29},{6,30},{7,31},{8,16},{9,... | collective-permute-start | bytes 1769480 | tf_op jit(solution)/shard_map/ppermute | solution.py:1209
  164.8 46.5 %collective-permute-start.9 = (bf16[4,96,768]{2,1,0:T(8,128)(2,1)S(1)}, bf16[4,96,768]{2,1,0:T(8,128)(2,1)S(1)}, u32[]{:S(2)}, u32[]{:S(2)}) collective-permute-start(bf16[4,96,768]{2,1,0:T(8,128)(2,1)S(1)} %maximum_add_fusion.1.refs_0_), channel_id=1, source_target_pairs={{0,16},{1,17},{2,18},{3,19},{4,20},{5,21},{6,22},{7,23},{8,24},{9,... | collective-permute-start | bytes 1769480 | tf_op jit(solution)/shard_map/ppermute | solution.py:1209
  166.8 43.4 %collective-permute-start.7 = (bf16[4,96,768]{2,1,0:T(8,128)(2,1)S(1)}, bf16[4,96,768]{2,1,0:T(8,128)(2,1)S(1)}, u32[]{:S(2)}, u32[]{:S(2)}) collective-permute-start(bf16[4,96,768]{2,1,0:T(8,128)(2,1)S(1)} %maximum_add_fusion.1.refs_0_), channel_id=1, source_target_pairs={{0,8},{1,9},{2,10},{3,11},{4,12},{5,13},{6,14},{7,15},{8,0},{9,1},... | collective-permute-start | bytes 1769480 | tf_op jit(solution)/shard_map/ppermute | solution.py:1209
  206.1 33.9 %collective-permute-start.6 = (bf16[4,96,768]{2,1,0:T(8,128)(2,1)}, bf16[4,96,768]{2,1,0:T(8,128)(2,1)S(1)}, u32[]{:S(2)}, u32[]{:S(2)}) collective-permute-start(bf16[4,96,768]{2,1,0:T(8,128)(2,1)} %copy-done.2), channel_id=1, source_target_pairs={{0,1},{1,0},{2,3},{3,2},{4,5},{5,4},{6,7},{7,6},{8,9},{9,8},{10,11... | collective-permute-start | bytes 1769480 | tf_op jit(solution)/shard_map/ppermute | solution.py:1209
  208.8 83.2 %collective-permute-start.18 = (bf16[4,288,768]{2,1,0:T(8,128)(2,1)}, bf16[4,288,768]{2,1,0:T(8,128)(2,1)}, u32[]{:S(2)}, u32[]{:S(2)}) collective-permute-start(bf16[4,288,768]{2,1,0:T(8,128)(2,1)} %maximum_add_fusion.refs_0_.refs_4_.refs_10_), channel_id=1, source_target_pairs={{0,24},{1,25},{2,26},{3,27},{4,28},{5,29},{6,30},{7,31},{8,16},{9,... | collective-permute-start | bytes 5308424 | tf_op jit(solution)/shard_map/ppermute | solution.py:1209
  211.1 29.8 %collective-permute-start.8 = (bf16[4,96,768]{2,1,0:T(8,128)(2,1)}, bf16[4,96,768]{2,1,0:T(8,128)(2,1)}, u32[]{:S(2)}, u32[]{:S(2)}) collective-permute-start(bf16[4,96,768]{2,1,0:T(8,128)(2,1)} %hold_place.7.refs_2_), channel_id=1, source_target_pairs={{0,1},{1,0},{2,3},{3,2},{4,5},{5,4},{6,7},{7,6},{8,9},{9,8},{10,11... | collective-permute-start | bytes 1769480 | tf_op jit(solution)/shard_map/ppermute | solution.py:1209
  212.1 30.0 %collective-permute-start.10 = (bf16[4,96,768]{2,1,0:T(8,128)(2,1)}, bf16[4,96,768]{2,1,0:T(8,128)(2,1)}, u32[]{:S(2)}, u32[]{:S(2)}) collective-permute-start(bf16[4,96,768]{2,1,0:T(8,128)(2,1)} %hold_place.8.refs_4_), channel_id=1, source_target_pairs={{0,1},{1,0},{2,3},{3,2},{4,5},{5,4},{6,7},{7,6},{8,9},{9,8},{10,11... | collective-permute-start | bytes 1769480 | tf_op jit(solution)/shard_map/ppermute | solution.py:1209
  213.3 28.8 %collective-permute-start.12 = (bf16[4,96,768]{2,1,0:T(8,128)(2,1)}, bf16[4,96,768]{2,1,0:T(8,128)(2,1)}, u32[]{:S(2)}, u32[]{:S(2)}) collective-permute-start(bf16[4,96,768]{2,1,0:T(8,128)(2,1)} %hold_place.9.refs_6_), channel_id=1, source_target_pairs={{0,1},{1,0},{2,3},{3,2},{4,5},{5,4},{6,7},{7,6},{8,9},{9,8},{10,11... | collective-permute-start | bytes 1769480 | tf_op jit(solution)/shard_map/ppermute | solution.py:1209
  240.0 50.4 %collective-permute-start.16 = (bf16[4,288,768]{2,1,0:T(8,128)(2,1)}, bf16[4,288,768]{2,1,0:T(8,128)(2,1)S(1)}, u32[]{:S(2)}, u32[]{:S(2)}) collective-permute-start(bf16[4,288,768]{2,1,0:T(8,128)(2,1)} %maximum_add_fusion.refs_0_.refs_4_.refs_10_), channel_id=1, source_target_pairs={{0,16},{1,17},{2,18},{3,19},{4,20},{5,21},{6,22},{7,23},{8,24},{9,... | collective-permute-start | bytes 5308424 | tf_op jit(solution)/shard_map/ppermute | solution.py:1209
  240.9 48.2 %collective-permute-start.14 = (bf16[4,288,768]{2,1,0:T(8,128)(2,1)}, bf16[4,288,768]{2,1,0:T(8,128)(2,1)S(1)}, u32[]{:S(2)}, u32[]{:S(2)}) collective-permute-start(bf16[4,288,768]{2,1,0:T(8,128)(2,1)} %maximum_add_fusion.refs_0_.refs_4_.refs_10_), channel_id=1, source_target_pairs={{0,8},{1,9},{2,10},{3,11},{4,12},{5,13},{6,14},{7,15},{8,0},{9,1},... | collective-permute-start | bytes 5308424 | tf_op jit(solution)/shard_map/ppermute | solution.py:1209
  242.2 50.0 %collective-permute-start.13 = (bf16[4,288,768]{2,1,0:T(8,128)(2,1)}, bf16[4,288,768]{2,1,0:T(8,128)(2,1)}, u32[]{:S(2)}, u32[]{:S(2)}) collective-permute-start(bf16[4,288,768]{2,1,0:T(8,128)(2,1)} %maximum_add_fusion.refs_0_.refs_4_.refs_10_), channel_id=1, source_target_pairs={{0,1},{1,0},{2,3},{3,2},{4,5},{5,4},{6,7},{7,6},{8,9},{9,8},{10,11... | collective-permute-start | bytes 5308424 | tf_op jit(solution)/shard_map/ppermute | solution.py:1209
  291.7 7.6 collective-permute-start.17
  292.0 7.3 collective-permute-start.19
  381.2 382.8 %reduce-scatter.5.cloned.1.call-start = ((), (), s32[]{:S(2)}) async-start(), calls=%async_computation.3 | async-start | bytes 7299072 | tf_op jit(solution)/shard_map/reduce_scatter | solution.py:1587
  453.1 50.0 %collective-permute-start.21 = (bf16[16,96,768]{2,1,0:T(8,128)(2,1)}, bf16[16,96,768]{2,1,0:T(8,128)(2,1)}, u32[]{:S(2)}, u32[]{:S(2)}) collective-permute-start(bf16[16,96,768]{2,1,0:T(8,128)(2,1)} %gather_fusion), channel_id=1, source_target_pairs={{0,1},{1,0},{2,3},{3,2},{4,5},{5,4},{6,7},{7,6},{8,9},{9,8},{10,11... | collective-permute-start | bytes 7077896 | tf_op jit(solution)/shard_map/ppermute | solution.py:1209
  493.0 53.5 %collective-permute-start.20 = (bf16[16,144,768]{2,1,0:T(8,128)(2,1)}, bf16[16,144,768]{2,1,0:T(8,128)(2,1)}, u32[]{:S(2)}, u32[]{:S(2)}) collective-permute-start(bf16[16,144,768]{2,1,0:T(8,128)(2,1)} %get-tuple-element.102.refs_3_), channel_id=1, source_target_pairs={{0,1},{1,0},{2,3},{3,2},{4,5},{5,4},{6,7},{7,6},{8,9},{9,8},{10,11... | collective-permute-start | bytes 10616840 | tf_op jit(solution)/shard_map/ppermute | solution.py:1209
  506.2 69.6 %collective-permute-start.24 = (bf16[4,96,768]{2,1,0:T(8,128)(2,1)}, bf16[4,96,768]{2,1,0:T(8,128)(2,1)}, u32[]{:S(2)}, u32[]{:S(2)}) collective-permute-start(bf16[4,96,768]{2,1,0:T(8,128)(2,1)} %get-tuple-element.228.refs_2_), channel_id=1, source_target_pairs={{0,16},{1,17},{2,18},{3,19},{4,20},{5,21},{6,22},{7,23},{8,24},{9,... | collective-permute-start | bytes 1769480 | tf_op jit(solution)/shard_map/ppermute | solution.py:1209
  507.3 69.7 %collective-permute-start.23 = (bf16[4,96,768]{2,1,0:T(8,128)(2,1)}, bf16[4,96,768]{2,1,0:T(8,128)(2,1)}, u32[]{:S(2)}, u32[]{:S(2)}) collective-permute-start(bf16[4,96,768]{2,1,0:T(8,128)(2,1)} %get-tuple-element.229.refs_1_), channel_id=1, source_target_pairs={{0,8},{1,9},{2,10},{3,11},{4,12},{5,13},{6,14},{7,15},{8,0},{9,1},... | collective-permute-start | bytes 1769480 | tf_op jit(solution)/shard_map/ppermute | solution.py:1209
  508.4 68.6 %collective-permute-start.22 = (bf16[4,96,768]{2,1,0:T(8,128)(2,1)}, bf16[4,96,768]{2,1,0:T(8,128)(2,1)}, u32[]{:S(2)}, u32[]{:S(2)}) collective-permute-start(bf16[4,96,768]{2,1,0:T(8,128)(2,1)} %get-tuple-element.230.refs_0_), channel_id=1, source_target_pairs={{0,24},{1,25},{2,26},{3,27},{4,28},{5,29},{6,30},{7,31},{8,16},{9,... | collective-permute-start | bytes 1769480 | tf_op jit(solution)/shard_map/ppermute | solution.py:1209
  551.1 70.8 %collective-permute-start.27 = (bf16[4,144,768]{2,1,0:T(8,128)(2,1)}, bf16[4,144,768]{2,1,0:T(8,128)(2,1)S(1)}, u32[]{:S(2)}, u32[]{:S(2)}) collective-permute-start(bf16[4,144,768]{2,1,0:T(8,128)(2,1)} %get-tuple-element.222.refs_2_), channel_id=1, source_target_pairs={{0,16},{1,17},{2,18},{3,19},{4,20},{5,21},{6,22},{7,23},{8,24},{9,... | collective-permute-start | bytes 2654216 | tf_op jit(solution)/shard_map/ppermute | solution.py:1209
  552.2 69.9 %collective-permute-start.26 = (bf16[4,144,768]{2,1,0:T(8,128)(2,1)}, bf16[4,144,768]{2,1,0:T(8,128)(2,1)S(1)}, u32[]{:S(2)}, u32[]{:S(2)}) collective-permute-start(bf16[4,144,768]{2,1,0:T(8,128)(2,1)} %get-tuple-element.223.refs_1_), channel_id=1, source_target_pairs={{0,8},{1,9},{2,10},{3,11},{4,12},{5,13},{6,14},{7,15},{8,0},{9,1},... | collective-permute-start | bytes 2654216 | tf_op jit(solution)/shard_map/ppermute | solution.py:1209
  575.8 46.3 %collective-permute-start.25 = (bf16[4,144,768]{2,1,0:T(8,128)(2,1)}, bf16[4,144,768]{2,1,0:T(8,128)(2,1)}, u32[]{:S(2)}, u32[]{:S(2)}) collective-permute-start(bf16[4,144,768]{2,1,0:T(8,128)(2,1)} %get-tuple-element.224.refs_0_), channel_id=1, source_target_pairs={{0,24},{1,25},{2,26},{3,27},{4,28},{5,29},{6,30},{7,31},{8,16},{9,... | collective-permute-start | bytes 2654216 | tf_op jit(solution)/shard_map/ppermute | solution.py:1209
  580.9 99.7 %collective-permute-start.43 = (bf16[96,768]{1,0:T(8,128)(2,1)}, bf16[96,768]{1,0:T(8,128)(2,1)}, u32[]{:S(2)}, u32[]{:S(2)}) collective-permute-start(bf16[96,768]{1,0:T(8,128)(2,1)} %get-tuple-element.248.refs_2_), channel_id=1, source_target_pairs={{0,6},{1,7},{2,4},{3,5},{4,2},{5,3},{6,0},{7,1},{8,14},{9,15},{10,... | collective-permute-start | bytes 442376 | tf_op jit(solution)/shard_map/ppermute | solution.py:1209
  582.2 100.1 %collective-permute-start.42 = (bf16[96,768]{1,0:T(8,128)(2,1)}, bf16[96,768]{1,0:T(8,128)(2,1)}, u32[]{:S(2)}, u32[]{:S(2)}) collective-permute-start(bf16[96,768]{1,0:T(8,128)(2,1)} %get-tuple-element.249.refs_1_), channel_id=1, source_target_pairs={{0,4},{1,5},{2,6},{3,7},{4,0},{5,1},{6,2},{7,3},{8,12},{9,13},{10,... | collective-permute-start | bytes 442376 | tf_op jit(solution)/shard_map/ppermute | solution.py:1209
  621.8 60.9 %collective-permute-start.41 = (bf16[96,768]{1,0:T(8,128)(2,1)}, bf16[96,768]{1,0:T(8,128)(2,1)}, u32[]{:S(2)}, u32[]{:S(2)}) collective-permute-start(bf16[96,768]{1,0:T(8,128)(2,1)} %get-tuple-element.250.refs_0_), channel_id=1, source_target_pairs={{0,2},{1,3},{2,0},{3,1},{4,6},{5,7},{6,4},{7,5},{8,10},{9,11},{10,... | collective-permute-start | bytes 442376 | tf_op jit(solution)/shard_map/ppermute | solution.py:1209
  626.6 69.2 %collective-permute-start.46 = (bf16[144,768]{1,0:T(8,128)(2,1)}, bf16[144,768]{1,0:T(8,128)(2,1)}, u32[]{:S(2)}, u32[]{:S(2)}) collective-permute-start(bf16[144,768]{1,0:T(8,128)(2,1)} %get-tuple-element.231.refs_2_), channel_id=1, source_target_pairs={{0,6},{1,7},{2,4},{3,5},{4,2},{5,3},{6,0},{7,1},{8,14},{9,15},{10,... | collective-permute-start | bytes 663560 | tf_op jit(solution)/shard_map/ppermute | solution.py:1209
  667.2 19.0 %collective-permute-start.29 = (bf16[16,96,768]{2,1,0:T(8,128)(2,1)}, bf16[16,96,768]{2,1,0:T(8,128)(2,1)}, u32[]{:S(2)}, u32[]{:S(2)}) collective-permute-start(bf16[16,96,768]{2,1,0:T(8,128)(2,1)} %gather_fusion.2), channel_id=1, source_target_pairs={{0,1},{1,0},{2,3},{3,2},{4,5},{5,4},{6,7},{7,6},{8,9},{9,8},{10,11... | collective-permute-start | bytes 7077896 | tf_op jit(solution)/shard_map/ppermute | solution.py:1209
  680.6 22.1 %collective-permute-start.45 = (bf16[144,768]{1,0:T(8,128)(2,1)}, bf16[144,768]{1,0:T(8,128)(2,1)}, u32[]{:S(2)}, u32[]{:S(2)}) collective-permute-start(bf16[144,768]{1,0:T(8,128)(2,1)} %get-tuple-element.232.refs_1_), channel_id=1, source_target_pairs={{0,4},{1,5},{2,6},{3,7},{4,0},{5,1},{6,2},{7,3},{8,12},{9,13},{10,... | collective-permute-start | bytes 663560 | tf_op jit(solution)/shard_map/ppermute | solution.py:1209
  682.3 21.3 %collective-permute-start.44 = (bf16[144,768]{1,0:T(8,128)(2,1)}, bf16[144,768]{1,0:T(8,128)(2,1)}, u32[]{:S(2)}, u32[]{:S(2)}) collective-permute-start(bf16[144,768]{1,0:T(8,128)(2,1)} %get-tuple-element.233.refs_0_), channel_id=1, source_target_pairs={{0,2},{1,3},{2,0},{3,1},{4,6},{5,7},{6,4},{7,5},{8,10},{9,11},{10,... | collective-permute-start | bytes 663560 | tf_op jit(solution)/shard_map/ppermute | solution.py:1209
  682.7 14.1 %collective-permute-start.28 = (f32[104,768]{1,0:T(8,128)S(1)}, f32[104,768]{1,0:T(8,128)}, u32[]{:S(2)}, u32[]{:S(2)}) collective-permute-start(f32[104,768]{1,0:T(8,128)S(1)} %dynamic-slice_bitcast_fusion), channel_id=1, source_target_pairs={{0,1},{1,0},{2,3},{3,2},{4,5},{5,4},{6,7},{7,6},{8,9},{9,8},{10,11... | collective-permute-start | bytes 958472 | tf_op jit(solution)/shard_map/ppermute | solution.py:1209
  690.4 23.6 %collective-permute-start.35 = (bf16[4,96,768]{2,1,0:T(8,128)(2,1)}, bf16[4,96,768]{2,1,0:T(8,128)(2,1)}, u32[]{:S(2)}, u32[]{:S(2)}) collective-permute-start(bf16[4,96,768]{2,1,0:T(8,128)(2,1)} %get-tuple-element.225), channel_id=1, source_target_pairs={{0,24},{1,25},{2,26},{3,27},{4,28},{5,29},{6,30},{7,31},{8,16},{9,... | collective-permute-start | bytes 1769480 | tf_op jit(solution)/shard_map/ppermute | solution.py:1209
  695.8 25.6 %collective-permute-start.37 = (bf16[4,96,768]{2,1,0:T(8,128)(2,1)}, bf16[4,96,768]{2,1,0:T(8,128)(2,1)S(1)}, u32[]{:S(2)}, u32[]{:S(2)}) collective-permute-start(bf16[4,96,768]{2,1,0:T(8,128)(2,1)} %get-tuple-element.226), channel_id=1, source_target_pairs={{0,16},{1,17},{2,18},{3,19},{4,20},{5,21},{6,22},{7,23},{8,24},{9,... | collective-permute-start | bytes 1769480 | tf_op jit(solution)/shard_map/ppermute | solution.py:1209
  696.8 24.6 %collective-permute-start.36 = (bf16[4,96,768]{2,1,0:T(8,128)(2,1)}, bf16[4,96,768]{2,1,0:T(8,128)(2,1)S(1)}, u32[]{:S(2)}, u32[]{:S(2)}) collective-permute-start(bf16[4,96,768]{2,1,0:T(8,128)(2,1)} %copy-done.21), channel_id=1, source_target_pairs={{0,8},{1,9},{2,10},{3,11},{4,12},{5,13},{6,14},{7,15},{8,0},{9,1},... | collective-permute-start | bytes 1769480 | tf_op jit(solution)/shard_map/ppermute | solution.py:1209
  702.7 11.1 %collective-permute-start.30 = (f32[104,768]{1,0:T(8,128)S(1)}, f32[104,768]{1,0:T(8,128)S(1)}, u32[]{:S(2)}, u32[]{:S(2)}) collective-permute-start(f32[104,768]{1,0:T(8,128)S(1)} %fusion.6), channel_id=1, source_target_pairs={{0,2},{1,3},{2,0},{3,1},{4,6},{5,7},{6,4},{7,5},{8,10},{9,11},{10,... | collective-permute-start | bytes 958472 | tf_op jit(solution)/shard_map/ppermute | solution.py:1209
  713.8 25.1 %collective-permute-start.31 = (f32[104,768]{1,0:T(8,128)S(1)}, f32[104,768]{1,0:T(8,128)S(1)}, u32[]{:S(2)}, u32[]{:S(2)}) collective-permute-start(f32[104,768]{1,0:T(8,128)S(1)} %add.383), channel_id=1, source_target_pairs={{0,4},{1,5},{2,6},{3,7},{4,0},{5,1},{6,2},{7,3},{8,12},{9,13},{10,... | collective-permute-start | bytes 958472 | tf_op jit(solution)/shard_map/ppermute | solution.py:1209
  723.1 16.4 %collective-permute-start.38 = (bf16[96,768]{1,0:T(8,128)(2,1)S(1)}, bf16[96,768]{1,0:T(8,128)(2,1)S(1)}, u32[]{:S(2)}, u32[]{:S(2)}) collective-permute-start(bf16[96,768]{1,0:T(8,128)(2,1)S(1)} %get-tuple-element.245), channel_id=1, source_target_pairs={{0,2},{1,3},{2,0},{3,1},{4,6},{5,7},{6,4},{7,5},{8,10},{9,11},{10,... | collective-permute-start | bytes 442376 | tf_op jit(solution)/shard_map/ppermute | solution.py:1209
  724.8 14.7 %collective-permute-start.40 = (bf16[96,768]{1,0:T(8,128)(2,1)S(1)}, bf16[96,768]{1,0:T(8,128)(2,1)S(1)}, u32[]{:S(2)}, u32[]{:S(2)}) collective-permute-start(bf16[96,768]{1,0:T(8,128)(2,1)S(1)} %get-tuple-element.246), channel_id=1, source_target_pairs={{0,6},{1,7},{2,4},{3,5},{4,2},{5,3},{6,0},{7,1},{8,14},{9,15},{10,... | collective-permute-start | bytes 442376 | tf_op jit(solution)/shard_map/ppermute | solution.py:1209
  726.6 17.9 %collective-permute-start.39 = (bf16[96,768]{1,0:T(8,128)(2,1)S(1)}, bf16[96,768]{1,0:T(8,128)(2,1)S(1)}, u32[]{:S(2)}, u32[]{:S(2)}) collective-permute-start(bf16[96,768]{1,0:T(8,128)(2,1)S(1)} %get-tuple-element.247), channel_id=1, source_target_pairs={{0,4},{1,5},{2,6},{3,7},{4,0},{5,1},{6,2},{7,3},{8,12},{9,13},{10,... | collective-permute-start | bytes 442376 | tf_op jit(solution)/shard_map/ppermute | solution.py:1209
  739.0 8.3 %collective-permute-start.32 = (f32[104,768]{1,0:T(8,128)S(1)}, f32[104,768]{1,0:T(8,128)S(1)}, u32[]{:S(2)}, u32[]{:S(2)}) collective-permute-start(f32[104,768]{1,0:T(8,128)S(1)} %add.384), channel_id=1, source_target_pairs={{0,8},{1,9},{2,10},{3,11},{4,12},{5,13},{6,14},{7,15},{8,0},{9,1},... | collective-permute-start | bytes 958472 | tf_op jit(solution)/shard_map/ppermute | solution.py:1209
  747.3 7.7 collective-permute-start.33
  (54 other events, 728.8 us)
Sparse Core Ops, SparseCore 0:
  11.7 136.4 all-gather.2
  381.3 199.8 reduce-scatter.2
  599.3 129.1 reduce-scatter.4
